TPU v7x, 32 devices: a whole 2x2x4 slice. The times are simulated.
32 devices in a mesh: row: 8 (over z, x), col: 4 (over y, core).
Axes of the slice: x: 2, y: 2, z: 4, core: 2. Of those that a mesh axis runs over, the one named last changes fastest.
Arguments:
- factors: bfloat16 [16384, 256], P(('row', 'col')), may hold values from -1.5 to 1.5
- cores: bfloat16 [8, 256, 256], replicated, may hold values from -0.375 to 0.375
- tiles: bfloat16 [1024, 256, 256], P(('row', 'col')), may hold values from -6 to 6
- tile_coords: int32 [1024, 3], P(('row', 'col')), may hold values from 0 to 15, as said below
- tile_counts: int32 [32], P(('row', 'col')), may hold values from 1 to 32, as said below
Outputs:
- gradient: float32 [16384, 256], P(('row', 'col'))
Inputs may be any that keep to these rules, and one draw needn't show every extreme that they name: `tile_coords`: column 0 is a relation below 8, column 1 below 8, column 2 below 16; within one device no two slots have the same three coordinates. `tile_counts`: some device has all 32 slots live.
All inputs are finite; a program needn't handle non-finite values.
Results may differ from a plain program's by a relative error of at most 0.0011.
Values may be sent and summed in bfloat16 or wider, within the bound.
No kernel may reach another device: no remote copies, remote signals or barrier semaphores. Data moves between devices by JAX's collectives and lax.ppermute only.
A program may use at most 128 MiB of HBM per device.

v0:
```python
import jax
import jax.numpy as jnp
from jax import lax
from jax.sharding import PartitionSpec as P

weight_decay = 1.0


def broadcast(value, axis, source):
    kept = jnp.where(lax.axis_index(axis) == source, value, 0).astype(value.dtype)
    return lax.psum(kept, axis)


def local(factors, cores, tiles, tile_coords, tile_counts):
    n_row = lax.axis_size("row")
    n_col = lax.axis_size("col")
    row_ratio = n_row // n_col
    shard_rows, rank_width = factors.shape
    tile_size = tiles.shape[1]
    relations = cores.shape[0]
    src_rows = shard_rows * n_col
    tgt_rows = src_rows * row_ratio
    src_blocks = src_rows // tile_size
    tgt_blocks = tgt_rows // tile_size
    row_pos = lax.axis_index("row")
    col_pos = lax.axis_index("col")
    source = lax.all_gather(factors, "col", axis=0, tiled=True)
    received = []
    for part_index in range(row_ratio):
        received.append(broadcast(source, "row", col_pos * row_ratio + part_index))
    target = jnp.concatenate(received, axis=0)
    left_core = jnp.einsum("nr,krs->kns", source, cores, preferred_element_type=jnp.float32).astype(
        jnp.bfloat16
    )
    left_core = left_core.reshape(relations, src_blocks, tile_size, rank_width)
    right_core = jnp.einsum(
        "nr,ksr->kns", target, cores, preferred_element_type=jnp.float32
    ).astype(jnp.bfloat16)
    right_core = right_core.reshape(relations, tgt_blocks, tile_size, rank_width)
    tgt_factor = target.reshape(tgt_blocks, tile_size, rank_width)
    live_count = tile_counts[0]

    def group_pass(group, carry):
        grad_src, grad_tgt = carry
        start = group * 8
        coords = lax.dynamic_slice_in_dim(tile_coords, start, 8, 0)
        values = lax.dynamic_slice_in_dim(tiles, start, 8, 0)
        is_live = start + jnp.arange(8, dtype=jnp.int32) < live_count
        relation = coords[:, 0]
        src_index = coords[:, 1]
        tgt_index = coords[:, 2]
        left = left_core[relation, src_index]
        right = tgt_factor[tgt_index]
        right_rel = right_core[relation, tgt_index]
        predicted = jnp.einsum("gtr,gur->gtu", left, right, preferred_element_type=jnp.float32)
        resid = jnp.where(
            is_live[:, None, None], values.astype(jnp.float32) - predicted, 0.0
        ).astype(jnp.bfloat16)
        src_grad = jnp.einsum("gtu,gur->gtr", resid, right_rel, preferred_element_type=jnp.float32)
        tgt_grad = jnp.einsum("gtu,gtr->gur", resid, left, preferred_element_type=jnp.float32)
        return (grad_src.at[src_index].add(src_grad), grad_tgt.at[tgt_index].add(tgt_grad))

    start_grads = (
        jnp.zeros((src_blocks, tile_size, rank_width), jnp.float32),
        jnp.zeros((tgt_blocks, tile_size, rank_width), jnp.float32),
    )
    grad_src, grad_tgt = lax.fori_loop(0, (live_count + 7) // 8, group_pass, start_grads)
    grad_src = grad_src.reshape(src_rows, rank_width)
    grad_tgt = grad_tgt.reshape(tgt_rows, rank_width)
    tgt_total = lax.psum(grad_tgt, "row")
    is_owner = row_pos // row_ratio == col_pos
    own_piece = lax.dynamic_slice_in_dim(tgt_total, row_pos % row_ratio * src_rows, src_rows, 0)
    src_terms = grad_src + jnp.where(is_owner, own_piece, 0.0)
    summed = lax.psum_scatter(src_terms, "col", scatter_dimension=0, tiled=True)
    return weight_decay * factors.astype(jnp.float32) - summed / tile_size


def solution(mesh):
    in_specs = (
        P(("row", "col"), None),
        P(),
        P(("row", "col"), None, None),
        P(("row", "col"), None),
        P(("row", "col")),
    )
    out_specs = P(("row", "col"), None)
    return jax.shard_map(local, mesh=mesh, in_specs=in_specs, out_specs=out_specs, check_vma=False)
```

profile of v0, /device:TPU:0, one launch (start us, length us, event | category | flops | bytes accessed | tf_op | source)
XLA Modules:
  0.0 464.5 jit_solution(3950184494900259578)
XLA Ops:
  7.3 21.1 %all-gather.2.cloned.1.call-done = bf16[2048,256]{1,0:T(8,128)(2,1)} async-done(((bf16[512,256]{1,0:T(8,128)(2,1)}), bf16[2048,256]{1,0:T(8,128)(2,1)}) %all-gather.2.cloned.1.call-update) | async-done | bytes 1048592 | tf_op jit(solution)/shard_map/all_gather | solution.py:27
  31.9 5.7 %convert_bitcast_fusion = bf16[8,2048,256]{1,2,0:T(8,128)(2,1)} fusion(bf16[8,256,256]{2,1,0:T(8,128)(2,1)S(1)} %copy-done, bf16[2048,256]{1,0:T(8,128)(2,1)S(1)} %copy-done.4), kind=kOutput, calls=%fused_computation.19 | convolution fusion | flops 2151677952 | bytes 10485760 | tf_op jit(solution)/shard_map/nr,krs->kns/dot_general | solution.py:32
  37.6 11.4 %copy.11 = bf16[8,2048,256]{2,1,0:T(8,128)(2,1)} copy(bf16[8,2048,256]{1,2,0:T(8,128)(2,1)} %convert_bitcast_fusion) | data formatting | bytes 16777216 | tf_op jit(solution)/shard_map/while | solution.py:67
  49.0 85.3 %all-reduce.6.cloned.1.call-done = (bf16[2048,256]{1,0:T(8,128)(2,1)}, bf16[2048,256]{1,0:T(8,128)(2,1)}) async-done(((bf16[2048,256]{1,0:T(8,128)(2,1)}, bf16[2048,256]{1,0:T(8,128)(2,1)}), (bf16[2048,256]{1,0:T(8,128)(2,1)}, bf16[2048,256]{1,0:T(8,128)(2,1)})) %all-reduce.6.cloned.1.call-update) | async-done | bytes 2097168 | tf_op jit(solution)/shard_map/psum | solution.py:11
  137.7 9.7 %convolution_convert_fusion = bf16[4096,8,256]{2,0,1:T(8,128)(2,1)} fusion(bf16[8,256,256]{2,1,0:T(8,128)(2,1)S(1)} %copy-done, bf16[4096,256]{1,0:T(8,128)(2,1)} %constant_dynamic-update-slice_fusion), kind=kOutput, calls=%fused_computation.18 | convolution fusion | flops 4303355904 | bytes 19922944 | tf_op jit(solution)/shard_map/nr,ksr->kns/dot_general | solution.py:36
  151.4 86.2 %while.12 = (s32[]{:T(128)}, f32[8,256,256]{2,1,0:T(8,128)}, f32[16,256,256]{2,1,0:T(8,128)}, s32[]{:T(128)}, s32[32,3]{0,1:T(4,128)S(1)}, /*index=5*/s32[]{:T(1...) while((s32[]{:T(128)}, f32[8,256,256]{2,1,0:T(8,128)}, ...), condition=%wide.region_5.6_spmd, body=%wide.region_2.5_spmd.sunk | while | flops 808453248 | bytes 35656592 | solution.py:67
  154.3 4.0 gather_fusion
  161.5 6.4 %gather_fusion.2 = bf16[8,256,256]{2,1,0:T(8,128)(2,1)S(1)} fusion(bf16[8,16,256,256]{3,2,1,0:T(8,128)(2,1)} %get-tuple-element.206, s32[8]{0:T(128)S(1)} %get-tuple-element.168), kind=kCustom, calls=%fused_computation.2.clone.1 | custom fusion | bytes 2097216 | tf_op jit(solution)/shard_map/while/body/gather | solution.py:54
  167.9 3.0 fusion.30
  170.9 5.0 %scatter_fusion = f32[8,256,256]{2,1,0:T(8,128)} fusion(f32[8,256,256]{2,1,0:T(8,128)} %get-tuple-element.184, s32[8]{0:T(128)S(1)} %get-tuple-element.165, f32[8,256,256]{2,1,0:T(8,128)} %fusion.30), kind=kCustom, calls=%fused_computation.3.clone.1 | custom fusion | flops 524288 | bytes 6291488 | tf_op jit(solution)/shard_map/while/body/scatter-add | solution.py:61
  175.9 4.3 scatter_fusion.1
  183.2 4.0 gather_fusion
  190.4 6.4 %gather_fusion.2 = bf16[8,256,256]{2,1,0:T(8,128)(2,1)S(1)} fusion(bf16[8,16,256,256]{3,2,1,0:T(8,128)(2,1)} %get-tuple-element.206, s32[8]{0:T(128)S(1)} %get-tuple-element.168), kind=kCustom, calls=%fused_computation.2.clone.1 | custom fusion | bytes 2097216 | tf_op jit(solution)/shard_map/while/body/gather | solution.py:54
  196.8 3.0 fusion.30
  199.7 5.0 %scatter_fusion = f32[8,256,256]{2,1,0:T(8,128)} fusion(f32[8,256,256]{2,1,0:T(8,128)} %get-tuple-element.184, s32[8]{0:T(128)S(1)} %get-tuple-element.165, f32[8,256,256]{2,1,0:T(8,128)} %fusion.30), kind=kCustom, calls=%fused_computation.3.clone.1 | custom fusion | flops 524288 | bytes 6291488 | tf_op jit(solution)/shard_map/while/body/scatter-add | solution.py:61
  204.7 4.1 scatter_fusion.1
  211.8 4.0 gather_fusion
  219.0 6.4 %gather_fusion.2 = bf16[8,256,256]{2,1,0:T(8,128)(2,1)S(1)} fusion(bf16[8,16,256,256]{3,2,1,0:T(8,128)(2,1)} %get-tuple-element.206, s32[8]{0:T(128)S(1)} %get-tuple-element.168), kind=kCustom, calls=%fused_computation.2.clone.1 | custom fusion | bytes 2097216 | tf_op jit(solution)/shard_map/while/body/gather | solution.py:54
  225.4 3.0 fusion.30
  228.4 4.8 %scatter_fusion = f32[8,256,256]{2,1,0:T(8,128)} fusion(f32[8,256,256]{2,1,0:T(8,128)} %get-tuple-element.184, s32[8]{0:T(128)S(1)} %get-tuple-element.165, f32[8,256,256]{2,1,0:T(8,128)} %fusion.30), kind=kCustom, calls=%fused_computation.3.clone.1 | custom fusion | flops 524288 | bytes 6291488 | tf_op jit(solution)/shard_map/while/body/scatter-add | solution.py:61
  233.2 4.3 scatter_fusion.1
  237.6 184.4 %all-reduce.4.cloned.1.call-done = f32[4096,256]{1,0:T(8,128)} async-done(((f32[4096,256]{1,0:T(8,128)}), f32[4096,256]{1,0:T(8,128)}) %all-reduce.4.cloned.1.call-update) | async-done | bytes 4194320 | tf_op jit(solution)/shard_map/psum | solution.py:70
  422.0 3.4 bitcast_add_fusion
  425.5 30.6 %reduce-scatter.2.cloned.1.call-done = f32[512,256]{1,0:T(8,128)} async-done(((f32[2048,256]{1,0:T(8,128)}), f32[512,256]{1,0:T(8,128)}) %reduce-scatter.2.cloned.1.call-update) | async-done | bytes 524304 | tf_op jit(solution)/shard_map/reduce_scatter | solution.py:74
  (55 shorter events, 31.3 us)
Async XLA Ops:
  6.5 25.4 %copy-start = (bf16[8,256,256]{2,1,0:T(8,128)(2,1)S(1)}, bf16[8,256,256]{2,1,0:T(8,128)(2,1)}, u32[]{:S(2)}) copy-start(bf16[8,256,256]{2,1,0:T(8,128)(2,1)} %param.8) | copy-start | bytes 3145732
  6.5 21.8 %all-gather.2.cloned.1.call-start = ((), (), s32[]{:S(2)}) async-start(), calls=%async_computation.1 | async-start | bytes 1310720 | tf_op jit(solution)/shard_map/all_gather | solution.py:27
  7.3 127.0 %all-reduce.6.cloned.1.call-start = ((), (), s32[]{:S(2)}) async-start(), calls=%async_computation.4 | async-start | bytes 4194304 | tf_op jit(solution)/shard_map/psum | solution.py:11
  28.4 3.5 copy-start.4
  31.2 390.8 %all-reduce.4.cloned.1.call-start = ((), (), s32[]{:S(2)}) async-start(), calls=%async_computation.2 | async-start | bytes 8388608 | tf_op jit(solution)/shard_map/psum | solution.py:70
  134.3 2.4 copy-start.6
  148.9 2.4 copy-start.7
  160.0 1.0 copy-start.2
  188.9 1.0 copy-start.2
  217.5 1.0 copy-start.2
  237.5 184.5 %copy-start.3 = (f32[8,256,256]{2,1,0:T(8,128)S(1)}, f32[8,256,256]{2,1,0:T(8,128)}, u32[]{:S(2)}) copy-start(f32[8,256,256]{2,1,0:T(8,128)} %get-tuple-element.59) | copy-start | bytes 6291460
  237.5 218.5 %reduce-scatter.2.cloned.1.call-start = ((), (), s32[]{:S(2)}) async-start(), calls=%async_computation.3 | async-start | bytes 2621440 | tf_op jit(solution)/shard_map/reduce_scatter | solution.py:74
  422.0 35.9 %copy-start.1 = (bf16[8,256,256]{2,1,0:T(8,128)(2,1)S(1)}, bf16[8,256,256]{2,1,0:T(8,128)(2,1)}, u32[]{:S(2)}) copy-start(bf16[8,256,256]{2,1,0:T(8,128)(2,1)} %param.8) | copy-start | bytes 3145732
  425.4 30.6 %copy-start.5 = (bf16[512,256]{1,0:T(8,128)(2,1)S(1)}, bf16[512,256]{1,0:T(8,128)(2,1)}, u32[]{:S(2)}) copy-start(bf16[512,256]{1,0:T(8,128)(2,1)} %param.7) | copy-start | bytes 786436
Sparse Core Ops, SparseCore 0:
  8.9 19.4 all-gather.1
  32.0 102.1 all-reduce.5
  237.7 184.2 all-reduce.3
  425.6 30.4 reduce-scatter.1
where the time goes:
time: 466 us; the launch traced here: 464 us
  waiting for transfers between devices  322 us (69%)
  local copies, waits for them, and re-layouts  59.7 us (13%)
  other arithmetic  37.6 us (8%)
  matrix products  31 us (7%)
  between operations  13.9 us (3%)
    psum x1, waiting for transfers between devices, local(): tgt_total = lax.psum(grad_tgt, 'row')  184 us
    psum x1, waiting for transfers between devices, broadcast(): return lax.psum(kept, axis)  85.3 us
    reduce_scatter x1, waiting for transfers between devices, local(): summed = lax.psum_scatter(src_terms, 'col', scatter_dimension=0, tiled=True)  30.6 us
    all_gather x1, waiting for transfers between devices, local(): source = lax.all_gather(factors, 'col', axis=0, tiled=True)  21.1 us
    gather x3, local copies, waits for them, and re-layouts, group_pass(): right_rel = right_core[relation, tgt_index]  19.2 us
    scatter-add x3, other arithmetic, group_pass(): grad_src.at[src_index].add(src_grad)  14.8 us
    scatter-add x3, other arithmetic, group_pass(): grad_tgt.at[tgt_index].add(tgt_grad)  12.8 us
    gather x3, local copies, waits for them, and re-layouts, group_pass(): left = left_core[relation, src_index]  12 us
  transfers between devices with their start and end apart: 4, of which 4 were waited for; matrix products, arithmetic and copies ran while one was open for 4% of the time, Pallas kernels for 0%

commit v1 on v0

v1 whole, which is shorter than its diff:
```python
import functools

import jax
import jax.numpy as jnp
from jax import lax
from jax.experimental import pallas as pl
from jax.experimental.pallas import tpu as pltpu
from jax.sharding import Mesh
from jax.sharding import PartitionSpec as P

weight_decay = 1.0
AXES = ("zz", "xx", "col")
UNROLL = 4
CONTRACT_LAST = (((1,), (1,)), ((), ()))
CONTRACT_FIRST = (((0,), (0,)), ((), ()))


def dot(a, b, dims=(((1,), (0,)), ((), ()))):
    return lax.dot_general(a, b, dims, preferred_element_type=jnp.float32)


def slots_kernel(n_col, ratio, scalars, coords, cores_ref, *refs):
    n_src, n_tgt = n_col, n_col * ratio
    src_refs, refs = refs[:n_src], refs[n_src:]
    tgt_refs, refs = refs[:n_tgt], refs[n_tgt:]
    tiles_ref, gt_out, keep_out, send_out = refs[:4]
    src, tgt, tile_buf, gs_acc, gt_acc, tile_sems, sems = refs[4:]
    cap, tile = tile_buf.shape[0], tile_buf.shape[1]
    rows = src_refs[0].shape[0]
    plane, x_pos, col_pos, live = scalars[0], scalars[1], scalars[2], scalars[3]

    for s in range(cap):
        pltpu.make_async_copy(tiles_ref.at[s], tile_buf.at[s], tile_sems.at[s]).start()
    copies = []
    for o in range(n_src):
        at = pl.multiple_of((col_pos ^ o) * rows, rows)
        copies.append(pltpu.make_async_copy(src_refs[o], src.at[pl.ds(at, rows)], sems.at[o]))
    for d in range(n_col):
        for s in range(ratio):
            part = lax.rem(x_pos + (ratio - s), ratio) * n_col + (plane ^ d)
            at = pl.multiple_of(part * rows, rows)
            index = d * ratio + s
            copies.append(
                pltpu.make_async_copy(tgt_refs[index], tgt.at[pl.ds(at, rows)], sems.at[n_src + index])
            )
    for copy in copies:
        copy.start()
    gs_acc[...] = jnp.zeros_like(gs_acc)
    gt_acc[...] = jnp.zeros_like(gt_acc)
    for copy in copies:
        copy.wait()
    for s in range(cap):
        pltpu.make_async_copy(tiles_ref.at[s], tile_buf.at[s], tile_sems.at[s]).wait()

    def group(g, carry):
        work = []
        for u in range(UNROLL):
            s = g * UNROLL + u
            k = coords[3 * s]
            a_at = pl.ds(pl.multiple_of(coords[3 * s + 1] * tile, tile), tile)
            b_at = pl.ds(pl.multiple_of(coords[3 * s + 2] * tile, tile), tile)
            core = cores_ref[k]
            right = tgt[b_at]
            left = dot(src[a_at], core).astype(jnp.bfloat16)
            right_rel = dot(right, core, CONTRACT_LAST).astype(jnp.bfloat16)
            predicted = dot(left, right, CONTRACT_LAST)
            resid = jnp.where(s < live, tile_buf[s].astype(jnp.float32) - predicted, 0.0)
            resid = resid.astype(jnp.bfloat16)
            work.append((a_at, b_at, dot(resid, right_rel), dot(resid, left, CONTRACT_FIRST)))
        for a_at, b_at, src_grad, tgt_grad in work:
            gs_acc[a_at] += src_grad
            gt_acc[b_at] += tgt_grad
        return carry

    lax.fori_loop(0, (live + UNROLL - 1) // UNROLL, group, 0)
    gt_out[...] = gt_acc[...].astype(gt_out.dtype)
    bit = col_pos & 1
    for h in range(n_col // 2):
        at = pl.multiple_of((2 * h + bit) * rows, rows)
        keep_out[h] = gs_acc[pl.ds(at, rows)]
        at = pl.multiple_of((2 * h + 1 - bit) * rows, rows)
        send_out[h] = gs_acc[pl.ds(at, rows)]


def swap(value, bit, n_col):
    return lax.ppermute(value, "col", [(i, i ^ bit) for i in range(n_col)])


def local(factors, cores, tiles, tile_coords, tile_counts):
    planes = lax.axis_size("zz")
    ratio = lax.axis_size("xx")
    n_col = lax.axis_size("col")
    rows, rank = factors.shape
    cap, tile = tiles.shape[0], tiles.shape[1]
    plane, x_pos, col_pos = lax.axis_index("zz"), lax.axis_index("xx"), lax.axis_index("col")

    tgt_parts = []
    for d in range(n_col):
        pairs = [
            ((p * ratio + x) * n_col + q, ((q ^ d) * ratio + x) * n_col + p)
            for p in range(planes)
            for x in range(ratio)
            for q in range(n_col)
        ]
        tgt_parts.append(lax.ppermute(factors, AXES, pairs))
    src_parts = {0: factors}
    bit = n_col // 2
    while bit:
        for o, value in list(src_parts.items()):
            src_parts[o | bit] = swap(value, bit, n_col)
        bit //= 2
    tgt_all = []
    for d in range(n_col):
        tgt_all.append(tgt_parts[d])
        for s in range(1, ratio):
            pairs = [(x, (x + s) % ratio) for x in range(ratio)]
            tgt_all.append(lax.ppermute(tgt_parts[d], "xx", pairs))

    scalars = jnp.stack([plane, x_pos, col_pos, tile_counts[0]]).astype(jnp.int32)
    src_rows, tgt_rows = n_col * rows, n_col * ratio * rows
    any_spec = pl.BlockSpec(memory_space=pl.ANY)
    vmem_spec = pl.BlockSpec(memory_space=pltpu.VMEM)
    smem_spec = pl.BlockSpec(memory_space=pltpu.SMEM)
    n_parts = n_col + n_col * ratio
    half = jax.ShapeDtypeStruct((n_col // 2, rows, rank), jnp.float32)
    tgt_grad, src_keep, src_send = pl.pallas_call(
        functools.partial(slots_kernel, n_col, ratio),
        out_shape=[jax.ShapeDtypeStruct((tgt_rows, rank), jnp.bfloat16), half, half],
        in_specs=[smem_spec, smem_spec, vmem_spec] + [any_spec] * (n_parts + 1),
        out_specs=[vmem_spec] * 3,
        scratch_shapes=[
            pltpu.VMEM((src_rows, rank), factors.dtype),
            pltpu.VMEM((tgt_rows, rank), factors.dtype),
            pltpu.VMEM(tiles.shape, tiles.dtype),
            pltpu.VMEM((src_rows, rank), jnp.float32),
            pltpu.VMEM((tgt_rows, rank), jnp.float32),
            pltpu.SemaphoreType.DMA((cap,)),
            pltpu.SemaphoreType.DMA((n_parts,)),
        ],
        compiler_params=pltpu.CompilerParams(vmem_limit_bytes=40 * 2**20),
        cost_estimate=pl.CostEstimate(
            flops=cap * 5 * 2 * tile**3, bytes_accessed=16 * 2**20, transcendentals=0
        ),
    )(scalars, tile_coords.reshape(-1), cores, *[src_parts[o] for o in range(n_col)], *tgt_all, tiles)

    recv = swap(src_send, 1, n_col)
    arrived = lax.all_to_all(tgt_grad, ("xx", "col"), 0, 0, tiled=True)
    src_sum = src_keep + recv
    bit = 2
    while bit < n_col:
        pairs = src_sum.reshape(src_sum.shape[0] // 2, 2, rows, rank)
        mine = (col_pos // bit) % 2
        out = lax.dynamic_index_in_dim(pairs, 1 - mine, 1, keepdims=False).astype(jnp.bfloat16)
        kept = lax.dynamic_index_in_dim(pairs, mine, 1, keepdims=False)
        src_sum = kept + swap(out, bit, n_col).astype(jnp.float32)
        bit *= 2
    summed = arrived.reshape(ratio, n_col, rows, rank).astype(jnp.float32).sum(0).astype(jnp.bfloat16)
    landed = lax.all_to_all(summed.reshape(n_col * rows, rank), "zz", 0, 0, tiled=True)
    tgt_sum = landed.reshape(planes, rows, rank).astype(jnp.float32).sum(0)
    return weight_decay * factors.astype(jnp.float32) - (src_sum[0] + tgt_sum) / tile


def solution(mesh):
    n_row, n_col = mesh.shape["row"], mesh.shape["col"]
    split = Mesh(mesh.devices.reshape(n_col, n_row // n_col, n_col), AXES)
    in_specs = (P(AXES, None), P(), P(AXES, None, None), P(AXES, None), P(AXES))
    return jax.shard_map(local, mesh=split, in_specs=in_specs, out_specs=P(AXES, None), check_vma=False)
```

time: 466 us -> 141 us (0.30)
  waiting for transfers between devices: 322 us -> 38.2 us
  local copies, waits for them, and re-layouts: 59.7 us -> 15.2 us
  starting transfers between devices: 0.12 us -> 32.9 us
  blocking collectives: 0 us -> 32.6 us
  other arithmetic: 37.6 us -> 5.74 us
  matrix products: 31 us -> 0 us
  Pallas kernels: 0 us -> 16.7 us
  between operations: 13.9 us -> 0.73 us
    psum x2 -> x0, waiting for transfers between devices: 270 us -> none  [the longest x1 184 us: local(): tgt_total = lax.psum(grad_tgt, 'row')]
    gather x9 -> x0, local copies, waits for them, and re-layouts: 37.8 us -> none  [the longest x3 19.2 us: group_pass(): right_rel = right_core[relation, tgt_index]]
    all_to_all x0 -> x1, blocking collectives: none -> 32.6 us  [local(): arrived = lax.all_to_all(tgt_grad, ('xx', 'col'), 0, 0, tiled=True)]
    dot_general x11 -> x0, matrix products: 31 us -> none  [the longest x1 9.71 us: local(): jnp.einsum('nr,ksr->kns', target, cores, preferred_element_type=jnp.float32)]
    reduce_scatter x1 -> x0, waiting for transfers between devices: 30.6 us -> none  [local(): summed = lax.psum_scatter(src_terms, 'col', scatter_dimension=0, tiled=True)]
    scatter-add x6 -> x0, other arithmetic: 27.5 us -> none  [the longest x3 14.8 us: group_pass(): grad_src.at[src_index].add(src_grad)]
    all_gather x1 -> x0, waiting for transfers between devices: 21.1 us -> none  [local(): source = lax.all_gather(factors, 'col', axis=0, tiled=True)]
    all_to_all x0 -> x1, waiting for transfers between devices: none -> 20.1 us  [local(): lax.all_to_all(summed.reshape(n_col * rows, rank), 'zz', 0, 0, tiled=True)]
  transfers between devices with their start and end apart: 4 -> 14, of which waited for: 4 -> 5; matrix products, arithmetic and copies ran while one was open for 4% -> 2% of each run, Pallas kernels for 0% -> 0%
where the time goes in v1:
time: 141 us; the launch traced here: 142 us
  waiting for transfers between devices  38.2 us (27%)
  starting transfers between devices  32.9 us (23%)
  blocking collectives  32.6 us (23%)
  Pallas kernels  16.7 us (12%)
  local copies, waits for them, and re-layouts  15.2 us (11%)
  other arithmetic  5.74 us (4%)
    all_to_all x1, blocking collectives, local(): arrived = lax.all_to_all(tgt_grad, ('xx', 'col'), 0, 0, tiled=True)  32.6 us
    all_to_all x1, waiting for transfers between devices, local(): lax.all_to_all(summed.reshape(n_col * rows, rank), 'zz', 0, 0, tiled=True)  20.1 us
    pallas_call x1, Pallas kernels, local(): pl.pallas_call(functools.partial(slots_kernel, n_col, ratio), out_shape=[...  16.7 us
    unnamed x33, local copies, waits for them, and re-layouts  15 us
    all_to_all x1, starting transfers between devices, local(): lax.all_to_all(summed.reshape(n_col * rows, rank), 'zz', 0, 0, tiled=True)  14.4 us
    ppermute x4, starting transfers between devices, local(): tgt_parts.append(lax.ppermute(factors, AXES, pairs))  8.97 us
    ppermute x4, waiting for transfers between devices, local(): tgt_parts.append(lax.ppermute(factors, AXES, pairs))  8.35 us
    ppermute x4, waiting for transfers between devices, local(): tgt_all.append(lax.ppermute(tgt_parts[d], 'xx', pairs))  6.87 us
  transfers between devices with their start and end apart: 14, of which 5 were waited for; matrix products, arithmetic and copies ran while one was open for 2% of the time, Pallas kernels for 0%

profile of v1, /device:TPU:0, one launch (start us, length us, event | category | flops | bytes accessed | tf_op | source)
XLA Modules:
  0.0 142.0 jit_solution(14604636176660299626)
XLA Ops:
  0.5 2.5 %collective-permute-start.1 = (bf16[512,256]{1,0:T(8,128)(2,1)}, bf16[512,256]{1,0:T(8,128)(2,1)S(1)}, u32[]{:S(2)}, u32[]{:S(2)}) collective-permute-start(bf16[512,256]{1,0:T(8,128)(2,1)} %refs_0_.1), channel_id=1, source_target_pairs={{0,2},{1,3},{2,0},{3,1},{4,6},{5,7},{6,4},{7,5},{8,10},{9,11},{10,... | collective-permute-start | bytes 786440 | tf_op jit(solution)/shard_map/ppermute | solution.py:86
  3.0 1.6 %collective-permute-start.3 = (bf16[512,256]{1,0:T(8,128)(2,1)}, bf16[512,256]{1,0:T(8,128)(2,1)S(1)}, u32[]{:S(2)}, u32[]{:S(2)}) collective-permute-start(bf16[512,256]{1,0:T(8,128)(2,1)} %refs_0_.1), channel_id=1, source_target_pairs={{0,0},{1,8},{2,16},{3,24},{4,4},{5,12},{6,20},{7,28},{8,1},{9,9},{... | collective-permute-start | bytes 786440 | tf_op jit(solution)/shard_map/ppermute | solution.py:105
  4.6 2.2 %collective-permute-start.5 = (bf16[512,256]{1,0:T(8,128)(2,1)}, bf16[512,256]{1,0:T(8,128)(2,1)S(1)}, u32[]{:S(2)}, u32[]{:S(2)}) collective-permute-start(bf16[512,256]{1,0:T(8,128)(2,1)} %refs_0_.1), channel_id=1, source_target_pairs={{0,8},{1,0},{2,24},{3,16},{4,12},{5,4},{6,28},{7,20},{8,9},{9,1},{... | collective-permute-start | bytes 786440 | tf_op jit(solution)/shard_map/ppermute | solution.py:105
  6.8 3.5 %collective-permute-start.7 = (bf16[512,256]{1,0:T(8,128)(2,1)}, bf16[512,256]{1,0:T(8,128)(2,1)S(1)}, u32[]{:S(2)}, u32[]{:S(2)}) collective-permute-start(bf16[512,256]{1,0:T(8,128)(2,1)} %refs_0_.1), channel_id=1, source_target_pairs={{0,16},{1,24},{2,0},{3,8},{4,20},{5,28},{6,4},{7,12},{8,17},{9,25}... | collective-permute-start | bytes 786440 | tf_op jit(solution)/shard_map/ppermute | solution.py:105
  10.3 1.7 %collective-permute-start.9 = (bf16[512,256]{1,0:T(8,128)(2,1)}, bf16[512,256]{1,0:T(8,128)(2,1)S(1)}, u32[]{:S(2)}, u32[]{:S(2)}) collective-permute-start(bf16[512,256]{1,0:T(8,128)(2,1)} %refs_0_.1), channel_id=1, source_target_pairs={{0,24},{1,16},{2,8},{3,0},{4,28},{5,20},{6,12},{7,4},{8,25},{9,17}... | collective-permute-start | bytes 786440 | tf_op jit(solution)/shard_map/ppermute | solution.py:105
  12.1 1.5 %collective-permute-start.4 = (bf16[512,256]{1,0:T(8,128)(2,1)S(1)}, bf16[512,256]{1,0:T(8,128)(2,1)S(1)}, u32[]{:S(2)}, u32[]{:S(2)}) collective-permute-start(bf16[512,256]{1,0:T(8,128)(2,1)S(1)} %collective-permute-done.3.refs_4_), channel_id=1, source_target_pairs={{0,4},{4,0},{1,5},{5,1},{2,6},{6,2},{3,7},{7,3},{8,12},{12,8},{9,1... | collective-permute-start | bytes 786440 | tf_op jit(solution)/shard_map/ppermute | solution.py:117
  14.4 8.3 %collective-permute-done.7.refs_8_ = bf16[512,256]{1,0:T(8,128)(2,1)S(1)} collective-permute-done((bf16[512,256]{1,0:T(8,128)(2,1)}, bf16[512,256]{1,0:T(8,128)(2,1)S(1)}, u32[]{:S(2)}, u32[]{:S(2)}) %collective-permute-start.7) | collective-permute-done | bytes 262176 | tf_op jit(solution)/shard_map/ppermute | solution.py:105
  22.8 1.5 %collective-permute-start.8 = (bf16[512,256]{1,0:T(8,128)(2,1)S(1)}, bf16[512,256]{1,0:T(8,128)(2,1)S(1)}, u32[]{:S(2)}, u32[]{:S(2)}) collective-permute-start(bf16[512,256]{1,0:T(8,128)(2,1)S(1)} %collective-permute-done.7.refs_8_), channel_id=1, source_target_pairs={{0,4},{4,0},{1,5},{5,1},{2,6},{6,2},{3,7},{7,3},{8,12},{12,8},{9,1... | collective-permute-start | bytes 786440 | tf_op jit(solution)/shard_map/ppermute | solution.py:117
  24.3 1.4 collective-permute-start.10
  30.1 2.0 %collective-permute-done.8.refs_9_ = bf16[512,256]{1,0:T(8,128)(2,1)S(1)} collective-permute-done((bf16[512,256]{1,0:T(8,128)(2,1)S(1)}, bf16[512,256]{1,0:T(8,128)(2,1)S(1)}, u32[]{:S(2)}, u32[]{:S(2)}) %collective-permute-start.8) | collective-permute-done | bytes 262176 | tf_op jit(solution)/shard_map/ppermute | solution.py:117
  32.7 4.9 %collective-permute-done.10.refs_11_ = bf16[512,256]{1,0:T(8,128)(2,1)S(1)} collective-permute-done((bf16[512,256]{1,0:T(8,128)(2,1)S(1)}, bf16[512,256]{1,0:T(8,128)(2,1)S(1)}, u32[]{:S(2)}, u32[]{:S(2)}) %collective-permute-start.10) | collective-permute-done | bytes 262176 | tf_op jit(solution)/shard_map/ppermute | solution.py:117
  38.3 0.9 copy-done
  39.3 2.2 %copy-done.2 = bf16[32,256,256]{2,1,0:T(8,128)(2,1)S(1)} copy-done((bf16[32,256,256]{2,1,0:T(8,128)(2,1)S(1)}, bf16[32,256,256]{2,1,0:T(8,128)(2,1)}, u32[]{:S(2)}) %copy-start.2) | copy-done | bytes 4194328
  41.5 1.2 copy-done.3
  43.7 0.9 copy-done.7
  44.6 0.9 copy-done.9
  48.4 16.7 %shard_map.55 = (bf16[4096,256]{1,0:T(8,128)(2,1)S(1)}, f32[2,512,256]{2,1,0:T(8,128)S(1)}, f32[2,512,256]{2,1,0:T(8,128)S(1)}) custom-call(s32[4]{0:T(128)S(1)} %pad_add_fusion.scalars, s32[96]{0:T(128)S(1)} %reshape.22.coords, bf16[8,256,256]{2,1,0:T(8,128)(2,1)S(1)} %copy-done.3, bf16[512,256]{1,0:T(8,128)(2,1)S(1)} %copy-done, ...), custom_call_target="tpu_custom_call" | custom-call | flops 5368709120 | bytes 16777216 | tf_op jit(solution)/shard_map/pallas_call | solution.py:126
  65.1 32.6 %all_to_all.15 = bf16[8,512,256]{2,1,0:T(8,128)(2,1)} all-to-all(bf16[8,512,256]{2,1,0:T(8,128)(2,1)S(1)} %bitcast.11), channel_id=1, replica_groups=mesh['zz'=4,'xx'=2,'col'=4] {'xx','col'}, dimensions={0} | all-to-all | bytes 4194304 | tf_op jit(solution)/shard_map/all_to_all | solution.py:147
  97.7 3.2 %reduce_sum.21 = bf16[4,512,256]{2,1,0:T(8,128)(2,1)} reduce(bf16[2,4,512,256]{3,2,1,0:T(8,128)(2,1)} %bitcast.12, bf16[]{:T(256)} %constant.49.clone.1), dimensions={0}, to_apply=%region_0.1 | reduce | flops 524288 | bytes 3145730 | tf_op jit(solution)/shard_map/reduce_sum | solution.py:157
  100.9 14.4 %all-to-all-start.1 = ((bf16[4,512,256]{2,1,0:T(8,128)(2,1)}), bf16[4,512,256]{2,1,0:T(8,128)(2,1)S(1)}, u32[]{:S(2)}, u32[]{:S(2)}) async-start(bf16[4,512,256]{2,1,0:T(8,128)(2,1)} %reduce_sum.21), calls=%async_computation.1 | async-start | bytes 2097152 | tf_op jit(solution)/shard_map/all_to_all | solution.py:158
  115.3 2.8 %collective-permute-done.11 = f32[2,512,256]{2,1,0:T(8,128)} collective-permute-done((f32[2,512,256]{2,1,0:T(8,128)S(1)}, f32[2,512,256]{2,1,0:T(8,128)}, u32[]{:S(2)}, u32[]{:S(2)}) %collective-permute-start.11) | collective-permute-done | bytes 1048608 | tf_op jit(solution)/shard_map/ppermute | solution.py:86
  118.1 1.4 add.22
  119.5 1.3 collective-permute-start.12
  120.8 20.1 %all-to-all-done.1 = bf16[4,512,256]{2,1,0:T(8,128)(2,1)S(1)} async-done(((bf16[4,512,256]{2,1,0:T(8,128)(2,1)}), bf16[4,512,256]{2,1,0:T(8,128)(2,1)S(1)}, u32[]{:S(2)}, u32[]{:S(2)}) %all-to-all-start.1) | async-done | bytes 1048608 | tf_op jit(solution)/shard_map/all_to_all | solution.py:158
  (46 shorter events, 11.5 us)
Async XLA Ops:
  0.0 10.3 %collective-permute-start = (bf16[512,256]{1,0:T(8,128)(2,1)}, bf16[512,256]{1,0:T(8,128)(2,1)S(1)}, u32[]{:S(2)}, u32[]{:S(2)}) collective-permute-start(bf16[512,256]{1,0:T(8,128)(2,1)} %refs_0_.1), channel_id=1, source_target_pairs={{0,1},{1,0},{2,3},{3,2},{4,5},{5,4},{6,7},{7,6},{8,9},{9,8},{10,11... | collective-permute-start | bytes 786440 | tf_op jit(solution)/shard_map/ppermute | solution.py:86
  0.5 11.5 %collective-permute-start.1 = (bf16[512,256]{1,0:T(8,128)(2,1)}, bf16[512,256]{1,0:T(8,128)(2,1)S(1)}, u32[]{:S(2)}, u32[]{:S(2)}) collective-permute-start(bf16[512,256]{1,0:T(8,128)(2,1)} %refs_0_.1), channel_id=1, source_target_pairs={{0,2},{1,3},{2,0},{3,1},{4,6},{5,7},{6,4},{7,5},{8,10},{9,11},{10,... | collective-permute-start | bytes 786440 | tf_op jit(solution)/shard_map/ppermute | solution.py:86
  3.0 9.1 %collective-permute-start.3 = (bf16[512,256]{1,0:T(8,128)(2,1)}, bf16[512,256]{1,0:T(8,128)(2,1)S(1)}, u32[]{:S(2)}, u32[]{:S(2)}) collective-permute-start(bf16[512,256]{1,0:T(8,128)(2,1)} %refs_0_.1), channel_id=1, source_target_pairs={{0,0},{1,8},{2,16},{3,24},{4,4},{5,12},{6,20},{7,28},{8,1},{9,9},{... | collective-permute-start | bytes 786440 | tf_op jit(solution)/shard_map/ppermute | solution.py:105
  4.6 9.0 %collective-permute-start.5 = (bf16[512,256]{1,0:T(8,128)(2,1)}, bf16[512,256]{1,0:T(8,128)(2,1)S(1)}, u32[]{:S(2)}, u32[]{:S(2)}) collective-permute-start(bf16[512,256]{1,0:T(8,128)(2,1)} %refs_0_.1), channel_id=1, source_target_pairs={{0,8},{1,0},{2,24},{3,16},{4,12},{5,4},{6,28},{7,20},{8,9},{9,1},{... | collective-permute-start | bytes 786440 | tf_op jit(solution)/shard_map/ppermute | solution.py:105
  6.8 16.0 %collective-permute-start.7 = (bf16[512,256]{1,0:T(8,128)(2,1)}, bf16[512,256]{1,0:T(8,128)(2,1)S(1)}, u32[]{:S(2)}, u32[]{:S(2)}) collective-permute-start(bf16[512,256]{1,0:T(8,128)(2,1)} %refs_0_.1), channel_id=1, source_target_pairs={{0,16},{1,24},{2,0},{3,8},{4,20},{5,28},{6,4},{7,12},{8,17},{9,25}... | collective-permute-start | bytes 786440 | tf_op jit(solution)/shard_map/ppermute | solution.py:105
  10.3 14.0 %collective-permute-start.9 = (bf16[512,256]{1,0:T(8,128)(2,1)}, bf16[512,256]{1,0:T(8,128)(2,1)S(1)}, u32[]{:S(2)}, u32[]{:S(2)}) collective-permute-start(bf16[512,256]{1,0:T(8,128)(2,1)} %refs_0_.1), channel_id=1, source_target_pairs={{0,24},{1,16},{2,8},{3,0},{4,28},{5,20},{6,12},{7,4},{8,25},{9,17}... | collective-permute-start | bytes 786440 | tf_op jit(solution)/shard_map/ppermute | solution.py:105
  12.0 16.0 %collective-permute-start.2 = (bf16[512,256]{1,0:T(8,128)(2,1)S(1)}, bf16[512,256]{1,0:T(8,128)(2,1)S(1)}, u32[]{:S(2)}, u32[]{:S(2)}) collective-permute-start(bf16[512,256]{1,0:T(8,128)(2,1)S(1)} %collective-permute-done.1.refs_2_), channel_id=1, source_target_pairs={{0,1},{1,0},{2,3},{3,2},{4,5},{5,4},{6,7},{7,6},{8,9},{9,8},{10,11... | collective-permute-start | bytes 786440 | tf_op jit(solution)/shard_map/ppermute | solution.py:86
  12.1 16.6 %collective-permute-start.4 = (bf16[512,256]{1,0:T(8,128)(2,1)S(1)}, bf16[512,256]{1,0:T(8,128)(2,1)S(1)}, u32[]{:S(2)}, u32[]{:S(2)}) collective-permute-start(bf16[512,256]{1,0:T(8,128)(2,1)S(1)} %collective-permute-done.3.refs_4_), channel_id=1, source_target_pairs={{0,4},{4,0},{1,5},{5,1},{2,6},{6,2},{3,7},{7,3},{8,12},{12,8},{9,1... | collective-permute-start | bytes 786440 | tf_op jit(solution)/shard_map/ppermute | solution.py:117
  13.6 15.8 %collective-permute-start.6 = (bf16[512,256]{1,0:T(8,128)(2,1)S(1)}, bf16[512,256]{1,0:T(8,128)(2,1)S(1)}, u32[]{:S(2)}, u32[]{:S(2)}) collective-permute-start(bf16[512,256]{1,0:T(8,128)(2,1)S(1)} %collective-permute-done.5.refs_6_), channel_id=1, source_target_pairs={{0,4},{4,0},{1,5},{5,1},{2,6},{6,2},{3,7},{7,3},{8,12},{12,8},{9,1... | collective-permute-start | bytes 786440 | tf_op jit(solution)/shard_map/ppermute | solution.py:117
  22.8 9.2 %collective-permute-start.8 = (bf16[512,256]{1,0:T(8,128)(2,1)S(1)}, bf16[512,256]{1,0:T(8,128)(2,1)S(1)}, u32[]{:S(2)}, u32[]{:S(2)}) collective-permute-start(bf16[512,256]{1,0:T(8,128)(2,1)S(1)} %collective-permute-done.7.refs_8_), channel_id=1, source_target_pairs={{0,4},{4,0},{1,5},{5,1},{2,6},{6,2},{3,7},{7,3},{8,12},{12,8},{9,1... | collective-permute-start | bytes 786440 | tf_op jit(solution)/shard_map/ppermute | solution.py:117
  24.3 13.4 %collective-permute-start.10 = (bf16[512,256]{1,0:T(8,128)(2,1)S(1)}, bf16[512,256]{1,0:T(8,128)(2,1)S(1)}, u32[]{:S(2)}, u32[]{:S(2)}) collective-permute-start(bf16[512,256]{1,0:T(8,128)(2,1)S(1)} %collective-permute-done.9.refs_10_), channel_id=1, source_target_pairs={{0,4},{4,0},{1,5},{5,1},{2,6},{6,2},{3,7},{7,3},{8,12},{12,8},{9,1... | collective-permute-start | bytes 786440 | tf_op jit(solution)/shard_map/ppermute | solution.py:117
  38.3 0.9 copy-start
  39.3 2.2 %copy-start.2 = (bf16[32,256,256]{2,1,0:T(8,128)(2,1)S(1)}, bf16[32,256,256]{2,1,0:T(8,128)(2,1)}, u32[]{:S(2)}) copy-start(bf16[32,256,256]{2,1,0:T(8,128)(2,1)} %refs_12_.1) | copy-start | bytes 12582916
  41.5 1.2 copy-start.3
  42.7 0.9 copy-start.5
  43.7 0.9 copy-start.7
  44.6 0.9 copy-start.9
  45.6 0.9 copy-start.11
  46.5 0.9 copy-start.13
  47.5 0.9 copy-start.15
  100.9 40.0 %all-to-all-start.1 = ((bf16[4,512,256]{2,1,0:T(8,128)(2,1)}), bf16[4,512,256]{2,1,0:T(8,128)(2,1)S(1)}, u32[]{:S(2)}, u32[]{:S(2)}) async-start(bf16[4,512,256]{2,1,0:T(8,128)(2,1)} %reduce_sum.21), calls=%async_computation.1 | async-start | bytes 2097152 | tf_op jit(solution)/shard_map/all_to_all | solution.py:158
  115.3 2.8 %collective-permute-start.11 = (f32[2,512,256]{2,1,0:T(8,128)S(1)}, f32[2,512,256]{2,1,0:T(8,128)}, u32[]{:S(2)}, u32[]{:S(2)}) collective-permute-start(f32[2,512,256]{2,1,0:T(8,128)S(1)} %get-tuple-element.9), channel_id=1, source_target_pairs={{0,1},{1,0},{2,3},{3,2},{4,5},{5,4},{6,7},{7,6},{8,9},{9,8},{10,11... | collective-permute-start | bytes 3145736 | tf_op jit(solution)/shard_map/ppermute | solution.py:86
  118.1 23.1 %copy-start.1 = (bf16[512,256]{1,0:T(8,128)(2,1)S(1)}, bf16[512,256]{1,0:T(8,128)(2,1)}, u32[]{:S(2)}) copy-start(bf16[512,256]{1,0:T(8,128)(2,1)} %refs_0_.1) | copy-start | bytes 786436
  119.5 21.6 %collective-permute-start.12 = (bf16[1,512,256]{2,1,0:T(8,128)(2,1)S(1)}, bf16[1,512,256]{2,1,0:T(8,128)(2,1)S(1)}, u32[]{:S(2)}, u32[]{:S(2)}) collective-permute-start(bf16[1,512,256]{2,1,0:T(8,128)(2,1)S(1)} %dynamic-slice_convert_fusion), channel_id=1, source_target_pairs={{0,2},{1,3},{2,0},{3,1},{4,6},{5,7},{6,4},{7,5},{8,10},{9,11},{10,... | collective-permute-start | bytes 786440 | tf_op jit(solution)/shard_map/ppermute | solution.py:86
  (6 other events, 4.2 us)

commit v2 on v1

v2 whole, which is shorter than its diff:
```python
import functools

import jax
import jax.numpy as jnp
from jax import lax
from jax.experimental import pallas as pl
from jax.experimental.pallas import tpu as pltpu
from jax.sharding import Mesh
from jax.sharding import PartitionSpec as P

weight_decay = 1.0
AXES = ("zz", "xx", "col")
UNROLL = 8
CONTRACT_LAST = (((1,), (1,)), ((), ()))
CONTRACT_FIRST = (((0,), (0,)), ((), ()))


def dot(a, b, dims=(((1,), (0,)), ((), ()))):
    return lax.dot_general(a, b, dims, preferred_element_type=jnp.float32)


def mirror(value, size):
    out, bit = 0, 1
    while bit < size:
        out = out * 2 + (value // bit) % 2
        bit *= 2
    return out


def slots_kernel(first, last, n_col, ratio, scalars, coords, cores_hbm, *refs):
    n_x = last - first
    opens, closes = first == 0, last == ratio
    src_refs, refs = refs[:n_col], refs[n_col:]
    tgt_refs, refs = refs[: n_col * n_x], refs[n_col * n_x :]
    tiles_hbm, refs = refs[0], refs[1:]
    if not opens:
        gs_in, refs = refs[0], refs[2:]
    gt_out, refs = refs[0], refs[1:]
    gs_outs, refs = (refs[:2], refs[2:]) if closes else (refs[:1], refs[1:])
    cores, src, tgt, tiles, resids, left, right, gs_acc, gt_acc, slot_of, tgt_of, sems = refs
    cap, tile = tiles.shape[0], tiles.shape[1]
    rows = src_refs[0].shape[0]
    block = n_col * rows
    plane, x_pos, col_pos, live = scalars[0], scalars[1], scalars[2], scalars[3]

    copies = [pltpu.make_async_copy(cores_hbm, cores, sems.at[0])]
    for o in range(n_col):
        at = pl.multiple_of((col_pos ^ o) * rows, rows)
        copies.append(pltpu.make_async_copy(src_refs[o], src.at[pl.ds(at, rows)], sems.at[1 + o]))
    for d in range(n_col):
        part = mirror(plane ^ col_pos ^ d, n_col)
        for n in range(n_x):
            at = pl.multiple_of((n * n_col + part) * rows, rows)
            index = d * n_x + n
            copies.append(
                pltpu.make_async_copy(tgt_refs[index], tgt.at[pl.ds(at, rows)], sems.at[1 + n_col + index])
            )
    if not opens:
        copies.append(pltpu.make_async_copy(gs_in, gs_acc, sems.at[1 + n_col * (n_x + 1)]))
    tiles_copy = pltpu.make_async_copy(tiles_hbm, tiles, sems.at[2 + n_col * (n_x + 1)])
    for copy in copies:
        copy.start()
    tiles_copy.start()
    if opens:
        gs_acc[...] = jnp.zeros_like(gs_acc)
    gt_acc[...] = jnp.zeros_like(gt_acc)

    def choose(s, count):
        b = coords[3 * s + 2]
        step = lax.rem(x_pos - b // (block // tile) + ratio, ratio)
        taken = (step >= first) & (step < last)
        slot_of[count] = s
        tgt_of[count] = (step - first) * (block // tile) + lax.rem(b, block // tile)
        return count + taken.astype(jnp.int32)

    count = lax.fori_loop(0, live, choose, 0)
    for u in range(UNROLL):
        slot_of[count + u] = 0
        tgt_of[count + u] = 0
    groups = (count + UNROLL - 1) // UNROLL
    for copy in copies:
        copy.wait()

    def place(index):
        return pl.ds(pl.multiple_of(index * tile, tile), tile)

    def products(g, carry):
        for u in range(UNROLL):
            i = g * UNROLL + u
            s = slot_of[i]
            core = cores[coords[3 * s]]
            left[i] = dot(src[place(coords[3 * s + 1])], core).astype(jnp.bfloat16)
            right[i] = dot(tgt[place(tgt_of[i])], core, CONTRACT_LAST).astype(jnp.bfloat16)
        return carry

    def residuals(g, carry):
        for u in range(UNROLL):
            i = g * UNROLL + u
            s = slot_of[i]
            predicted = dot(left[i], tgt[place(tgt_of[i])], CONTRACT_LAST)
            resid = jnp.where(i < count, tiles[s].astype(jnp.float32) - predicted, 0.0)
            resids[i] = resid.astype(jnp.bfloat16)
        return carry

    def gradients(g, carry):
        for u in range(UNROLL):
            i = g * UNROLL + u
            resid = resids[i]
            gs_acc[place(coords[3 * slot_of[i] + 1])] += dot(resid, right[i])
            gt_acc[place(tgt_of[i])] += dot(resid, left[i], CONTRACT_FIRST)
        return carry

    lax.fori_loop(0, groups, products, 0)
    tiles_copy.wait()
    lax.fori_loop(0, groups, residuals, 0)
    lax.fori_loop(0, groups, gradients, 0)

    outs = []
    if closes:
        for h in range(n_col // 2):
            for n in range(2):
                at = pl.multiple_of((2 * h + ((col_pos + n) & 1)) * rows, rows)
                outs.append((gs_acc.at[pl.ds(at, rows)], gs_outs[n].at[h]))
    else:
        outs.append((gs_acc, gs_outs[0]))
    outs = [pltpu.make_async_copy(a, b, sems.at[i]) for i, (a, b) in enumerate(outs)]
    for copy in outs:
        copy.start()
    tgt[...] = gt_acc[...].astype(tgt.dtype)
    used = len(outs)
    for n in range(n_x):
        x_of = lax.rem(x_pos + (ratio - first - n), ratio)
        outs.append(pltpu.make_async_copy(tgt.at[pl.ds(n * block, block)], gt_out.at[x_of], sems.at[used + n]))
        outs[-1].start()
    for copy in outs:
        copy.wait()


def run_slots(first, last, n_col, ratio, scalars, coords, cores, src_parts, tgt_parts, tiles, carried):
    rows, rank = src_parts[0].shape
    cap, tile = tiles.shape[0], tiles.shape[1]
    n_x, block = last - first, n_col * rows
    any_spec = pl.BlockSpec(memory_space=pl.ANY)
    smem_spec = pl.BlockSpec(memory_space=pltpu.SMEM)
    gt = jax.ShapeDtypeStruct((ratio, block, rank), jnp.bfloat16)
    if last == ratio:
        half = jax.ShapeDtypeStruct((n_col // 2, rows, rank), jnp.float32)
        gs = [half, half]
    else:
        gs = [jax.ShapeDtypeStruct((block, rank), jnp.float32)]
    operands = [scalars, coords, cores, *src_parts, *tgt_parts, tiles, *carried]
    return pl.pallas_call(
        functools.partial(slots_kernel, first, last, n_col, ratio),
        out_shape=[gt, *gs],
        in_specs=[smem_spec, smem_spec] + [any_spec] * (len(operands) - 2),
        out_specs=[any_spec] * (1 + len(gs)),
        input_output_aliases={len(operands) - 1: 0} if carried else {},
        scratch_shapes=[
            pltpu.VMEM(cores.shape, cores.dtype),
            pltpu.VMEM((block, rank), jnp.bfloat16),
            pltpu.VMEM((n_x * block, rank), jnp.bfloat16),
            pltpu.VMEM((cap, tile, tile), jnp.bfloat16),
            pltpu.VMEM((cap, tile, tile), jnp.bfloat16),
            pltpu.VMEM((cap, tile, rank), jnp.bfloat16),
            pltpu.VMEM((cap, tile, rank), jnp.bfloat16),
            pltpu.VMEM((block, rank), jnp.float32),
            pltpu.VMEM((n_x * block, rank), jnp.float32),
            pltpu.SMEM((cap + UNROLL,), jnp.int32),
            pltpu.SMEM((cap + UNROLL,), jnp.int32),
            pltpu.SemaphoreType.DMA((n_col * (n_x + 1) + 3,)),
        ],
        compiler_params=pltpu.CompilerParams(vmem_limit_bytes=56 * 2**20),
        cost_estimate=pl.CostEstimate(
            flops=cap * 5 * 2 * tile**3 // ratio, bytes_accessed=12 * 2**20, transcendentals=0
        ),
    )(*operands)


def swap(value, bit, n_col):
    return lax.ppermute(value, "col", [(i, i ^ bit) for i in range(n_col)])


def local(factors, cores, tiles, tile_coords, tile_counts):
    planes = lax.axis_size("zz")
    ratio = lax.axis_size("xx")
    n_col = lax.axis_size("col")
    rows, rank = factors.shape
    tile = tiles.shape[1]
    plane, x_pos, col_pos = lax.axis_index("zz"), lax.axis_index("xx"), lax.axis_index("col")
    scalars = jnp.stack([plane, x_pos, col_pos, tile_counts[0]]).astype(jnp.int32)
    coords = tile_coords.reshape(-1)

    own = []
    for d in range(n_col):
        pairs = [
            ((p * ratio + x) * n_col + q, ((mirror(q, n_col) ^ p ^ d) * ratio + x) * n_col + p)
            for p in range(planes)
            for x in range(ratio)
            for q in range(n_col)
        ]
        own.append(lax.ppermute(factors, AXES, pairs))
    src = {0: factors}
    bit = n_col // 2
    while bit:
        for o, value in list(src.items()):
            src[o | bit] = swap(value, bit, n_col)
        bit //= 2
    src = [src[o] for o in range(n_col)]
    cross = [
        lax.ppermute(own[d], "xx", [(x, (x + s) % ratio) for x in range(ratio)])
        for d in range(n_col)
        for s in range(1, ratio)
    ]

    fixed = (n_col, ratio, scalars, coords, cores, src)
    done = run_slots(0, 1, *fixed, own, tiles, [])
    if ratio > 1:
        done = run_slots(1, ratio, *fixed, cross, tiles, [done[1], done[0]])
    tgt_grad, src_keep, src_send = done

    recv = swap(src_send, 1, n_col)
    arrived = lax.all_to_all(tgt_grad.reshape(-1, rank), ("xx", "col"), 0, 0, tiled=True)
    src_sum = src_keep + recv
    bit = 2
    while bit < n_col:
        pairs = src_sum.reshape(src_sum.shape[0] // 2, 2, rows, rank)
        mine = (col_pos // bit) % 2
        out = lax.dynamic_index_in_dim(pairs, 1 - mine, 1, keepdims=False).astype(jnp.bfloat16)
        kept = lax.dynamic_index_in_dim(pairs, mine, 1, keepdims=False)
        src_sum = kept + swap(out, bit, n_col).astype(jnp.float32)
        bit *= 2
    arrived = arrived.reshape(ratio, n_col * rows, rank)
    summed = sum(arrived[s].astype(jnp.float32) for s in range(ratio)).astype(jnp.bfloat16)
    landed = lax.all_to_all(summed, "zz", 0, 0, tiled=True).reshape(planes, rows, rank)
    tgt_sum = sum(landed[p].astype(jnp.float32) for p in range(planes))
    return weight_decay * factors.astype(jnp.float32) - (src_sum[0] + tgt_sum) / tile


def solution(mesh):
    n_row, n_col = mesh.shape["row"], mesh.shape["col"]
    split = Mesh(mesh.devices.reshape(n_col, n_row // n_col, n_col), AXES)
    in_specs = (P(AXES, None), P(), P(AXES, None, None), P(AXES, None), P(AXES))
    return jax.shard_map(local, mesh=split, in_specs=in_specs, out_specs=P(AXES, None), check_vma=False)
```

time: 141 us -> 117 us (0.83)
  local copies, waits for them, and re-layouts: 15.2 us -> 3.85 us
  waiting for transfers between devices: 38.2 us -> 32 us
  starting transfers between devices: 32.9 us -> 27.8 us
  Pallas kernels: 16.7 us -> 14.2 us
  other arithmetic: 5.74 us -> 4.21 us
  blocking collectives: 32.6 us -> 34.1 us
    unnamed x33 -> x29, local copies, waits for them, and re-layouts: 15 us -> 3.18 us
    all_to_all x1, waiting for transfers between devices: 20.1 us -> 12 us  [local(): lax.all_to_all(summed, 'zz', 0, 0, tiled=True).reshape(planes, rows, rank)]
    all_to_all x1, starting transfers between devices: 14.4 us -> 6.4 us  [local(): lax.all_to_all(summed, 'zz', 0, 0, tiled=True).reshape(planes, rows, rank)]
    ppermute x5, waiting for transfers between devices: 2.8 us -> 9.76 us  [swap(): return lax.ppermute(value, 'col', [(i, i ^ bit) for i in range(n_col)])]
    ppermute x8, waiting for transfers between devices: 15.2 us -> 10.3 us  [the longest x4 5.29 us: local(): lax.ppermute(own[d], 'xx', [(x, (x + s) % ratio) for x in range(ratio)])]
    reduce_sum x2 -> x0, other arithmetic: 3.36 us -> none  [the longest x1 3.21 us: local(): arrived.reshape(ratio, n_col, rows, rank).astype(jnp.float32).sum(0)]
    ppermute x8, starting transfers between devices: 14.2 us -> 16.8 us  [the longest x4 12.3 us: local(): own.append(lax.ppermute(factors, AXES, pairs))]
    pallas_call x1 -> x2, Pallas kernels: 16.7 us -> 14.2 us  [run_slots(): pl.pallas_call(functools.partial(slots_kernel, first, last, n_col, ratio)...]
  transfers between devices with their start and end apart: 14 -> 14, of which waited for: 5 -> 6; matrix products, arithmetic and copies ran while one was open for 2% -> 3% of each run, Pallas kernels for 0% -> 6%
where the time goes in v2:
time: 117 us
  blocking collectives  34.1 us (29%)
  waiting for transfers between devices  32 us (27%)
  starting transfers between devices  27.8 us (24%)
  Pallas kernels  14.2 us (12%)
  other arithmetic  4.21 us (4%)
  local copies, waits for them, and re-layouts  3.85 us (3%)
    all_to_all x1, blocking collectives, local(): lax.all_to_all(tgt_grad.reshape(-1, rank), ('xx', 'col'), 0, 0, tiled=True)  34.1 us
    pallas_call x2, Pallas kernels, run_slots(): pl.pallas_call(functools.partial(slots_kernel, first, last, n_col, ratio)...  14.2 us
    ppermute x4, starting transfers between devices, local(): own.append(lax.ppermute(factors, AXES, pairs))  12.3 us
    all_to_all x1, waiting for transfers between devices, local(): lax.all_to_all(summed, 'zz', 0, 0, tiled=True).reshape(planes, rows, rank)  12 us
    ppermute x5, waiting for transfers between devices, swap(): return lax.ppermute(value, 'col', [(i, i ^ bit) for i in range(n_col)])  9.76 us
    all_to_all x1, starting transfers between devices, local(): lax.all_to_all(summed, 'zz', 0, 0, tiled=True).reshape(planes, rows, rank)  6.4 us
    ppermute x4, waiting for transfers between devices, local(): lax.ppermute(own[d], 'xx', [(x, (x + s) % ratio) for x in range(ratio)])  5.29 us
    ppermute x4, waiting for transfers between devices, local(): own.append(lax.ppermute(factors, AXES, pairs))  4.99 us
  transfers between devices with their start and end apart: 14, of which 6 were waited for; matrix products, arithmetic and copies ran while one was open for 3% of the time, Pallas kernels for 6%

profile of v2, /device:TPU:0, one launch (start us, length us, event | category | flops | bytes accessed | tf_op | source)
XLA Modules:
  0.0 117.0 jit_solution(9391510440775542413)
XLA Ops:
  0.0 3.0 %collective-permute-start.1 = (bf16[512,256]{1,0:T(8,128)(2,1)}, bf16[512,256]{1,0:T(8,128)(2,1)S(1)}, u32[]{:S(2)}, u32[]{:S(2)}) collective-permute-start(bf16[512,256]{1,0:T(8,128)(2,1)} %refs_0_.3), channel_id=1, source_target_pairs={{0,2},{1,3},{2,0},{3,1},{4,6},{5,7},{6,4},{7,5},{8,10},{9,11},{10,... | collective-permute-start | bytes 786440 | tf_op jit(solution)/shard_map/ppermute | solution.py:180
  3.0 5.5 %collective-permute-start.9 = (bf16[512,256]{1,0:T(8,128)(2,1)}, bf16[512,256]{1,0:T(8,128)(2,1)S(1)}, u32[]{:S(2)}, u32[]{:S(2)}) collective-permute-start(bf16[512,256]{1,0:T(8,128)(2,1)} %refs_0_.3), channel_id=1, source_target_pairs={{0,24},{1,8},{2,16},{3,0},{4,28},{5,12},{6,20},{7,4},{8,17},{9,1},... | collective-permute-start | bytes 786440 | tf_op jit(solution)/shard_map/ppermute | solution.py:201
  8.5 1.6 %collective-permute-start.3 = (bf16[512,256]{1,0:T(8,128)(2,1)}, bf16[512,256]{1,0:T(8,128)(2,1)S(1)}, u32[]{:S(2)}, u32[]{:S(2)}) collective-permute-start(bf16[512,256]{1,0:T(8,128)(2,1)} %refs_0_.3), channel_id=1, source_target_pairs={{0,0},{1,16},{2,8},{3,24},{4,4},{5,20},{6,12},{7,28},{8,9},{9,25},... | collective-permute-start | bytes 786440 | tf_op jit(solution)/shard_map/ppermute | solution.py:201
  10.1 1.9 %collective-permute-start.5 = (bf16[512,256]{1,0:T(8,128)(2,1)}, bf16[512,256]{1,0:T(8,128)(2,1)S(1)}, u32[]{:S(2)}, u32[]{:S(2)}) collective-permute-start(bf16[512,256]{1,0:T(8,128)(2,1)} %refs_0_.3), channel_id=1, source_target_pairs={{0,8},{1,24},{2,0},{3,16},{4,12},{5,28},{6,4},{7,20},{8,1},{9,17},... | collective-permute-start | bytes 786440 | tf_op jit(solution)/shard_map/ppermute | solution.py:201
  12.0 3.3 %collective-permute-start.7 = (bf16[512,256]{1,0:T(8,128)(2,1)}, bf16[512,256]{1,0:T(8,128)(2,1)S(1)}, u32[]{:S(2)}, u32[]{:S(2)}) collective-permute-start(bf16[512,256]{1,0:T(8,128)(2,1)} %refs_0_.3), channel_id=1, source_target_pairs={{0,16},{1,0},{2,24},{3,8},{4,20},{5,4},{6,28},{7,12},{8,25},{9,9},... | collective-permute-start | bytes 786440 | tf_op jit(solution)/shard_map/ppermute | solution.py:201
  16.1 1.6 %collective-permute-start.10 = (bf16[512,256]{1,0:T(8,128)(2,1)S(1)}, bf16[512,256]{1,0:T(8,128)(2,1)S(1)}, u32[]{:S(2)}, u32[]{:S(2)}) collective-permute-start(bf16[512,256]{1,0:T(8,128)(2,1)S(1)} %collective-permute-done.9.refs_7_), channel_id=1, source_target_pairs={{0,4},{4,0},{1,5},{5,1},{2,6},{6,2},{3,7},{7,3},{8,12},{12,8},{9,1... | collective-permute-start | bytes 786440 | tf_op jit(solution)/shard_map/ppermute | solution.py:210
  18.2 4.0 %collective-permute-done.5.refs_5_ = bf16[512,256]{1,0:T(8,128)(2,1)S(1)} collective-permute-done((bf16[512,256]{1,0:T(8,128)(2,1)}, bf16[512,256]{1,0:T(8,128)(2,1)S(1)}, u32[]{:S(2)}, u32[]{:S(2)}) %collective-permute-start.5) | collective-permute-done | bytes 262176 | tf_op jit(solution)/shard_map/ppermute | solution.py:201
  22.2 0.9 collective-permute-start.6
  23.1 1.0 collective-permute-done.7.refs_6_
  24.2 1.5 %collective-permute-start.8 = (bf16[512,256]{1,0:T(8,128)(2,1)S(1)}, bf16[512,256]{1,0:T(8,128)(2,1)S(1)}, u32[]{:S(2)}, u32[]{:S(2)}) collective-permute-start(bf16[512,256]{1,0:T(8,128)(2,1)S(1)} %collective-permute-done.7.refs_6_), channel_id=1, source_target_pairs={{0,4},{4,0},{1,5},{5,1},{2,6},{6,2},{3,7},{7,3},{8,12},{12,8},{9,1... | collective-permute-start | bytes 786440 | tf_op jit(solution)/shard_map/ppermute | solution.py:210
  26.2 0.8 copy.8
  28.4 6.8 %shard_map.55 = (bf16[2,2048,256]{2,1,0:T(8,128)(2,1)}, f32[2048,256]{1,0:T(8,128)}) custom-call(s32[4]{0:T(128)} %pad_add_fusion.scalars, s32[96]{0:T(128)} %reshape.47.coords, bf16[8,256,256]{2,1,0:T(8,128)(2,1)} %cores_hbm.3, bf16[512,256]{1,0:T(8,128)(2,1)} %refs_0_.3, bf16[512,256]{1,0:T(8,128)(2,1)} %copy-done.4, bf16[512,256]{1,0:T(8,128)(2,1)} %copy-done.3, ...), custom_call_target="tpu_custom_call" | custom-call | flops 2684354560 | bytes 12582912 | tf_op jit(solution)/shard_map/pallas_call | solution.py:152
  35.3 5.3 %collective-permute-done.8.refs_6_ = bf16[512,256]{1,0:T(8,128)(2,1)S(1)} collective-permute-done((bf16[512,256]{1,0:T(8,128)(2,1)S(1)}, bf16[512,256]{1,0:T(8,128)(2,1)S(1)}, u32[]{:S(2)}, u32[]{:S(2)}) %collective-permute-start.8) | collective-permute-done | bytes 262176 | tf_op jit(solution)/shard_map/ppermute | solution.py:210
  41.2 7.4 %shard_map.56 = (bf16[2,2048,256]{2,1,0:T(8,128)(2,1)}, f32[2,512,256]{2,1,0:T(8,128)}, f32[2,512,256]{2,1,0:T(8,128)}) custom-call(s32[4]{0:T(128)} %pad_add_fusion.scalars, s32[96]{0:T(128)} %reshape.47.coords, bf16[8,256,256]{2,1,0:T(8,128)(2,1)} %cores_hbm.3, bf16[512,256]{1,0:T(8,128)(2,1)} %refs_0_.3, ...), custom_call_target="tpu_custom_call", output_to_operand_aliasing={{0}: (13, {})} | custom-call | flops 2684354560 | bytes 12582912 | tf_op jit(solution)/shard_map/pallas_call | solution.py:152
  48.6 34.1 %all_to_all.15 = bf16[8,512,256]{2,1,0:T(8,128)(2,1)S(1)} all-to-all(bf16[8,512,256]{2,1,0:T(8,128)(2,1)} %bitcast.6), channel_id=1, replica_groups=mesh['zz'=4,'xx'=2,'col'=4] {'xx','col'}, dimensions={0} | all-to-all | bytes 4194304 | tf_op jit(solution)/shard_map/all_to_all | solution.py:222
  82.7 1.3 %add_convert_fusion = bf16[4,512,256]{2,1,0:T(8,128)(2,1)} fusion(bf16[8,512,256]{2,1,0:T(8,128)(2,1)S(1)} %all_to_all.15), kind=kLoop, calls=%fused_computation | loop fusion | flops 2097152 | bytes 3145728 | tf_op jit(solution)/shard_map/convert_element_type | solution.py:233
  84.0 6.4 %all-to-all-start.1 = ((bf16[4,512,256]{2,1,0:T(8,128)(2,1)}), bf16[4,512,256]{2,1,0:T(8,128)(2,1)S(1)}, u32[]{:S(2)}, u32[]{:S(2)}) async-start(bf16[4,512,256]{2,1,0:T(8,128)(2,1)} %add_convert_fusion), calls=%async_computation.1 | async-start | bytes 2097152 | tf_op jit(solution)/shard_map/all_to_all | solution.py:234
  90.4 2.9 %collective-permute-done.11 = f32[2,512,256]{2,1,0:T(8,128)S(1)} collective-permute-done((f32[2,512,256]{2,1,0:T(8,128)}, f32[2,512,256]{2,1,0:T(8,128)S(1)}, u32[]{:S(2)}, u32[]{:S(2)}) %collective-permute-start.11) | collective-permute-done | bytes 1048608 | tf_op jit(solution)/shard_map/ppermute | solution.py:180
  93.2 1.0 copy-done.1
  94.2 1.4 %add.40 = f32[2,512,256]{2,1,0:T(8,128)S(1)} add(f32[2,512,256]{2,1,0:T(8,128)S(1)} %copy-done, f32[2,512,256]{2,1,0:T(8,128)} %copy-done.1) | non-fusion elementwise | flops 262144 | bytes 3145728 | tf_op jit(solution)/shard_map/add | solution.py:223
  95.6 1.5 %collective-permute-start.12 = (bf16[1,512,256]{2,1,0:T(8,128)(2,1)S(1)}, bf16[1,512,256]{2,1,0:T(8,128)(2,1)S(1)}, u32[]{:S(2)}, u32[]{:S(2)}) collective-permute-start(bf16[1,512,256]{2,1,0:T(8,128)(2,1)S(1)} %dynamic-slice_convert_fusion), channel_id=1, source_target_pairs={{0,2},{1,3},{2,0},{3,1},{4,6},{5,7},{6,4},{7,5},{8,10},{9,11},{10,... | collective-permute-start | bytes 786440 | tf_op jit(solution)/shard_map/ppermute | solution.py:180
  97.1 6.9 %collective-permute-done.12 = bf16[1,512,256]{2,1,0:T(8,128)(2,1)S(1)} collective-permute-done((bf16[1,512,256]{2,1,0:T(8,128)(2,1)S(1)}, bf16[1,512,256]{2,1,0:T(8,128)(2,1)S(1)}, u32[]{:S(2)}, u32[]{:S(2)}) %collective-permute-start.12) | collective-permute-done | bytes 262176 | tf_op jit(solution)/shard_map/ppermute | solution.py:180
  104.0 12.0 %all-to-all-done.1 = bf16[4,512,256]{2,1,0:T(8,128)(2,1)S(1)} async-done(((bf16[4,512,256]{2,1,0:T(8,128)(2,1)}), bf16[4,512,256]{2,1,0:T(8,128)(2,1)S(1)}, u32[]{:S(2)}, u32[]{:S(2)}) %all-to-all-start.1) | async-done | bytes 1048608 | tf_op jit(solution)/shard_map/all_to_all | solution.py:234
  116.0 1.0 bitcast_subtract_fusion
  (42 shorter events, 3.3 us)
Async XLA Ops:
  0.0 12.0 %collective-permute-start.1 = (bf16[512,256]{1,0:T(8,128)(2,1)}, bf16[512,256]{1,0:T(8,128)(2,1)S(1)}, u32[]{:S(2)}, u32[]{:S(2)}) collective-permute-start(bf16[512,256]{1,0:T(8,128)(2,1)} %refs_0_.3), channel_id=1, source_target_pairs={{0,2},{1,3},{2,0},{3,1},{4,6},{5,7},{6,4},{7,5},{8,10},{9,11},{10,... | collective-permute-start | bytes 786440 | tf_op jit(solution)/shard_map/ppermute | solution.py:180
  3.0 12.4 %collective-permute-start = (bf16[512,256]{1,0:T(8,128)(2,1)}, bf16[512,256]{1,0:T(8,128)(2,1)S(1)}, u32[]{:S(2)}, u32[]{:S(2)}) collective-permute-start(bf16[512,256]{1,0:T(8,128)(2,1)} %refs_0_.3), channel_id=1, source_target_pairs={{0,1},{1,0},{2,3},{3,2},{4,5},{5,4},{6,7},{7,6},{8,9},{9,8},{10,11... | collective-permute-start | bytes 786440 | tf_op jit(solution)/shard_map/ppermute | solution.py:180
  3.0 13.1 %collective-permute-start.9 = (bf16[512,256]{1,0:T(8,128)(2,1)}, bf16[512,256]{1,0:T(8,128)(2,1)S(1)}, u32[]{:S(2)}, u32[]{:S(2)}) collective-permute-start(bf16[512,256]{1,0:T(8,128)(2,1)} %refs_0_.3), channel_id=1, source_target_pairs={{0,24},{1,8},{2,16},{3,0},{4,28},{5,12},{6,20},{7,4},{8,17},{9,1},... | collective-permute-start | bytes 786440 | tf_op jit(solution)/shard_map/ppermute | solution.py:201
  8.5 9.2 %collective-permute-start.3 = (bf16[512,256]{1,0:T(8,128)(2,1)}, bf16[512,256]{1,0:T(8,128)(2,1)S(1)}, u32[]{:S(2)}, u32[]{:S(2)}) collective-permute-start(bf16[512,256]{1,0:T(8,128)(2,1)} %refs_0_.3), channel_id=1, source_target_pairs={{0,0},{1,16},{2,8},{3,24},{4,4},{5,20},{6,12},{7,28},{8,9},{9,25},... | collective-permute-start | bytes 786440 | tf_op jit(solution)/shard_map/ppermute | solution.py:201
  10.1 12.1 %collective-permute-start.5 = (bf16[512,256]{1,0:T(8,128)(2,1)}, bf16[512,256]{1,0:T(8,128)(2,1)S(1)}, u32[]{:S(2)}, u32[]{:S(2)}) collective-permute-start(bf16[512,256]{1,0:T(8,128)(2,1)} %refs_0_.3), channel_id=1, source_target_pairs={{0,8},{1,24},{2,0},{3,16},{4,12},{5,28},{6,4},{7,20},{8,1},{9,17},... | collective-permute-start | bytes 786440 | tf_op jit(solution)/shard_map/ppermute | solution.py:201
  12.0 15.6 %copy-start.3 = (bf16[512,256]{1,0:T(8,128)(2,1)}, bf16[512,256]{1,0:T(8,128)(2,1)S(1)}, u32[]{:S(2)}) copy-start(bf16[512,256]{1,0:T(8,128)(2,1)S(1)} %collective-permute-done.1.refs_2_) | copy-start | bytes 786436
  12.0 12.1 %collective-permute-start.7 = (bf16[512,256]{1,0:T(8,128)(2,1)}, bf16[512,256]{1,0:T(8,128)(2,1)S(1)}, u32[]{:S(2)}, u32[]{:S(2)}) collective-permute-start(bf16[512,256]{1,0:T(8,128)(2,1)} %refs_0_.3), channel_id=1, source_target_pairs={{0,16},{1,0},{2,24},{3,8},{4,20},{5,4},{6,28},{7,12},{8,25},{9,9},... | collective-permute-start | bytes 786440 | tf_op jit(solution)/shard_map/ppermute | solution.py:201
  15.3 12.3 %copy-start.4 = (bf16[512,256]{1,0:T(8,128)(2,1)}, bf16[512,256]{1,0:T(8,128)(2,1)S(1)}, u32[]{:S(2)}) copy-start(bf16[512,256]{1,0:T(8,128)(2,1)S(1)} %collective-permute-done.refs_1_) | copy-start | bytes 786436
  15.4 12.2 %collective-permute-start.2 = (bf16[512,256]{1,0:T(8,128)(2,1)S(1)}, bf16[512,256]{1,0:T(8,128)(2,1)S(1)}, u32[]{:S(2)}, u32[]{:S(2)}) collective-permute-start(bf16[512,256]{1,0:T(8,128)(2,1)S(1)} %collective-permute-done.1.refs_2_), channel_id=1, source_target_pairs={{0,1},{1,0},{2,3},{3,2},{4,5},{5,4},{6,7},{7,6},{8,9},{9,8},{10,11... | collective-permute-start | bytes 786440 | tf_op jit(solution)/shard_map/ppermute | solution.py:180
  16.1 11.5 %copy-start.10 = (bf16[512,256]{1,0:T(8,128)(2,1)}, bf16[512,256]{1,0:T(8,128)(2,1)S(1)}, u32[]{:S(2)}) copy-start(bf16[512,256]{1,0:T(8,128)(2,1)S(1)} %collective-permute-done.9.refs_7_) | copy-start | bytes 786436
  16.1 19.1 %collective-permute-start.10 = (bf16[512,256]{1,0:T(8,128)(2,1)S(1)}, bf16[512,256]{1,0:T(8,128)(2,1)S(1)}, u32[]{:S(2)}, u32[]{:S(2)}) collective-permute-start(bf16[512,256]{1,0:T(8,128)(2,1)S(1)} %collective-permute-done.9.refs_7_), channel_id=1, source_target_pairs={{0,4},{4,0},{1,5},{5,1},{2,6},{6,2},{3,7},{7,3},{8,12},{12,8},{9,1... | collective-permute-start | bytes 786440 | tf_op jit(solution)/shard_map/ppermute | solution.py:210
  17.7 9.9 %copy-start.11 = (bf16[512,256]{1,0:T(8,128)(2,1)}, bf16[512,256]{1,0:T(8,128)(2,1)S(1)}, u32[]{:S(2)}) copy-start(bf16[512,256]{1,0:T(8,128)(2,1)S(1)} %collective-permute-done.3.refs_4_) | copy-start | bytes 786436
  17.7 17.5 %collective-permute-start.4 = (bf16[512,256]{1,0:T(8,128)(2,1)S(1)}, bf16[512,256]{1,0:T(8,128)(2,1)S(1)}, u32[]{:S(2)}, u32[]{:S(2)}) collective-permute-start(bf16[512,256]{1,0:T(8,128)(2,1)S(1)} %collective-permute-done.3.refs_4_), channel_id=1, source_target_pairs={{0,4},{4,0},{1,5},{5,1},{2,6},{6,2},{3,7},{7,3},{8,12},{12,8},{9,1... | collective-permute-start | bytes 786440 | tf_op jit(solution)/shard_map/ppermute | solution.py:210
  22.2 5.5 %copy-start.12 = (bf16[512,256]{1,0:T(8,128)(2,1)}, bf16[512,256]{1,0:T(8,128)(2,1)S(1)}, u32[]{:S(2)}) copy-start(bf16[512,256]{1,0:T(8,128)(2,1)S(1)} %collective-permute-done.5.refs_5_) | copy-start | bytes 786436
  22.2 13.1 %collective-permute-start.6 = (bf16[512,256]{1,0:T(8,128)(2,1)S(1)}, bf16[512,256]{1,0:T(8,128)(2,1)S(1)}, u32[]{:S(2)}, u32[]{:S(2)}) collective-permute-start(bf16[512,256]{1,0:T(8,128)(2,1)S(1)} %collective-permute-done.5.refs_5_), channel_id=1, source_target_pairs={{0,4},{4,0},{1,5},{5,1},{2,6},{6,2},{3,7},{7,3},{8,12},{12,8},{9,1... | collective-permute-start | bytes 786440 | tf_op jit(solution)/shard_map/ppermute | solution.py:210
  24.2 16.4 %collective-permute-start.8 = (bf16[512,256]{1,0:T(8,128)(2,1)S(1)}, bf16[512,256]{1,0:T(8,128)(2,1)S(1)}, u32[]{:S(2)}, u32[]{:S(2)}) collective-permute-start(bf16[512,256]{1,0:T(8,128)(2,1)S(1)} %collective-permute-done.7.refs_6_), channel_id=1, source_target_pairs={{0,4},{4,0},{1,5},{5,1},{2,6},{6,2},{3,7},{7,3},{8,12},{12,8},{9,1... | collective-permute-start | bytes 786440 | tf_op jit(solution)/shard_map/ppermute | solution.py:210
  35.2 5.3 %copy-start.6 = (bf16[512,256]{1,0:T(8,128)(2,1)}, bf16[512,256]{1,0:T(8,128)(2,1)S(1)}, u32[]{:S(2)}) copy-start(bf16[512,256]{1,0:T(8,128)(2,1)S(1)} %collective-permute-done.10.refs_7_) | copy-start | bytes 786436
  35.2 5.3 %copy-start.7 = (bf16[512,256]{1,0:T(8,128)(2,1)}, bf16[512,256]{1,0:T(8,128)(2,1)S(1)}, u32[]{:S(2)}) copy-start(bf16[512,256]{1,0:T(8,128)(2,1)S(1)} %collective-permute-done.4.refs_4_) | copy-start | bytes 786436
  35.3 5.3 %copy-start.8 = (bf16[512,256]{1,0:T(8,128)(2,1)}, bf16[512,256]{1,0:T(8,128)(2,1)S(1)}, u32[]{:S(2)}) copy-start(bf16[512,256]{1,0:T(8,128)(2,1)S(1)} %collective-permute-done.6.refs_5_) | copy-start | bytes 786436
  82.7 11.5 %copy-start = (f32[2,512,256]{2,1,0:T(8,128)S(1)}, f32[2,512,256]{2,1,0:T(8,128)}, u32[]{:S(2)}) copy-start(f32[2,512,256]{2,1,0:T(8,128)} %get-tuple-element.12) | copy-start | bytes 3145732
  84.0 32.1 %all-to-all-start.1 = ((bf16[4,512,256]{2,1,0:T(8,128)(2,1)}), bf16[4,512,256]{2,1,0:T(8,128)(2,1)S(1)}, u32[]{:S(2)}, u32[]{:S(2)}) async-start(bf16[4,512,256]{2,1,0:T(8,128)(2,1)} %add_convert_fusion), calls=%async_computation.1 | async-start | bytes 2097152 | tf_op jit(solution)/shard_map/all_to_all | solution.py:234
  90.4 25.7 %copy-start.2 = (bf16[512,256]{1,0:T(8,128)(2,1)S(1)}, bf16[512,256]{1,0:T(8,128)(2,1)}, u32[]{:S(2)}) copy-start(bf16[512,256]{1,0:T(8,128)(2,1)} %refs_0_.3) | copy-start | bytes 786436
  90.4 2.9 %collective-permute-start.11 = (f32[2,512,256]{2,1,0:T(8,128)}, f32[2,512,256]{2,1,0:T(8,128)S(1)}, u32[]{:S(2)}, u32[]{:S(2)}) collective-permute-start(f32[2,512,256]{2,1,0:T(8,128)} %get-tuple-element.13), channel_id=1, source_target_pairs={{0,1},{1,0},{2,3},{3,2},{4,5},{5,4},{6,7},{7,6},{8,9},{9,8},{10,11... | collective-permute-start | bytes 3145736 | tf_op jit(solution)/shard_map/ppermute | solution.py:180
  95.6 8.4 %collective-permute-start.12 = (bf16[1,512,256]{2,1,0:T(8,128)(2,1)S(1)}, bf16[1,512,256]{2,1,0:T(8,128)(2,1)S(1)}, u32[]{:S(2)}, u32[]{:S(2)}) collective-permute-start(bf16[1,512,256]{2,1,0:T(8,128)(2,1)S(1)} %dynamic-slice_convert_fusion), channel_id=1, source_target_pairs={{0,2},{1,3},{2,0},{3,1},{4,6},{5,7},{6,4},{7,5},{8,10},{9,11},{10,... | collective-permute-start | bytes 786440 | tf_op jit(solution)/shard_map/ppermute | solution.py:180
  (4 other events, 5.9 us)

commit v3 on v2

v3 whole, which is shorter than its diff:
```python
import functools

import jax
import jax.numpy as jnp
from jax import lax
from jax.experimental import pallas as pl
from jax.experimental.pallas import tpu as pltpu
from jax.sharding import Mesh
from jax.sharding import PartitionSpec as P

weight_decay = 1.0
AXES = ("zz", "xx", "col")
UNROLL = 8
VMEM_LIMIT = 56 * 2**20
COST = 0
CONTRACT_LAST = (((1,), (1,)), ((), ()))
CONTRACT_FIRST = (((0,), (0,)), ((), ()))


def dot(a, b, dims=(((1,), (0,)), ((), ()))):
    return lax.dot_general(a, b, dims, preferred_element_type=jnp.float32)


def mirror(value, size):
    out, bit = 0, 1
    while bit < size:
        out = out * 2 + (value // bit) % 2
        bit *= 2
    return out


def slots_kernel(first, last, late, n_wait, n_col, ratio, scalars, coords, cores_hbm, *refs):
    n_x = last - first
    opens, closes = first == 0, last == ratio and late != 1
    parts = [d for d in range(n_col) if late is None or d // 2 % 2 == late]
    src_refs, refs = refs[:n_col], refs[n_col:]
    tgt_refs, refs = refs[: len(parts) * n_x], refs[len(parts) * n_x :]
    tiles_hbm, refs = refs[0], refs[1:]
    if not opens:
        gs_in, refs = refs[0], refs[1:]
    refs = refs[n_wait:]
    gt_outs, refs = refs[: len(parts) * n_x], refs[len(parts) * n_x :]
    gs_outs, refs = (refs[:2], refs[2:]) if closes else (refs[:1], refs[1:])
    cores, src, tgt, tiles, resids, left, right, gs_acc, gt_acc, slot_of, tgt_of, tile_sems, sems = refs
    cap, tile = tiles.shape[0], tiles.shape[1]
    rows = src_refs[0].shape[0]
    src_tiles = n_col * rows // tile
    plane, x_pos, col_pos, live = scalars[0], scalars[1], scalars[2], scalars[3]

    def part_at(d, n):
        place = n * n_col + mirror(plane ^ col_pos ^ d, n_col)
        return pl.ds(pl.multiple_of(place * rows, rows), rows)

    copies = [pltpu.make_async_copy(cores_hbm, cores, sems.at[0])]
    for o in range(n_col):
        at = pl.multiple_of((col_pos ^ o) * rows, rows)
        copies.append(pltpu.make_async_copy(src_refs[o], src.at[pl.ds(at, rows)], sems.at[1 + o]))
    for i, d in enumerate(parts):
        for n in range(n_x):
            index = i * n_x + n
            copies.append(
                pltpu.make_async_copy(tgt_refs[index], tgt.at[part_at(d, n)], sems.at[1 + n_col + index])
            )
    for copy in copies:
        copy.start()
    if not opens:
        gs_copy = pltpu.make_async_copy(gs_in, gs_acc, sems.at[1 + n_col + len(parts) * n_x])
        gs_copy.start()

    def choose(s, count):
        b = coords[2, s]
        step = lax.rem(x_pos - b // src_tiles + ratio, ratio)
        place = lax.rem(b, src_tiles)
        taken = (step >= first) & (step < last)
        if late is not None:
            part = mirror(place * tile // rows, n_col) ^ plane ^ col_pos
            taken = taken & ((part // 2) % 2 == late)
        slot_of[count] = s
        tgt_of[count] = (step - first) * src_tiles + place

        @pl.when(taken)
        def _():
            pltpu.make_async_copy(tiles_hbm.at[s], tiles.at[count], tile_sems.at[count]).start()

        return count + taken.astype(jnp.int32)

    count = lax.fori_loop(0, live, choose, 0)
    for u in range(UNROLL):
        slot_of[count + u] = 0
        tgt_of[count + u] = 0
    groups = (count + UNROLL - 1) // UNROLL
    if opens:
        gs_acc[...] = jnp.zeros_like(gs_acc)
    gt_acc[...] = jnp.zeros_like(gt_acc)
    for copy in copies:
        copy.wait()

    def place(index):
        return pl.ds(pl.multiple_of(index * tile, tile), tile)

    def products(g, carry):
        for u in range(UNROLL):
            i = g * UNROLL + u
            s = slot_of[i]
            core = cores[coords[0, s]]
            left[i] = dot(src[place(coords[1, s])], core).astype(jnp.bfloat16)
            right[i] = dot(tgt[place(tgt_of[i])], core, CONTRACT_LAST).astype(jnp.bfloat16)
        return carry

    def residuals(g, carry):
        for u in range(UNROLL):
            i = g * UNROLL + u
            predicted = dot(left[i], tgt[place(tgt_of[i])], CONTRACT_LAST)
            resid = jnp.where(i < count, tiles[i].astype(jnp.float32) - predicted, 0.0)
            resids[i] = resid.astype(jnp.bfloat16)
        return carry

    def gradients(g, carry):
        for u in range(UNROLL):
            i = g * UNROLL + u
            resid = resids[i]
            gs_acc[place(coords[1, slot_of[i]])] += dot(resid, right[i])
            gt_acc[place(tgt_of[i])] += dot(resid, left[i], CONTRACT_FIRST)
        return carry

    def arrive(i, carry):
        pltpu.make_async_copy(tiles_hbm.at[slot_of[i]], tiles.at[i], tile_sems.at[i]).wait()
        return carry

    lax.fori_loop(0, groups, products, 0)
    lax.fori_loop(0, count, arrive, 0)
    lax.fori_loop(0, groups, residuals, 0)
    if not opens:
        gs_copy.wait()
    lax.fori_loop(0, groups, gradients, 0)

    outs = []
    if closes:
        for h in range(n_col // 2):
            for n in range(2):
                at = pl.multiple_of((2 * h + ((col_pos + n) & 1)) * rows, rows)
                outs.append((gs_acc.at[pl.ds(at, rows)], gs_outs[n].at[h]))
    else:
        outs.append((gs_acc, gs_outs[0]))
    outs = [pltpu.make_async_copy(a, b, sems.at[i]) for i, (a, b) in enumerate(outs)]
    for copy in outs:
        copy.start()
    for i, d in enumerate(parts):
        for n in range(n_x):
            tgt[part_at(d, n)] = gt_acc[part_at(d, n)].astype(tgt.dtype)
            copy = pltpu.make_async_copy(tgt.at[part_at(d, n)], gt_outs[i * n_x + n], sems.at[len(outs)])
            copy.start()
            outs.append(copy)
    for copy in outs:
        copy.wait()


def run_slots(
    first, last, late, n_col, ratio, scalars, coords, cores, src_parts, tgt_parts, tiles, carried, wait=()
):
    rows, rank = src_parts[0].shape
    cap, tile = tiles.shape[0], tiles.shape[1]
    n_x, block = last - first, n_col * rows
    any_spec = pl.BlockSpec(memory_space=pl.ANY)
    smem_spec = pl.BlockSpec(memory_space=pltpu.SMEM)
    n_out = len(tgt_parts)
    outs = [jax.ShapeDtypeStruct((rows, rank), jnp.bfloat16)] * n_out
    if last == ratio and late != 1:
        outs += [jax.ShapeDtypeStruct((n_col // 2, rows, rank), jnp.float32)] * 2
    else:
        outs += [jax.ShapeDtypeStruct((block, rank), jnp.float32)]
    operands = [scalars, coords, cores, *src_parts, *tgt_parts, tiles, *carried, *wait]
    outs = pl.pallas_call(
        functools.partial(slots_kernel, first, last, late, len(wait), n_col, ratio),
        out_shape=outs,
        in_specs=[smem_spec, smem_spec] + [any_spec] * (len(operands) - 2),
        out_specs=[any_spec] * len(outs),
        scratch_shapes=[
            pltpu.VMEM(cores.shape, cores.dtype),
            pltpu.VMEM((block, rank), jnp.bfloat16),
            pltpu.VMEM((n_x * block, rank), jnp.bfloat16),
            pltpu.VMEM((cap, tile, tile), jnp.bfloat16),
            pltpu.VMEM((cap, tile, tile), jnp.bfloat16),
            pltpu.VMEM((cap, tile, rank), jnp.bfloat16),
            pltpu.VMEM((cap, tile, rank), jnp.bfloat16),
            pltpu.VMEM((block, rank), jnp.float32),
            pltpu.VMEM((n_x * block, rank), jnp.float32),
            pltpu.SMEM((cap + UNROLL,), jnp.int32),
            pltpu.SMEM((cap + UNROLL,), jnp.int32),
            pltpu.SemaphoreType.DMA((cap,)),
            pltpu.SemaphoreType.DMA((2 * n_col * (n_x + 1) + 2,)),
        ],
        compiler_params=pltpu.CompilerParams(vmem_limit_bytes=VMEM_LIMIT),
        cost_estimate=pl.CostEstimate(flops=COST, bytes_accessed=COST, transcendentals=0),
    )(*operands)
    return outs[:n_out], outs[n_out:]


def swap(value, bit, n_col):
    return lax.ppermute(value, "col", [(i, i ^ bit) for i in range(n_col)])


def local(factors, cores, tiles, tile_coords, tile_counts):
    planes = lax.axis_size("zz")
    ratio = lax.axis_size("xx")
    n_col = lax.axis_size("col")
    rows, rank = factors.shape
    tile = tiles.shape[1]
    plane, x_pos, col_pos = lax.axis_index("zz"), lax.axis_index("xx"), lax.axis_index("col")
    scalars = jnp.stack([plane, x_pos, col_pos, tile_counts[0]]).astype(jnp.int32)
    coords = tile_coords.T

    def part_pairs(d, target):
        spots = [(p, x, j) for p in range(planes) for x in range(ratio) for j in range(n_col)]
        at = lambda p, x, j: (p * ratio + x) * n_col + j
        return [(at(p, x, j), at(*target(p, x, j, mirror(p ^ j ^ d, n_col)))) for p, x, j in spots]

    own = {}
    for d in [*range(1, n_col, 2), *range(0, n_col, 2)]:
        pairs = part_pairs(d, lambda p, x, j, q: (j, x, q))
        own[d] = lax.ppermute(factors, AXES, [(b, a) for a, b in pairs])
    src = {0: factors}
    bit = n_col // 2
    while bit:
        for o, value in list(src.items()):
            src[o | bit] = swap(value, bit, n_col)
        bit //= 2
    src = [src[o] for o in range(n_col)]
    cross = {
        d: [lax.ppermute(own[d], "xx", [(x, (x + s) % ratio) for x in range(ratio)]) for s in range(1, ratio)]
        for d in own
    }

    fixed = (n_col, ratio, scalars, coords, cores, src)
    own_grad, src_grad = run_slots(0, 1, None, *fixed, [own[d] for d in range(n_col)], tiles, [])
    grads = {d: [own_grad[d]] for d in range(n_col)}
    if ratio > 1:
        held = [v for d in range(n_col) for v in cross[d]]
        target, src_grad = run_slots(1, ratio, None, *fixed, held, tiles, src_grad)
        for d in range(n_col):
            grads[d].extend(target[d * (ratio - 1) : (d + 1) * (ratio - 1)])
    src_keep, src_send = src_grad

    for d in range(0, n_col, 4):
        gone = [lax.ppermute(v, "zz", [(p, p ^ 1) for p in range(planes)]) for v in grads.pop(d + 1)]
        grads[d] = [
            (a.astype(jnp.float32) + b.astype(jnp.float32)).astype(jnp.bfloat16) for a, b in zip(grads[d], gone)
        ]
    src_sum = src_keep + swap(src_send, 1, n_col)
    bit = 2
    while bit < n_col:
        pairs = src_sum.reshape(src_sum.shape[0] // 2, 2, rows, rank)
        mine = (col_pos // bit) % 2
        out = lax.dynamic_index_in_dim(pairs, 1 - mine, 1, keepdims=False).astype(jnp.bfloat16)
        kept = lax.dynamic_index_in_dim(pairs, mine, 1, keepdims=False)
        src_sum = kept + swap(out, bit, n_col).astype(jnp.float32)
        bit *= 2
    total = src_sum[0]
    for d in sorted(grads, key=lambda d: -(d // 2 % 2)):
        arrived = [
            lax.ppermute(grads[d][t], AXES, part_pairs(d, lambda p, x, j, q, t=t: (p, (x - t) % ratio, q)))
            for t in range(ratio)
        ]
        term = sum(v.astype(jnp.float32) for v in arrived).astype(jnp.bfloat16)
        pairs = [
            ((p * ratio + x) * n_col + q, ((p ^ mirror(q, n_col) ^ d) * ratio + x) * n_col + q)
            for p in range(planes)
            for x in range(ratio)
            for q in range(n_col)
        ]
        total = total + lax.ppermute(term, AXES, pairs).astype(jnp.float32)
    return weight_decay * factors.astype(jnp.float32) - total / tile


def solution(mesh):
    n_row, n_col = mesh.shape["row"], mesh.shape["col"]
    split = Mesh(mesh.devices.reshape(n_col, n_row // n_col, n_col), AXES)
    in_specs = (P(AXES, None), P(), P(AXES, None, None), P(AXES, None), P(AXES))
    return jax.shard_map(local, mesh=split, in_specs=in_specs, out_specs=P(AXES, None), check_vma=False)
```

time: 117 us -> 98.9 us (0.85)
  blocking collectives: 34.1 us -> 0 us
  starting transfers between devices: 27.8 us -> 51.9 us
  waiting for transfers between devices: 32 us -> 26.6 us
  local copies, waits for them, and re-layouts: 3.85 us -> 1.48 us
    all_to_all x1 -> x0, blocking collectives: 34.1 us -> none  [local(): lax.all_to_all(tgt_grad.reshape(-1, rank), ('xx', 'col'), 0, 0, tiled=True)]
    ppermute x4 -> x15, starting transfers between devices: 12.3 us -> 42.2 us  [the longest x4 14.6 us: local(): own[d] = lax.ppermute(factors, AXES, [(b, a) for a, b in pairs])]
    ppermute x4 -> x15, waiting for transfers between devices: 4.99 us -> 17.1 us  [the longest x3 10.1 us: local(): total = total + lax.ppermute(term, AXES, pairs).astype(jnp.float32)]
    all_to_all x1 -> x0, waiting for transfers between devices: 12 us -> none  [local(): lax.all_to_all(summed, 'zz', 0, 0, tiled=True).reshape(planes, rows, rank)]
    ppermute x5, waiting for transfers between devices: 9.76 us -> 0.01 us  [swap(): return lax.ppermute(value, 'col', [(i, i ^ bit) for i in range(n_col)])]
    all_to_all x1 -> x0, starting transfers between devices: 6.4 us -> none  [local(): lax.all_to_all(summed, 'zz', 0, 0, tiled=True).reshape(planes, rows, rank)]
    ppermute x4, waiting for transfers between devices: 5.29 us -> 9.44 us  [local(): lax.ppermute(own[d], 'xx', [(x, (x + s) % ratio) for x in range(ratio)])]
    unnamed x29 -> x34, local copies, waits for them, and re-layouts: 3.18 us -> 1.44 us
  transfers between devices with their start and end apart: 14 -> 24, of which waited for: 6 -> 6; matrix products, arithmetic and copies ran while one was open for 3% -> 3% of each run, Pallas kernels for 6% -> 7%
where the time goes in v3:
time: 98.9 us
  starting transfers between devices  51.9 us (52%)
  waiting for transfers between devices  26.6 us (27%)
  Pallas kernels  13.3 us (13%)
  other arithmetic  4.64 us (5%)
  local copies, waits for them, and re-layouts  1.48 us (1%)
  between operations  0.99 us (1%)
    ppermute x4, starting transfers between devices, local(): own[d] = lax.ppermute(factors, AXES, [(b, a) for a, b in pairs])  14.6 us
    ppermute x3, starting transfers between devices, local(): total = total + lax.ppermute(term, AXES, pairs).astype(jnp.float32)  13.6 us
    pallas_call x2, Pallas kernels, run_slots(): pl.pallas_call(functools.partial(slots_kernel, first, last, late, len(wai...  13.3 us
    ppermute x6, starting transfers between devices, local(): lax.ppermute(grads[d][t], AXES, part_pairs(d, lambda p, x, j, q, t=t: (p,...  11.9 us
    ppermute x3, waiting for transfers between devices, local(): total = total + lax.ppermute(term, AXES, pairs).astype(jnp.float32)  10.1 us
    ppermute x4, waiting for transfers between devices, local(): lax.ppermute(own[d], 'xx', [(x, (x + s) % ratio) for x in range(ratio)])  9.44 us
    ppermute x4, starting transfers between devices, local(): lax.ppermute(own[d], 'xx', [(x, (x + s) % ratio) for x in range(ratio)])  5.01 us
    ppermute x2, waiting for transfers between devices, local(): lax.ppermute(v, 'zz', [(p, p ^ 1) for p in range(planes)])  4.86 us
  transfers between devices with their start and end apart: 24, of which 6 were waited for; matrix products, arithmetic and copies ran while one was open for 3% of the time, Pallas kernels for 7%

profile of v3, /device:TPU:0, one launch (start us, length us, event | category | flops | bytes accessed | tf_op | source)
XLA Modules:
  0.0 98.9 jit_solution(18032806126586489122)
XLA Ops:
  0.5 2.5 %collective-permute-start.1 = (bf16[512,256]{1,0:T(8,128)(2,1)}, bf16[512,256]{1,0:T(8,128)(2,1)S(1)}, u32[]{:S(2)}, u32[]{:S(2)}) collective-permute-start(bf16[512,256]{1,0:T(8,128)(2,1)} %refs_0_.3), channel_id=1, source_target_pairs={{0,2},{1,3},{2,0},{3,1},{4,6},{5,7},{6,4},{7,5},{8,10},{9,11},{10,... | collective-permute-start | bytes 786440 | tf_op jit(solution)/shard_map/ppermute | solution.py:200
  3.0 1.6 %collective-permute-start.3 = (bf16[512,256]{1,0:T(8,128)(2,1)}, bf16[512,256]{1,0:T(8,128)(2,1)S(1)}, u32[]{:S(2)}, u32[]{:S(2)}) collective-permute-start(bf16[512,256]{1,0:T(8,128)(2,1)} %refs_0_.3), channel_id=1, source_target_pairs={{0,0},{10,1},{17,2},{27,3},{4,4},{14,5},{21,6},{31,7},{2,8},{8,9},... | collective-permute-start | bytes 786440 | tf_op jit(solution)/shard_map/ppermute | solution.py:221
  4.6 4.0 %collective-permute-start.5 = (bf16[512,256]{1,0:T(8,128)(2,1)}, bf16[512,256]{1,0:T(8,128)(2,1)S(1)}, u32[]{:S(2)}, u32[]{:S(2)}) collective-permute-start(bf16[512,256]{1,0:T(8,128)(2,1)} %refs_0_.3), channel_id=1, source_target_pairs={{2,0},{8,1},{19,2},{25,3},{6,4},{12,5},{23,6},{29,7},{0,8},{10,9},... | collective-permute-start | bytes 786440 | tf_op jit(solution)/shard_map/ppermute | solution.py:221
  8.6 4.5 %collective-permute-start.7 = (bf16[512,256]{1,0:T(8,128)(2,1)}, bf16[512,256]{1,0:T(8,128)(2,1)S(1)}, u32[]{:S(2)}, u32[]{:S(2)}) collective-permute-start(bf16[512,256]{1,0:T(8,128)(2,1)} %refs_0_.3), channel_id=1, source_target_pairs={{1,0},{11,1},{16,2},{26,3},{5,4},{15,5},{20,6},{30,7},{3,8},{9,9},... | collective-permute-start | bytes 786440 | tf_op jit(solution)/shard_map/ppermute | solution.py:221
  13.1 4.5 %collective-permute-start.9 = (bf16[512,256]{1,0:T(8,128)(2,1)}, bf16[512,256]{1,0:T(8,128)(2,1)S(1)}, u32[]{:S(2)}, u32[]{:S(2)}) collective-permute-start(bf16[512,256]{1,0:T(8,128)(2,1)} %refs_0_.3), channel_id=1, source_target_pairs={{3,0},{9,1},{18,2},{24,3},{7,4},{13,5},{22,6},{28,7},{1,8},{11,9},... | collective-permute-start | bytes 786440 | tf_op jit(solution)/shard_map/ppermute | solution.py:221
  17.7 1.5 %collective-permute-start.2 = (bf16[512,256]{1,0:T(8,128)(2,1)S(1)}, bf16[512,256]{1,0:T(8,128)(2,1)S(1)}, u32[]{:S(2)}, u32[]{:S(2)}) collective-permute-start(bf16[512,256]{1,0:T(8,128)(2,1)S(1)} %collective-permute-done.1.refs_2_), channel_id=1, source_target_pairs={{0,1},{1,0},{2,3},{3,2},{4,5},{5,4},{6,7},{7,6},{8,9},{9,8},{10,11... | collective-permute-start | bytes 786440 | tf_op jit(solution)/shard_map/ppermute | solution.py:200
  19.2 1.5 %collective-permute-start.4 = (bf16[512,256]{1,0:T(8,128)(2,1)S(1)}, bf16[512,256]{1,0:T(8,128)(2,1)S(1)}, u32[]{:S(2)}, u32[]{:S(2)}) collective-permute-start(bf16[512,256]{1,0:T(8,128)(2,1)S(1)} %collective-permute-done.3.refs_4_), channel_id=1, source_target_pairs={{0,4},{4,0},{1,5},{5,1},{2,6},{6,2},{3,7},{7,3},{8,12},{12,8},{9,1... | collective-permute-start | bytes 786440 | tf_op jit(solution)/shard_map/ppermute | solution.py:230
  22.7 2.1 %collective-permute-done.9.refs_7_ = bf16[512,256]{1,0:T(8,128)(2,1)S(1)} collective-permute-done((bf16[512,256]{1,0:T(8,128)(2,1)}, bf16[512,256]{1,0:T(8,128)(2,1)S(1)}, u32[]{:S(2)}, u32[]{:S(2)}) %collective-permute-start.9) | collective-permute-done | bytes 262176 | tf_op jit(solution)/shard_map/ppermute | solution.py:221
  28.3 6.6 %shard_map.55 = (bf16[512,256]{1,0:T(8,128)(2,1)}, bf16[512,256]{1,0:T(8,128)(2,1)}, bf16[512,256]{1,0:T(8,128)(2,1)}, bf16[512,256]{1,0:T(8,128)(2,1)}, f32[2048,256]{1,0:T(8,128)}) custom-call(s32[4]{0:T(128)} %pad_add_fusion.scalars, s32[3,32]{1,0:T(4,128)} %bitcast.14, bf16[8,256,256]{2,1,0:T(8,128)(2,1)} %cores_hbm.3, bf16[512,256]{1,0:T(8,128)(2,1)} %refs_0_.3, ...), custom_call_target="tpu_custom_call" | custom-call | tf_op jit(solution)/shard_map/pallas_call | solution.py:173
  34.9 4.7 %collective-permute-done.8.refs_6_ = bf16[512,256]{1,0:T(8,128)(2,1)S(1)} collective-permute-done((bf16[512,256]{1,0:T(8,128)(2,1)S(1)}, bf16[512,256]{1,0:T(8,128)(2,1)S(1)}, u32[]{:S(2)}, u32[]{:S(2)}) %collective-permute-start.8) | collective-permute-done | bytes 262176 | tf_op jit(solution)/shard_map/ppermute | solution.py:230
  39.6 4.8 %collective-permute-done.10.refs_7_ = bf16[512,256]{1,0:T(8,128)(2,1)S(1)} collective-permute-done((bf16[512,256]{1,0:T(8,128)(2,1)S(1)}, bf16[512,256]{1,0:T(8,128)(2,1)S(1)}, u32[]{:S(2)}, u32[]{:S(2)}) %collective-permute-start.10) | collective-permute-done | bytes 262176 | tf_op jit(solution)/shard_map/ppermute | solution.py:230
  45.1 6.7 %shard_map.56 = (bf16[512,256]{1,0:T(8,128)(2,1)}, bf16[512,256]{1,0:T(8,128)(2,1)}, bf16[512,256]{1,0:T(8,128)(2,1)}, bf16[512,256]{1,0:T(8,128)(2,1)}, f32[2,512,256]{2,1,0:T(8,128)}, /*index=5*/f32[2,512,256]{2,1,0:T(8,128)}) custom-call(s32[4]{0:T(128)} %pad_add_fusion.scalars, s32[3,32]{1,0:T(4,128)} %bitcast.15, bf16[8,256,256]{2,1,0:T(8,128)(2,1)} %cores_hbm.3, ...), custom_call_target="tpu_custom_call" | custom-call | tf_op jit(solution)/shard_map/pallas_call | solution.py:173
  52.0 2.0 %collective-permute-start.19 = (bf16[512,256]{1,0:T(8,128)(2,1)S(1)}, bf16[512,256]{1,0:T(8,128)(2,1)S(1)}, u32[]{:S(2)}, u32[]{:S(2)}) collective-permute-start(bf16[512,256]{1,0:T(8,128)(2,1)S(1)} %copy-done.16), channel_id=1, source_target_pairs={{0,8},{8,0},{16,24},{24,16},{1,9},{9,1},{17,25},{25,17},{2,10},{10... | collective-permute-start | bytes 786440 | tf_op jit(solution)/shard_map/ppermute | solution.py:245
  54.0 3.9 %collective-permute-start.17 = (bf16[512,256]{1,0:T(8,128)(2,1)}, bf16[512,256]{1,0:T(8,128)(2,1)S(1)}, u32[]{:S(2)}, u32[]{:S(2)}) collective-permute-start(bf16[512,256]{1,0:T(8,128)(2,1)} %get-tuple-element.22), channel_id=1, source_target_pairs={{0,7},{1,5},{2,6},{3,4},{4,3},{5,1},{6,2},{7,0},{8,13},{9,15},{10,... | collective-permute-start | bytes 786440 | tf_op jit(solution)/shard_map/ppermute | solution.py:261
  57.8 1.9 %collective-permute-start.16 = (bf16[512,256]{1,0:T(8,128)(2,1)S(1)}, bf16[512,256]{1,0:T(8,128)(2,1)S(1)}, u32[]{:S(2)}, u32[]{:S(2)}) collective-permute-start(bf16[512,256]{1,0:T(8,128)(2,1)S(1)} %copy-done.15), channel_id=1, source_target_pairs={{0,3},{1,1},{2,2},{3,0},{4,7},{5,5},{6,6},{7,4},{8,9},{9,11},{10,8... | collective-permute-start | bytes 786440 | tf_op jit(solution)/shard_map/ppermute | solution.py:261
  59.8 1.5 %collective-permute-done.21 = bf16[512,256]{1,0:T(8,128)(2,1)S(1)} collective-permute-done((bf16[512,256]{1,0:T(8,128)(2,1)}, bf16[512,256]{1,0:T(8,128)(2,1)S(1)}, u32[]{:S(2)}, u32[]{:S(2)}) %collective-permute-start.21) | collective-permute-done | bytes 262176 | tf_op jit(solution)/shard_map/ppermute | solution.py:245
  62.4 3.3 %collective-permute-done.19 = bf16[512,256]{1,0:T(8,128)(2,1)S(1)} collective-permute-done((bf16[512,256]{1,0:T(8,128)(2,1)S(1)}, bf16[512,256]{1,0:T(8,128)(2,1)S(1)}, u32[]{:S(2)}, u32[]{:S(2)}) %collective-permute-start.19) | collective-permute-done | bytes 262176 | tf_op jit(solution)/shard_map/ppermute | solution.py:245
  65.7 1.9 %collective-permute-start.13 = (bf16[512,256]{1,0:T(8,128)(2,1)S(1)}, bf16[512,256]{1,0:T(8,128)(2,1)S(1)}, u32[]{:S(2)}, u32[]{:S(2)}) collective-permute-start(bf16[512,256]{1,0:T(8,128)(2,1)S(1)} %copy-done.14), channel_id=1, source_target_pairs={{0,1},{1,3},{2,0},{3,2},{4,5},{5,7},{6,4},{7,6},{8,11},{9,9},{10,1... | collective-permute-start | bytes 786440 | tf_op jit(solution)/shard_map/ppermute | solution.py:261
  67.7 3.5 %collective-permute-start.22 = (bf16[512,256]{1,0:T(8,128)(2,1)S(1)}, bf16[512,256]{1,0:T(8,128)(2,1)S(1)}, u32[]{:S(2)}, u32[]{:S(2)}) collective-permute-start(bf16[512,256]{1,0:T(8,128)(2,1)S(1)} %add_convert_fusion.1), channel_id=1, source_target_pairs={{0,4},{1,6},{2,5},{3,7},{4,0},{5,2},{6,1},{7,3},{8,14},{9,12},{10,... | collective-permute-start | bytes 786440 | tf_op jit(solution)/shard_map/ppermute | solution.py:261
  72.0 5.8 %collective-permute-start.18 = (bf16[512,256]{1,0:T(8,128)(2,1)S(1)}, bf16[512,256]{1,0:T(8,128)(2,1)S(1)}, u32[]{:S(2)}, u32[]{:S(2)}) collective-permute-start(bf16[512,256]{1,0:T(8,128)(2,1)S(1)} %add_convert_fusion.3), channel_id=1, source_target_pairs={{0,24},{1,9},{2,18},{3,3},{4,28},{5,13},{6,22},{7,7},{8,16},{9,1},... | collective-permute-start | bytes 786440 | tf_op jit(solution)/shard_map/ppermute | solution.py:271
  77.9 4.1 %collective-permute-start.15 = (bf16[512,256]{1,0:T(8,128)(2,1)S(1)}, bf16[512,256]{1,0:T(8,128)(2,1)S(1)}, u32[]{:S(2)}, u32[]{:S(2)}) collective-permute-start(bf16[512,256]{1,0:T(8,128)(2,1)S(1)} %add_convert_fusion.4), channel_id=1, source_target_pairs={{0,16},{1,1},{2,26},{3,11},{4,20},{5,5},{6,30},{7,15},{8,24},{9,9}... | collective-permute-start | bytes 786440 | tf_op jit(solution)/shard_map/ppermute | solution.py:271
  82.8 3.6 %collective-permute-start.23 = (bf16[512,256]{1,0:T(8,128)(2,1)}, bf16[512,256]{1,0:T(8,128)(2,1)}, u32[]{:S(2)}, u32[]{:S(2)}) collective-permute-start(bf16[512,256]{1,0:T(8,128)(2,1)} %add_convert_fusion), channel_id=1, source_target_pairs={{0,0},{1,17},{2,10},{3,27},{4,4},{5,21},{6,14},{7,31},{8,8},{9,25}... | collective-permute-start | bytes 786440 | tf_op jit(solution)/shard_map/ppermute | solution.py:271
  86.8 10.1 %collective-permute-done.15 = bf16[512,256]{1,0:T(8,128)(2,1)S(1)} collective-permute-done((bf16[512,256]{1,0:T(8,128)(2,1)S(1)}, bf16[512,256]{1,0:T(8,128)(2,1)S(1)}, u32[]{:S(2)}, u32[]{:S(2)}) %collective-permute-start.15) | collective-permute-done | bytes 262176 | tf_op jit(solution)/shard_map/ppermute | solution.py:271
  96.9 1.9 %fusion.3 = f32[512,256]{1,0:T(8,128)} fusion(bf16[512,256]{1,0:T(8,128)(2,1)} %collective-permute-done.23, bf16[512,256]{1,0:T(8,128)(2,1)S(1)} %collective-permute-done.18, bf16[512,256]{1,0:T(8,128)(2,1)S(1)} %collective-permute-done.15, bf16[1,512,256]{2,1,0:T(8,128)(2,1)S(1)} %collective-permute-done.12, f32[2,512,256]{2,1,0:T(8,128)S(1)} %add.43, ...), kind=kLoop, calls=%fused_computation.4 | loop fusion | flops 1441792 | bytes 2359300 | tf_op jit(solution)/shard_map/sub | solution.py:272
  (69 shorter events, 9.2 us)
Async XLA Ops:
  0.0 13.1 %collective-permute-start = (bf16[512,256]{1,0:T(8,128)(2,1)}, bf16[512,256]{1,0:T(8,128)(2,1)S(1)}, u32[]{:S(2)}, u32[]{:S(2)}) collective-permute-start(bf16[512,256]{1,0:T(8,128)(2,1)} %refs_0_.3), channel_id=1, source_target_pairs={{0,1},{1,0},{2,3},{3,2},{4,5},{5,4},{6,7},{7,6},{8,9},{9,8},{10,11... | collective-permute-start | bytes 786440 | tf_op jit(solution)/shard_map/ppermute | solution.py:200
  0.5 17.2 %collective-permute-start.1 = (bf16[512,256]{1,0:T(8,128)(2,1)}, bf16[512,256]{1,0:T(8,128)(2,1)S(1)}, u32[]{:S(2)}, u32[]{:S(2)}) collective-permute-start(bf16[512,256]{1,0:T(8,128)(2,1)} %refs_0_.3), channel_id=1, source_target_pairs={{0,2},{1,3},{2,0},{3,1},{4,6},{5,7},{6,4},{7,5},{8,10},{9,11},{10,... | collective-permute-start | bytes 786440 | tf_op jit(solution)/shard_map/ppermute | solution.py:200
  3.0 16.2 %collective-permute-start.3 = (bf16[512,256]{1,0:T(8,128)(2,1)}, bf16[512,256]{1,0:T(8,128)(2,1)S(1)}, u32[]{:S(2)}, u32[]{:S(2)}) collective-permute-start(bf16[512,256]{1,0:T(8,128)(2,1)} %refs_0_.3), channel_id=1, source_target_pairs={{0,0},{10,1},{17,2},{27,3},{4,4},{14,5},{21,6},{31,7},{2,8},{8,9},... | collective-permute-start | bytes 786440 | tf_op jit(solution)/shard_map/ppermute | solution.py:221
  4.6 16.1 %collective-permute-start.5 = (bf16[512,256]{1,0:T(8,128)(2,1)}, bf16[512,256]{1,0:T(8,128)(2,1)S(1)}, u32[]{:S(2)}, u32[]{:S(2)}) collective-permute-start(bf16[512,256]{1,0:T(8,128)(2,1)} %refs_0_.3), channel_id=1, source_target_pairs={{2,0},{8,1},{19,2},{25,3},{6,4},{12,5},{23,6},{29,7},{0,8},{10,9},... | collective-permute-start | bytes 786440 | tf_op jit(solution)/shard_map/ppermute | solution.py:221
  8.6 12.6 %collective-permute-start.7 = (bf16[512,256]{1,0:T(8,128)(2,1)}, bf16[512,256]{1,0:T(8,128)(2,1)S(1)}, u32[]{:S(2)}, u32[]{:S(2)}) collective-permute-start(bf16[512,256]{1,0:T(8,128)(2,1)} %refs_0_.3), channel_id=1, source_target_pairs={{1,0},{11,1},{16,2},{26,3},{5,4},{15,5},{20,6},{30,7},{3,8},{9,9},... | collective-permute-start | bytes 786440 | tf_op jit(solution)/shard_map/ppermute | solution.py:221
  13.1 11.7 %collective-permute-start.9 = (bf16[512,256]{1,0:T(8,128)(2,1)}, bf16[512,256]{1,0:T(8,128)(2,1)S(1)}, u32[]{:S(2)}, u32[]{:S(2)}) collective-permute-start(bf16[512,256]{1,0:T(8,128)(2,1)} %refs_0_.3), channel_id=1, source_target_pairs={{3,0},{9,1},{18,2},{24,3},{7,4},{13,5},{22,6},{28,7},{1,8},{11,9},... | collective-permute-start | bytes 786440 | tf_op jit(solution)/shard_map/ppermute | solution.py:221
  17.7 9.9 %collective-permute-start.2 = (bf16[512,256]{1,0:T(8,128)(2,1)S(1)}, bf16[512,256]{1,0:T(8,128)(2,1)S(1)}, u32[]{:S(2)}, u32[]{:S(2)}) collective-permute-start(bf16[512,256]{1,0:T(8,128)(2,1)S(1)} %collective-permute-done.1.refs_2_), channel_id=1, source_target_pairs={{0,1},{1,0},{2,3},{3,2},{4,5},{5,4},{6,7},{7,6},{8,9},{9,8},{10,11... | collective-permute-start | bytes 786440 | tf_op jit(solution)/shard_map/ppermute | solution.py:200
  19.2 15.7 %collective-permute-start.4 = (bf16[512,256]{1,0:T(8,128)(2,1)S(1)}, bf16[512,256]{1,0:T(8,128)(2,1)S(1)}, u32[]{:S(2)}, u32[]{:S(2)}) collective-permute-start(bf16[512,256]{1,0:T(8,128)(2,1)S(1)} %collective-permute-done.3.refs_4_), channel_id=1, source_target_pairs={{0,4},{4,0},{1,5},{5,1},{2,6},{6,2},{3,7},{7,3},{8,12},{12,8},{9,1... | collective-permute-start | bytes 786440 | tf_op jit(solution)/shard_map/ppermute | solution.py:230
  20.7 14.2 %collective-permute-start.6 = (bf16[512,256]{1,0:T(8,128)(2,1)S(1)}, bf16[512,256]{1,0:T(8,128)(2,1)S(1)}, u32[]{:S(2)}, u32[]{:S(2)}) collective-permute-start(bf16[512,256]{1,0:T(8,128)(2,1)S(1)} %collective-permute-done.5.refs_5_), channel_id=1, source_target_pairs={{0,4},{4,0},{1,5},{5,1},{2,6},{6,2},{3,7},{7,3},{8,12},{12,8},{9,1... | collective-permute-start | bytes 786440 | tf_op jit(solution)/shard_map/ppermute | solution.py:230
  21.2 18.4 %collective-permute-start.8 = (bf16[512,256]{1,0:T(8,128)(2,1)S(1)}, bf16[512,256]{1,0:T(8,128)(2,1)S(1)}, u32[]{:S(2)}, u32[]{:S(2)}) collective-permute-start(bf16[512,256]{1,0:T(8,128)(2,1)S(1)} %collective-permute-done.7.refs_6_), channel_id=1, source_target_pairs={{0,4},{4,0},{1,5},{5,1},{2,6},{6,2},{3,7},{7,3},{8,12},{12,8},{9,1... | collective-permute-start | bytes 786440 | tf_op jit(solution)/shard_map/ppermute | solution.py:230
  24.9 19.5 %collective-permute-start.10 = (bf16[512,256]{1,0:T(8,128)(2,1)S(1)}, bf16[512,256]{1,0:T(8,128)(2,1)S(1)}, u32[]{:S(2)}, u32[]{:S(2)}) collective-permute-start(bf16[512,256]{1,0:T(8,128)(2,1)S(1)} %collective-permute-done.9.refs_7_), channel_id=1, source_target_pairs={{0,4},{4,0},{1,5},{5,1},{2,6},{6,2},{3,7},{7,3},{8,12},{12,8},{9,1... | collective-permute-start | bytes 786440 | tf_op jit(solution)/shard_map/ppermute | solution.py:230
  51.9 9.5 %collective-permute-start.21 = (bf16[512,256]{1,0:T(8,128)(2,1)}, bf16[512,256]{1,0:T(8,128)(2,1)S(1)}, u32[]{:S(2)}, u32[]{:S(2)}) collective-permute-start(bf16[512,256]{1,0:T(8,128)(2,1)} %get-tuple-element.26), channel_id=1, source_target_pairs={{0,8},{8,0},{16,24},{24,16},{1,9},{9,1},{17,25},{25,17},{2,10},{10... | collective-permute-start | bytes 786440 | tf_op jit(solution)/shard_map/ppermute | solution.py:245
  52.0 13.8 %collective-permute-start.19 = (bf16[512,256]{1,0:T(8,128)(2,1)S(1)}, bf16[512,256]{1,0:T(8,128)(2,1)S(1)}, u32[]{:S(2)}, u32[]{:S(2)}) collective-permute-start(bf16[512,256]{1,0:T(8,128)(2,1)S(1)} %copy-done.16), channel_id=1, source_target_pairs={{0,8},{8,0},{16,24},{24,16},{1,9},{9,1},{17,25},{25,17},{2,10},{10... | collective-permute-start | bytes 786440 | tf_op jit(solution)/shard_map/ppermute | solution.py:245
  54.0 13.8 %collective-permute-start.17 = (bf16[512,256]{1,0:T(8,128)(2,1)}, bf16[512,256]{1,0:T(8,128)(2,1)S(1)}, u32[]{:S(2)}, u32[]{:S(2)}) collective-permute-start(bf16[512,256]{1,0:T(8,128)(2,1)} %get-tuple-element.22), channel_id=1, source_target_pairs={{0,7},{1,5},{2,6},{3,4},{4,3},{5,1},{6,2},{7,0},{8,13},{9,15},{10,... | collective-permute-start | bytes 786440 | tf_op jit(solution)/shard_map/ppermute | solution.py:261
  57.8 13.4 %collective-permute-start.16 = (bf16[512,256]{1,0:T(8,128)(2,1)S(1)}, bf16[512,256]{1,0:T(8,128)(2,1)S(1)}, u32[]{:S(2)}, u32[]{:S(2)}) collective-permute-start(bf16[512,256]{1,0:T(8,128)(2,1)S(1)} %copy-done.15), channel_id=1, source_target_pairs={{0,3},{1,1},{2,2},{3,0},{4,7},{5,5},{6,6},{7,4},{8,9},{9,11},{10,8... | collective-permute-start | bytes 786440 | tf_op jit(solution)/shard_map/ppermute | solution.py:261
  59.8 12.2 %collective-permute-start.14 = (bf16[512,256]{1,0:T(8,128)(2,1)}, bf16[512,256]{1,0:T(8,128)(2,1)S(1)}, u32[]{:S(2)}, u32[]{:S(2)}) collective-permute-start(bf16[512,256]{1,0:T(8,128)(2,1)} %get-tuple-element.20), channel_id=1, source_target_pairs={{0,5},{1,7},{2,4},{3,6},{4,1},{5,3},{6,0},{7,2},{8,15},{9,13},{10,... | collective-permute-start | bytes 786440 | tf_op jit(solution)/shard_map/ppermute | solution.py:261
  61.3 25.1 %collective-permute-start.11 = (f32[2,512,256]{2,1,0:T(8,128)}, f32[2,512,256]{2,1,0:T(8,128)S(1)}, u32[]{:S(2)}, u32[]{:S(2)}) collective-permute-start(f32[2,512,256]{2,1,0:T(8,128)} %get-tuple-element.18), channel_id=1, source_target_pairs={{0,1},{1,0},{2,3},{3,2},{4,5},{5,4},{6,7},{7,6},{8,9},{9,8},{10,11... | collective-permute-start | bytes 3145736 | tf_op jit(solution)/shard_map/ppermute | solution.py:200
  65.7 12.1 %collective-permute-start.13 = (bf16[512,256]{1,0:T(8,128)(2,1)S(1)}, bf16[512,256]{1,0:T(8,128)(2,1)S(1)}, u32[]{:S(2)}, u32[]{:S(2)}) collective-permute-start(bf16[512,256]{1,0:T(8,128)(2,1)S(1)} %copy-done.14), channel_id=1, source_target_pairs={{0,1},{1,3},{2,0},{3,2},{4,5},{5,7},{6,4},{7,6},{8,11},{9,9},{10,1... | collective-permute-start | bytes 786440 | tf_op jit(solution)/shard_map/ppermute | solution.py:261
  67.7 14.3 %collective-permute-start.22 = (bf16[512,256]{1,0:T(8,128)(2,1)S(1)}, bf16[512,256]{1,0:T(8,128)(2,1)S(1)}, u32[]{:S(2)}, u32[]{:S(2)}) collective-permute-start(bf16[512,256]{1,0:T(8,128)(2,1)S(1)} %add_convert_fusion.1), channel_id=1, source_target_pairs={{0,4},{1,6},{2,5},{3,7},{4,0},{5,2},{6,1},{7,3},{8,14},{9,12},{10,... | collective-permute-start | bytes 786440 | tf_op jit(solution)/shard_map/ppermute | solution.py:261
  71.2 10.9 %collective-permute-start.20 = (bf16[512,256]{1,0:T(8,128)(2,1)S(1)}, bf16[512,256]{1,0:T(8,128)(2,1)S(1)}, u32[]{:S(2)}, u32[]{:S(2)}) collective-permute-start(bf16[512,256]{1,0:T(8,128)(2,1)S(1)} %add_convert_fusion.2), channel_id=1, source_target_pairs={{0,0},{1,2},{2,1},{3,3},{4,4},{5,6},{6,5},{7,7},{8,10},{9,8},{10,1... | collective-permute-start | bytes 786440 | tf_op jit(solution)/shard_map/ppermute | solution.py:261
  72.0 14.8 %collective-permute-start.18 = (bf16[512,256]{1,0:T(8,128)(2,1)S(1)}, bf16[512,256]{1,0:T(8,128)(2,1)S(1)}, u32[]{:S(2)}, u32[]{:S(2)}) collective-permute-start(bf16[512,256]{1,0:T(8,128)(2,1)S(1)} %add_convert_fusion.3), channel_id=1, source_target_pairs={{0,24},{1,9},{2,18},{3,3},{4,28},{5,13},{6,22},{7,7},{8,16},{9,1},... | collective-permute-start | bytes 786440 | tf_op jit(solution)/shard_map/ppermute | solution.py:271
  77.9 19.0 %collective-permute-start.15 = (bf16[512,256]{1,0:T(8,128)(2,1)S(1)}, bf16[512,256]{1,0:T(8,128)(2,1)S(1)}, u32[]{:S(2)}, u32[]{:S(2)}) collective-permute-start(bf16[512,256]{1,0:T(8,128)(2,1)S(1)} %add_convert_fusion.4), channel_id=1, source_target_pairs={{0,16},{1,1},{2,26},{3,11},{4,20},{5,5},{6,30},{7,15},{8,24},{9,9}... | collective-permute-start | bytes 786440 | tf_op jit(solution)/shard_map/ppermute | solution.py:271
  82.8 14.1 %collective-permute-start.23 = (bf16[512,256]{1,0:T(8,128)(2,1)}, bf16[512,256]{1,0:T(8,128)(2,1)}, u32[]{:S(2)}, u32[]{:S(2)}) collective-permute-start(bf16[512,256]{1,0:T(8,128)(2,1)} %add_convert_fusion), channel_id=1, source_target_pairs={{0,0},{1,17},{2,10},{3,27},{4,4},{5,21},{6,14},{7,31},{8,8},{9,25}... | collective-permute-start | bytes 786440 | tf_op jit(solution)/shard_map/ppermute | solution.py:271
  86.6 10.3 %collective-permute-start.12 = (bf16[1,512,256]{2,1,0:T(8,128)(2,1)S(1)}, bf16[1,512,256]{2,1,0:T(8,128)(2,1)S(1)}, u32[]{:S(2)}, u32[]{:S(2)}) collective-permute-start(bf16[1,512,256]{2,1,0:T(8,128)(2,1)S(1)} %dynamic-slice_convert_fusion), channel_id=1, source_target_pairs={{0,2},{1,3},{2,0},{3,1},{4,6},{5,7},{6,4},{7,5},{8,10},{9,11},{10,... | collective-permute-start | bytes 786440 | tf_op jit(solution)/shard_map/ppermute | solution.py:200
  (17 other events, 216.5 us)

commit v4 on v3

--- a/solution.py
+++ b/solution.py
@@ -223,29 +223,43 @@
     bit = n_col // 2
     while bit:
         for o, value in list(src.items()):
+            if bit == 1 and o:
+                value = lax.optimization_barrier((value, own[0]))[0]
             src[o | bit] = swap(value, bit, n_col)
         bit //= 2
     src = [src[o] for o in range(n_col)]
     cross = {
         d: [lax.ppermute(own[d], "xx", [(x, (x + s) % ratio) for x in range(ratio)]) for s in range(1, ratio)]
-        for d in own
+        for d in range(n_col)
     }
 
     fixed = (n_col, ratio, scalars, coords, cores, src)
+    def to_owner(value, d, t):
+        return lax.ppermute(value, AXES, part_pairs(d, lambda p, x, j, q: (p, (x - t) % ratio, q)))
+
+    def to_pair(value):
+        return lax.ppermute(value, "zz", [(p, p ^ 1) for p in range(planes)])
+
+    halving = [d for d in range(n_col) if d // 2 % 2 == 1]
+    direct = [d for d in range(n_col) if d // 2 % 2 == 0]
     own_grad, src_grad = run_slots(0, 1, None, *fixed, [own[d] for d in range(n_col)], tiles, [])
+    came = {d: [to_pair(own_grad[d + 1])] for d in halving[::2]}
+    arrived = {d: [to_owner(own_grad[d], d, 0)] for d in direct}
     grads = {d: [own_grad[d]] for d in range(n_col)}
     if ratio > 1:
         held = [v for d in range(n_col) for v in cross[d]]
-        target, src_grad = run_slots(1, ratio, None, *fixed, held, tiles, src_grad)
+        target, src_grad = run_slots(1, ratio, None, *fixed, held, tiles, src_grad, own_grad)
+        target = {d: target[d * (ratio - 1) : (d + 1) * (ratio - 1)] for d in range(n_col)}
+        target, came, arrived = lax.optimization_barrier((target, came, arrived))
         for d in range(n_col):
-            grads[d].extend(target[d * (ratio - 1) : (d + 1) * (ratio - 1)])
+            grads[d].extend(target[d])
+        for t in range(1, ratio):
+            for d in came:
+                came[d].append(to_pair(grads[d + 1][t]))
+            for d in direct:
+                arrived[d].append(to_owner(grads[d][t], d, t))
     src_keep, src_send = src_grad
 
-    for d in range(0, n_col, 4):
-        gone = [lax.ppermute(v, "zz", [(p, p ^ 1) for p in range(planes)]) for v in grads.pop(d + 1)]
-        grads[d] = [
-            (a.astype(jnp.float32) + b.astype(jnp.float32)).astype(jnp.bfloat16) for a, b in zip(grads[d], gone)
-        ]
     src_sum = src_keep + swap(src_send, 1, n_col)
     bit = 2
     while bit < n_col:
@@ -256,19 +270,23 @@
         src_sum = kept + swap(out, bit, n_col).astype(jnp.float32)
         bit *= 2
     total = src_sum[0]
-    for d in sorted(grads, key=lambda d: -(d // 2 % 2)):
-        arrived = [
-            lax.ppermute(grads[d][t], AXES, part_pairs(d, lambda p, x, j, q, t=t: (p, (x - t) % ratio, q)))
-            for t in range(ratio)
+
+    for d in came:
+        arrived[d] = [
+            to_owner((a.astype(jnp.float32) + b.astype(jnp.float32)).astype(jnp.bfloat16), d, t)
+            for t, (a, b) in enumerate(zip(grads[d], came[d]))
         ]
-        term = sum(v.astype(jnp.float32) for v in arrived).astype(jnp.bfloat16)
+    landed = []
+    for d, values in arrived.items():
+        term = sum(v.astype(jnp.float32) for v in values).astype(jnp.bfloat16)
         pairs = [
             ((p * ratio + x) * n_col + q, ((p ^ mirror(q, n_col) ^ d) * ratio + x) * n_col + q)
             for p in range(planes)
             for x in range(ratio)
             for q in range(n_col)
         ]
-        total = total + lax.ppermute(term, AXES, pairs).astype(jnp.float32)
+        landed.append(lax.ppermute(term, AXES, pairs))
+    total = total + sum(v.astype(jnp.float32) for v in landed)
     return weight_decay * factors.astype(jnp.float32) - total / tile
 
 

time: 98.9 us -> 94.3 us (0.953)
  waiting for transfers between devices: 26.6 us -> 21.4 us
    ppermute x4, waiting for transfers between devices: 9.44 us -> 0.01 us  [local(): lax.ppermute(own[d], 'xx', [(x, (x + s) % ratio) for x in range(ratio)])]
    ppermute x5, starting transfers between devices: 4.69 us -> 11.4 us  [swap(): return lax.ppermute(value, 'col', [(i, i ^ bit) for i in range(n_col)])]
    ppermute x11, waiting for transfers between devices: 15 us -> 20 us  [the longest x6 9.54 us: to_owner(): lax.ppermute(value, AXES, part_pairs(d, lambda p, x, j, q: (p, (x - t) %...]
    ppermute x4, starting transfers between devices: 14.6 us -> 10.9 us  [local(): own[d] = lax.ppermute(factors, AXES, [(b, a) for a, b in pairs])]
    ppermute x11, starting transfers between devices: 27.6 us -> 24 us  [the longest x6 12.3 us: to_owner(): lax.ppermute(value, AXES, part_pairs(d, lambda p, x, j, q: (p, (x - t) %...]
  transfers between devices with their start and end apart: 24 -> 24, of which waited for: 6 -> 7; matrix products, arithmetic and copies ran while one was open for 3% -> 3% of each run, Pallas kernels for 7% -> 14%
where the time goes in v4:
time: 94.3 us; the launch traced here: 93.3 us
  starting transfers between devices  51.4 us (55%)
  waiting for transfers between devices  21.4 us (23%)
  Pallas kernels  13.4 us (14%)
  other arithmetic  4.68 us (5%)
  local copies, waits for them, and re-layouts  1.46 us (2%)
  between operations  1 us (1%)
    pallas_call x2, Pallas kernels, run_slots(): pl.pallas_call(functools.partial(slots_kernel, first, last, late, len(wai...  13.4 us
    ppermute x6, starting transfers between devices, to_owner(): lax.ppermute(value, AXES, part_pairs(d, lambda p, x, j, q: (p, (x - t) %...  12.3 us
    ppermute x5, starting transfers between devices, swap(): return lax.ppermute(value, 'col', [(i, i ^ bit) for i in range(n_col)])  11.4 us
    ppermute x4, starting transfers between devices, local(): own[d] = lax.ppermute(factors, AXES, [(b, a) for a, b in pairs])  10.9 us
    ppermute x6, waiting for transfers between devices, to_owner(): lax.ppermute(value, AXES, part_pairs(d, lambda p, x, j, q: (p, (x - t) %...  9.54 us
    ppermute x3, waiting for transfers between devices, local(): landed.append(lax.ppermute(term, AXES, pairs))  8.75 us
    ppermute x2, starting transfers between devices, to_pair(): return lax.ppermute(value, 'zz', [(p, p ^ 1) for p in range(planes)])  6.38 us
    ppermute x3, starting transfers between devices, local(): landed.append(lax.ppermute(term, AXES, pairs))  5.31 us
  transfers between devices with their start and end apart: 24, of which 7 were waited for; matrix products, arithmetic and copies ran while one was open for 3% of the time, Pallas kernels for 14%

profile of v4, /device:TPU:0, one launch (start us, length us, event | category | flops | bytes accessed | tf_op | source)
XLA Modules:
  0.0 93.3 jit_solution(7638443954971508816)
XLA Ops:
  0.0 3.0 %collective-permute-start.1 = (bf16[512,256]{1,0:T(8,128)(2,1)}, bf16[512,256]{1,0:T(8,128)(2,1)S(1)}, u32[]{:S(2)}, u32[]{:S(2)}) collective-permute-start(bf16[512,256]{1,0:T(8,128)(2,1)} %refs_0_.3), channel_id=1, source_target_pairs={{0,2},{1,3},{2,0},{3,1},{4,6},{5,7},{6,4},{7,5},{8,10},{9,11},{10,... | collective-permute-start | bytes 786440 | tf_op jit(solution)/shard_map/ppermute | solution.py:200
  3.0 1.6 %collective-permute-start.2 = (bf16[512,256]{1,0:T(8,128)(2,1)}, bf16[512,256]{1,0:T(8,128)(2,1)S(1)}, u32[]{:S(2)}, u32[]{:S(2)}) collective-permute-start(bf16[512,256]{1,0:T(8,128)(2,1)} %refs_0_.3), channel_id=1, source_target_pairs={{0,0},{10,1},{17,2},{27,3},{4,4},{14,5},{21,6},{31,7},{2,8},{8,9},... | collective-permute-start | bytes 786440 | tf_op jit(solution)/shard_map/ppermute | solution.py:221
  4.6 3.1 %collective-permute-start = (bf16[512,256]{1,0:T(8,128)(2,1)}, bf16[512,256]{1,0:T(8,128)(2,1)S(1)}, u32[]{:S(2)}, u32[]{:S(2)}) collective-permute-start(bf16[512,256]{1,0:T(8,128)(2,1)} %refs_0_.3), channel_id=1, source_target_pairs={{0,1},{1,0},{2,3},{3,2},{4,5},{5,4},{6,7},{7,6},{8,9},{9,8},{10,11... | collective-permute-start | bytes 786440 | tf_op jit(solution)/shard_map/ppermute | solution.py:200
  7.6 2.8 %collective-permute-start.9 = (bf16[512,256]{1,0:T(8,128)(2,1)}, bf16[512,256]{1,0:T(8,128)(2,1)S(1)}, u32[]{:S(2)}, u32[]{:S(2)}) collective-permute-start(bf16[512,256]{1,0:T(8,128)(2,1)} %refs_0_.3), channel_id=1, source_target_pairs={{3,0},{9,1},{18,2},{24,3},{7,4},{13,5},{22,6},{28,7},{1,8},{11,9},... | collective-permute-start | bytes 786440 | tf_op jit(solution)/shard_map/ppermute | solution.py:221
  10.5 2.0 %collective-permute-start.5 = (bf16[512,256]{1,0:T(8,128)(2,1)}, bf16[512,256]{1,0:T(8,128)(2,1)S(1)}, u32[]{:S(2)}, u32[]{:S(2)}) collective-permute-start(bf16[512,256]{1,0:T(8,128)(2,1)} %refs_0_.3), channel_id=1, source_target_pairs={{2,0},{8,1},{19,2},{25,3},{6,4},{12,5},{23,6},{29,7},{0,8},{10,9},... | collective-permute-start | bytes 786440 | tf_op jit(solution)/shard_map/ppermute | solution.py:221
  12.6 4.4 %collective-permute-start.7 = (bf16[512,256]{1,0:T(8,128)(2,1)}, bf16[512,256]{1,0:T(8,128)(2,1)S(1)}, u32[]{:S(2)}, u32[]{:S(2)}) collective-permute-start(bf16[512,256]{1,0:T(8,128)(2,1)} %refs_0_.3), channel_id=1, source_target_pairs={{1,0},{11,1},{16,2},{26,3},{5,4},{15,5},{20,6},{30,7},{3,8},{9,9},... | collective-permute-start | bytes 786440 | tf_op jit(solution)/shard_map/ppermute | solution.py:221
  17.0 2.0 %collective-permute-start.3 = (bf16[512,256]{1,0:T(8,128)(2,1)S(1)}, bf16[512,256]{1,0:T(8,128)(2,1)S(1)}, u32[]{:S(2)}, u32[]{:S(2)}) collective-permute-start(bf16[512,256]{1,0:T(8,128)(2,1)S(1)} %collective-permute-done.1.refs_2_), channel_id=1, source_target_pairs={{0,1},{1,0},{2,3},{3,2},{4,5},{5,4},{6,7},{7,6},{8,9},{9,8},{10,11... | collective-permute-start | bytes 786440 | tf_op jit(solution)/shard_map/ppermute | solution.py:200
  27.4 6.6 %shard_map.55 = (bf16[512,256]{1,0:T(8,128)(2,1)}, bf16[512,256]{1,0:T(8,128)(2,1)}, bf16[512,256]{1,0:T(8,128)(2,1)}, bf16[512,256]{1,0:T(8,128)(2,1)}, f32[2048,256]{1,0:T(8,128)}) custom-call(s32[4]{0:T(128)} %pad_add_fusion.scalars, s32[3,32]{1,0:T(4,128)} %bitcast.10, bf16[8,256,256]{2,1,0:T(8,128)(2,1)} %cores_hbm.3, bf16[512,256]{1,0:T(8,128)(2,1)} %refs_0_.3, ...), custom_call_target="tpu_custom_call" | custom-call | tf_op jit(solution)/shard_map/pallas_call | solution.py:173
  34.0 6.3 %collective-permute-start.13 = (bf16[512,256]{1,0:T(8,128)(2,1)}, bf16[512,256]{1,0:T(8,128)(2,1)S(1)}, u32[]{:S(2)}, u32[]{:S(2)}) collective-permute-start(bf16[512,256]{1,0:T(8,128)(2,1)} %get-tuple-element.29.refs_13_), channel_id=1, source_target_pairs={{0,8},{8,0},{16,24},{24,16},{1,9},{9,1},{17,25},{25,17},{2,10},{10... | collective-permute-start | bytes 786440 | tf_op jit(solution)/shard_map/ppermute | solution.py:241
  40.3 1.6 %collective-permute-start.14 = (bf16[512,256]{1,0:T(8,128)(2,1)}, bf16[512,256]{1,0:T(8,128)(2,1)S(1)}, u32[]{:S(2)}, u32[]{:S(2)}) collective-permute-start(bf16[512,256]{1,0:T(8,128)(2,1)} %get-tuple-element.26.refs_10_), channel_id=1, source_target_pairs={{0,0},{1,2},{2,1},{3,3},{4,4},{5,6},{6,5},{7,7},{8,10},{9,8},{10,1... | collective-permute-start | bytes 786440 | tf_op jit(solution)/shard_map/ppermute | solution.py:238
  41.9 6.0 %collective-permute-start.15 = (bf16[512,256]{1,0:T(8,128)(2,1)}, bf16[512,256]{1,0:T(8,128)(2,1)S(1)}, u32[]{:S(2)}, u32[]{:S(2)}) collective-permute-start(bf16[512,256]{1,0:T(8,128)(2,1)} %get-tuple-element.27.refs_11_), channel_id=1, source_target_pairs={{0,2},{1,0},{2,3},{3,1},{4,6},{5,4},{6,7},{7,5},{8,8},{9,10},{10,9... | collective-permute-start | bytes 786440 | tf_op jit(solution)/shard_map/ppermute | solution.py:238
  48.7 6.8 %shard_map.56 = (bf16[512,256]{1,0:T(8,128)(2,1)}, bf16[512,256]{1,0:T(8,128)(2,1)}, bf16[512,256]{1,0:T(8,128)(2,1)}, bf16[512,256]{1,0:T(8,128)(2,1)}, f32[2,512,256]{2,1,0:T(8,128)}, /*index=5*/f32[2,512,256]{2,1,0:T(8,128)}) custom-call(s32[4]{0:T(128)} %pad_add_fusion.scalars, s32[3,32]{1,0:T(4,128)} %bitcast.11, bf16[8,256,256]{2,1,0:T(8,128)(2,1)} %cores_hbm.3, ...), custom_call_target="tpu_custom_call" | custom-call | tf_op jit(solution)/shard_map/pallas_call | solution.py:173
  55.7 2.0 %collective-permute-start.11 = (f32[2,512,256]{2,1,0:T(8,128)}, f32[2,512,256]{2,1,0:T(8,128)S(1)}, u32[]{:S(2)}, u32[]{:S(2)}) collective-permute-start(f32[2,512,256]{2,1,0:T(8,128)} %get-tuple-element.31), channel_id=1, source_target_pairs={{0,1},{1,0},{2,3},{3,2},{4,5},{5,4},{6,7},{7,6},{8,9},{9,8},{10,11... | collective-permute-start | bytes 3145736 | tf_op jit(solution)/shard_map/ppermute | solution.py:200
  57.7 2.6 %collective-permute-start.18 = (bf16[512,256]{1,0:T(8,128)(2,1)}, bf16[512,256]{1,0:T(8,128)(2,1)S(1)}, u32[]{:S(2)}, u32[]{:S(2)}) collective-permute-start(bf16[512,256]{1,0:T(8,128)(2,1)} %get-tuple-element.39), channel_id=1, source_target_pairs={{0,6},{1,4},{2,7},{3,5},{4,2},{5,0},{6,3},{7,1},{8,12},{9,14},{10,... | collective-permute-start | bytes 786440 | tf_op jit(solution)/shard_map/ppermute | solution.py:238
  60.4 1.9 %collective-permute-start.20 = (bf16[512,256]{1,0:T(8,128)(2,1)S(1)}, bf16[512,256]{1,0:T(8,128)(2,1)S(1)}, u32[]{:S(2)}, u32[]{:S(2)}) collective-permute-start(bf16[512,256]{1,0:T(8,128)(2,1)S(1)} %add_convert_fusion.2), channel_id=1, source_target_pairs={{0,1},{1,3},{2,0},{3,2},{4,5},{5,7},{6,4},{7,6},{8,11},{9,9},{10,1... | collective-permute-start | bytes 786440 | tf_op jit(solution)/shard_map/ppermute | solution.py:238
  62.3 1.7 %collective-permute-done.21 = bf16[512,256]{1,0:T(8,128)(2,1)S(1)} collective-permute-done((bf16[512,256]{1,0:T(8,128)(2,1)}, bf16[512,256]{1,0:T(8,128)(2,1)S(1)}, u32[]{:S(2)}, u32[]{:S(2)}) %collective-permute-start.21) | collective-permute-done | bytes 262176 | tf_op jit(solution)/shard_map/ppermute | solution.py:241
  65.2 1.8 %collective-permute-done.16 = bf16[512,256]{1,0:T(8,128)(2,1)S(1)} collective-permute-done((bf16[512,256]{1,0:T(8,128)(2,1)}, bf16[512,256]{1,0:T(8,128)(2,1)S(1)}, u32[]{:S(2)}, u32[]{:S(2)}) %collective-permute-start.16) | collective-permute-done | bytes 262176 | tf_op jit(solution)/shard_map/ppermute | solution.py:238
  67.8 4.6 %collective-permute-done.18 = bf16[512,256]{1,0:T(8,128)(2,1)S(1)} collective-permute-done((bf16[512,256]{1,0:T(8,128)(2,1)}, bf16[512,256]{1,0:T(8,128)(2,1)S(1)}, u32[]{:S(2)}, u32[]{:S(2)}) %collective-permute-start.18) | collective-permute-done | bytes 262176 | tf_op jit(solution)/shard_map/ppermute | solution.py:238
  72.5 2.7 %collective-permute-start.19 = (bf16[512,256]{1,0:T(8,128)(2,1)S(1)}, bf16[512,256]{1,0:T(8,128)(2,1)S(1)}, u32[]{:S(2)}, u32[]{:S(2)}) collective-permute-start(bf16[512,256]{1,0:T(8,128)(2,1)S(1)} %add_convert_fusion.3), channel_id=1, source_target_pairs={{0,8},{1,25},{2,2},{3,19},{4,12},{5,29},{6,6},{7,23},{8,0},{9,17},... | collective-permute-start | bytes 786440 | tf_op jit(solution)/shard_map/ppermute | solution.py:288
  75.3 3.1 %collective-permute-done.22 = bf16[512,256]{1,0:T(8,128)(2,1)S(1)} collective-permute-done((bf16[512,256]{1,0:T(8,128)(2,1)S(1)}, bf16[512,256]{1,0:T(8,128)(2,1)S(1)}, u32[]{:S(2)}, u32[]{:S(2)}) %collective-permute-start.22) | collective-permute-done | bytes 262176 | tf_op jit(solution)/shard_map/ppermute | solution.py:238
  79.1 1.9 %collective-permute-start.23 = (bf16[512,256]{1,0:T(8,128)(2,1)}, bf16[512,256]{1,0:T(8,128)(2,1)}, u32[]{:S(2)}, u32[]{:S(2)}) collective-permute-start(bf16[512,256]{1,0:T(8,128)(2,1)} %add_convert_fusion), channel_id=1, source_target_pairs={{0,16},{1,1},{2,26},{3,11},{4,20},{5,5},{6,30},{7,15},{8,24},{9,9}... | collective-permute-start | bytes 786440 | tf_op jit(solution)/shard_map/ppermute | solution.py:288
  82.7 1.5 %collective-permute-done.19 = bf16[512,256]{1,0:T(8,128)(2,1)S(1)} collective-permute-done((bf16[512,256]{1,0:T(8,128)(2,1)S(1)}, bf16[512,256]{1,0:T(8,128)(2,1)S(1)}, u32[]{:S(2)}, u32[]{:S(2)}) %collective-permute-start.19) | collective-permute-done | bytes 262176 | tf_op jit(solution)/shard_map/ppermute | solution.py:288
  84.2 7.2 %collective-permute-done.23 = bf16[512,256]{1,0:T(8,128)(2,1)} collective-permute-done((bf16[512,256]{1,0:T(8,128)(2,1)}, bf16[512,256]{1,0:T(8,128)(2,1)}, u32[]{:S(2)}, u32[]{:S(2)}) %collective-permute-start.23) | collective-permute-done | bytes 262176 | tf_op jit(solution)/shard_map/ppermute | solution.py:288
  91.4 1.9 %fusion.1 = f32[512,256]{1,0:T(8,128)} fusion(bf16[512,256]{1,0:T(8,128)(2,1)} %collective-permute-done.23, bf16[512,256]{1,0:T(8,128)(2,1)S(1)} %collective-permute-done.19, bf16[512,256]{1,0:T(8,128)(2,1)S(1)} %collective-permute-done.17, bf16[1,512,256]{2,1,0:T(8,128)(2,1)S(1)} %collective-permute-done.12, f32[2,512,256]{2,1,0:T(8,128)S(1)} %add.43, ...), kind=kLoop, calls=%fused_computation.2 | loop fusion | flops 1441792 | bytes 2359300 | tf_op jit(solution)/shard_map/sub | solution.py:290
  (63 shorter events, 13.1 us)
Async XLA Ops:
  0.0 12.5 %collective-permute-start.1 = (bf16[512,256]{1,0:T(8,128)(2,1)}, bf16[512,256]{1,0:T(8,128)(2,1)S(1)}, u32[]{:S(2)}, u32[]{:S(2)}) collective-permute-start(bf16[512,256]{1,0:T(8,128)(2,1)} %refs_0_.3), channel_id=1, source_target_pairs={{0,2},{1,3},{2,0},{3,1},{4,6},{5,7},{6,4},{7,5},{8,10},{9,11},{10,... | collective-permute-start | bytes 786440 | tf_op jit(solution)/shard_map/ppermute | solution.py:200
  3.0 14.0 %collective-permute-start.2 = (bf16[512,256]{1,0:T(8,128)(2,1)}, bf16[512,256]{1,0:T(8,128)(2,1)S(1)}, u32[]{:S(2)}, u32[]{:S(2)}) collective-permute-start(bf16[512,256]{1,0:T(8,128)(2,1)} %refs_0_.3), channel_id=1, source_target_pairs={{0,0},{10,1},{17,2},{27,3},{4,4},{14,5},{21,6},{31,7},{2,8},{8,9},... | collective-permute-start | bytes 786440 | tf_op jit(solution)/shard_map/ppermute | solution.py:221
  4.6 14.4 %collective-permute-start = (bf16[512,256]{1,0:T(8,128)(2,1)}, bf16[512,256]{1,0:T(8,128)(2,1)S(1)}, u32[]{:S(2)}, u32[]{:S(2)}) collective-permute-start(bf16[512,256]{1,0:T(8,128)(2,1)} %refs_0_.3), channel_id=1, source_target_pairs={{0,1},{1,0},{2,3},{3,2},{4,5},{5,4},{6,7},{7,6},{8,9},{9,8},{10,11... | collective-permute-start | bytes 786440 | tf_op jit(solution)/shard_map/ppermute | solution.py:200
  7.6 12.8 %collective-permute-start.9 = (bf16[512,256]{1,0:T(8,128)(2,1)}, bf16[512,256]{1,0:T(8,128)(2,1)S(1)}, u32[]{:S(2)}, u32[]{:S(2)}) collective-permute-start(bf16[512,256]{1,0:T(8,128)(2,1)} %refs_0_.3), channel_id=1, source_target_pairs={{3,0},{9,1},{18,2},{24,3},{7,4},{13,5},{22,6},{28,7},{1,8},{11,9},... | collective-permute-start | bytes 786440 | tf_op jit(solution)/shard_map/ppermute | solution.py:221
  10.5 11.8 %collective-permute-start.5 = (bf16[512,256]{1,0:T(8,128)(2,1)}, bf16[512,256]{1,0:T(8,128)(2,1)S(1)}, u32[]{:S(2)}, u32[]{:S(2)}) collective-permute-start(bf16[512,256]{1,0:T(8,128)(2,1)} %refs_0_.3), channel_id=1, source_target_pairs={{2,0},{8,1},{19,2},{25,3},{6,4},{12,5},{23,6},{29,7},{0,8},{10,9},... | collective-permute-start | bytes 786440 | tf_op jit(solution)/shard_map/ppermute | solution.py:221
  12.6 12.6 %collective-permute-start.7 = (bf16[512,256]{1,0:T(8,128)(2,1)}, bf16[512,256]{1,0:T(8,128)(2,1)S(1)}, u32[]{:S(2)}, u32[]{:S(2)}) collective-permute-start(bf16[512,256]{1,0:T(8,128)(2,1)} %refs_0_.3), channel_id=1, source_target_pairs={{1,0},{11,1},{16,2},{26,3},{5,4},{15,5},{20,6},{30,7},{3,8},{9,9},... | collective-permute-start | bytes 786440 | tf_op jit(solution)/shard_map/ppermute | solution.py:221
  17.0 9.7 %collective-permute-start.3 = (bf16[512,256]{1,0:T(8,128)(2,1)S(1)}, bf16[512,256]{1,0:T(8,128)(2,1)S(1)}, u32[]{:S(2)}, u32[]{:S(2)}) collective-permute-start(bf16[512,256]{1,0:T(8,128)(2,1)S(1)} %collective-permute-done.1.refs_2_), channel_id=1, source_target_pairs={{0,1},{1,0},{2,3},{3,2},{4,5},{5,4},{6,7},{7,6},{8,9},{9,8},{10,11... | collective-permute-start | bytes 786440 | tf_op jit(solution)/shard_map/ppermute | solution.py:200
  19.0 21.3 %collective-permute-start.4 = (bf16[512,256]{1,0:T(8,128)(2,1)S(1)}, bf16[512,256]{1,0:T(8,128)(2,1)S(1)}, u32[]{:S(2)}, u32[]{:S(2)}) collective-permute-start(bf16[512,256]{1,0:T(8,128)(2,1)S(1)} %collective-permute-done.2.refs_4_), channel_id=1, source_target_pairs={{0,4},{4,0},{1,5},{5,1},{2,6},{6,2},{3,7},{7,3},{8,12},{12,8},{9,1... | collective-permute-start | bytes 786440 | tf_op jit(solution)/shard_map/ppermute | solution.py:232
  20.5 21.4 %collective-permute-start.10 = (bf16[512,256]{1,0:T(8,128)(2,1)S(1)}, bf16[512,256]{1,0:T(8,128)(2,1)S(1)}, u32[]{:S(2)}, u32[]{:S(2)}) collective-permute-start(bf16[512,256]{1,0:T(8,128)(2,1)S(1)} %collective-permute-done.9.refs_7_), channel_id=1, source_target_pairs={{0,4},{4,0},{1,5},{5,1},{2,6},{6,2},{3,7},{7,3},{8,12},{12,8},{9,1... | collective-permute-start | bytes 786440 | tf_op jit(solution)/shard_map/ppermute | solution.py:232
  22.3 25.6 %collective-permute-start.6 = (bf16[512,256]{1,0:T(8,128)(2,1)S(1)}, bf16[512,256]{1,0:T(8,128)(2,1)S(1)}, u32[]{:S(2)}, u32[]{:S(2)}) collective-permute-start(bf16[512,256]{1,0:T(8,128)(2,1)S(1)} %collective-permute-done.5.refs_5_), channel_id=1, source_target_pairs={{0,4},{4,0},{1,5},{5,1},{2,6},{6,2},{3,7},{7,3},{8,12},{12,8},{9,1... | collective-permute-start | bytes 786440 | tf_op jit(solution)/shard_map/ppermute | solution.py:232
  25.2 22.7 %collective-permute-start.8 = (bf16[512,256]{1,0:T(8,128)(2,1)S(1)}, bf16[512,256]{1,0:T(8,128)(2,1)S(1)}, u32[]{:S(2)}, u32[]{:S(2)}) collective-permute-start(bf16[512,256]{1,0:T(8,128)(2,1)S(1)} %collective-permute-done.7.refs_6_), channel_id=1, source_target_pairs={{0,4},{4,0},{1,5},{5,1},{2,6},{6,2},{3,7},{7,3},{8,12},{12,8},{9,1... | collective-permute-start | bytes 786440 | tf_op jit(solution)/shard_map/ppermute | solution.py:232
  34.0 21.5 %collective-permute-start.13 = (bf16[512,256]{1,0:T(8,128)(2,1)}, bf16[512,256]{1,0:T(8,128)(2,1)S(1)}, u32[]{:S(2)}, u32[]{:S(2)}) collective-permute-start(bf16[512,256]{1,0:T(8,128)(2,1)} %get-tuple-element.29.refs_13_), channel_id=1, source_target_pairs={{0,8},{8,0},{16,24},{24,16},{1,9},{9,1},{17,25},{25,17},{2,10},{10... | collective-permute-start | bytes 786440 | tf_op jit(solution)/shard_map/ppermute | solution.py:241
  40.3 15.2 %collective-permute-start.14 = (bf16[512,256]{1,0:T(8,128)(2,1)}, bf16[512,256]{1,0:T(8,128)(2,1)S(1)}, u32[]{:S(2)}, u32[]{:S(2)}) collective-permute-start(bf16[512,256]{1,0:T(8,128)(2,1)} %get-tuple-element.26.refs_10_), channel_id=1, source_target_pairs={{0,0},{1,2},{2,1},{3,3},{4,4},{5,6},{6,5},{7,7},{8,10},{9,8},{10,1... | collective-permute-start | bytes 786440 | tf_op jit(solution)/shard_map/ppermute | solution.py:238
  41.9 13.6 %collective-permute-start.15 = (bf16[512,256]{1,0:T(8,128)(2,1)}, bf16[512,256]{1,0:T(8,128)(2,1)S(1)}, u32[]{:S(2)}, u32[]{:S(2)}) collective-permute-start(bf16[512,256]{1,0:T(8,128)(2,1)} %get-tuple-element.27.refs_11_), channel_id=1, source_target_pairs={{0,2},{1,0},{2,3},{3,1},{4,6},{5,4},{6,7},{7,5},{8,8},{9,10},{10,9... | collective-permute-start | bytes 786440 | tf_op jit(solution)/shard_map/ppermute | solution.py:238
  55.5 8.5 %collective-permute-start.21 = (bf16[512,256]{1,0:T(8,128)(2,1)}, bf16[512,256]{1,0:T(8,128)(2,1)S(1)}, u32[]{:S(2)}, u32[]{:S(2)}) collective-permute-start(bf16[512,256]{1,0:T(8,128)(2,1)} %get-tuple-element.42), channel_id=1, source_target_pairs={{0,8},{8,0},{16,24},{24,16},{1,9},{9,1},{17,25},{25,17},{2,10},{10... | collective-permute-start | bytes 786440 | tf_op jit(solution)/shard_map/ppermute | solution.py:241
  55.7 25.4 %collective-permute-start.11 = (f32[2,512,256]{2,1,0:T(8,128)}, f32[2,512,256]{2,1,0:T(8,128)S(1)}, u32[]{:S(2)}, u32[]{:S(2)}) collective-permute-start(f32[2,512,256]{2,1,0:T(8,128)} %get-tuple-element.31), channel_id=1, source_target_pairs={{0,1},{1,0},{2,3},{3,2},{4,5},{5,4},{6,7},{7,6},{8,9},{9,8},{10,11... | collective-permute-start | bytes 3145736 | tf_op jit(solution)/shard_map/ppermute | solution.py:200
  57.7 9.4 %collective-permute-start.16 = (bf16[512,256]{1,0:T(8,128)(2,1)}, bf16[512,256]{1,0:T(8,128)(2,1)S(1)}, u32[]{:S(2)}, u32[]{:S(2)}) collective-permute-start(bf16[512,256]{1,0:T(8,128)(2,1)} %get-tuple-element.37), channel_id=1, source_target_pairs={{0,4},{1,6},{2,5},{3,7},{4,0},{5,2},{6,1},{7,3},{8,14},{9,12},{10,... | collective-permute-start | bytes 786440 | tf_op jit(solution)/shard_map/ppermute | solution.py:238
  57.7 14.8 %collective-permute-start.18 = (bf16[512,256]{1,0:T(8,128)(2,1)}, bf16[512,256]{1,0:T(8,128)(2,1)S(1)}, u32[]{:S(2)}, u32[]{:S(2)}) collective-permute-start(bf16[512,256]{1,0:T(8,128)(2,1)} %get-tuple-element.39), channel_id=1, source_target_pairs={{0,6},{1,4},{2,7},{3,5},{4,2},{5,0},{6,3},{7,1},{8,12},{9,14},{10,... | collective-permute-start | bytes 786440 | tf_op jit(solution)/shard_map/ppermute | solution.py:238
  60.4 14.9 %collective-permute-start.20 = (bf16[512,256]{1,0:T(8,128)(2,1)S(1)}, bf16[512,256]{1,0:T(8,128)(2,1)S(1)}, u32[]{:S(2)}, u32[]{:S(2)}) collective-permute-start(bf16[512,256]{1,0:T(8,128)(2,1)S(1)} %add_convert_fusion.2), channel_id=1, source_target_pairs={{0,1},{1,3},{2,0},{3,2},{4,5},{5,7},{6,4},{7,6},{8,11},{9,9},{10,1... | collective-permute-start | bytes 786440 | tf_op jit(solution)/shard_map/ppermute | solution.py:238
  65.0 13.3 %collective-permute-start.22 = (bf16[512,256]{1,0:T(8,128)(2,1)S(1)}, bf16[512,256]{1,0:T(8,128)(2,1)S(1)}, u32[]{:S(2)}, u32[]{:S(2)}) collective-permute-start(bf16[512,256]{1,0:T(8,128)(2,1)S(1)} %add_convert_fusion.1), channel_id=1, source_target_pairs={{0,5},{1,7},{2,4},{3,6},{4,1},{5,3},{6,0},{7,2},{8,15},{9,13},{10,... | collective-permute-start | bytes 786440 | tf_op jit(solution)/shard_map/ppermute | solution.py:238
  67.2 15.5 %collective-permute-start.17 = (bf16[512,256]{1,0:T(8,128)(2,1)S(1)}, bf16[512,256]{1,0:T(8,128)(2,1)S(1)}, u32[]{:S(2)}, u32[]{:S(2)}) collective-permute-start(bf16[512,256]{1,0:T(8,128)(2,1)S(1)} %add_convert_fusion.4), channel_id=1, source_target_pairs={{0,0},{1,17},{2,10},{3,27},{4,4},{5,21},{6,14},{7,31},{8,8},{9,25}... | collective-permute-start | bytes 786440 | tf_op jit(solution)/shard_map/ppermute | solution.py:288
  72.5 11.7 %collective-permute-start.19 = (bf16[512,256]{1,0:T(8,128)(2,1)S(1)}, bf16[512,256]{1,0:T(8,128)(2,1)S(1)}, u32[]{:S(2)}, u32[]{:S(2)}) collective-permute-start(bf16[512,256]{1,0:T(8,128)(2,1)S(1)} %add_convert_fusion.3), channel_id=1, source_target_pairs={{0,8},{1,25},{2,2},{3,19},{4,12},{5,29},{6,6},{7,23},{8,0},{9,17},... | collective-permute-start | bytes 786440 | tf_op jit(solution)/shard_map/ppermute | solution.py:288
  79.1 12.3 %collective-permute-start.23 = (bf16[512,256]{1,0:T(8,128)(2,1)}, bf16[512,256]{1,0:T(8,128)(2,1)}, u32[]{:S(2)}, u32[]{:S(2)}) collective-permute-start(bf16[512,256]{1,0:T(8,128)(2,1)} %add_convert_fusion), channel_id=1, source_target_pairs={{0,16},{1,1},{2,26},{3,11},{4,20},{5,5},{6,30},{7,15},{8,24},{9,9}... | collective-permute-start | bytes 786440 | tf_op jit(solution)/shard_map/ppermute | solution.py:288
  81.3 10.2 %collective-permute-start.12 = (bf16[1,512,256]{2,1,0:T(8,128)(2,1)S(1)}, bf16[1,512,256]{2,1,0:T(8,128)(2,1)S(1)}, u32[]{:S(2)}, u32[]{:S(2)}) collective-permute-start(bf16[1,512,256]{2,1,0:T(8,128)(2,1)S(1)} %dynamic-slice_convert_fusion), channel_id=1, source_target_pairs={{0,2},{1,3},{2,0},{3,1},{4,6},{5,7},{6,4},{7,5},{8,10},{9,11},{10,... | collective-permute-start | bytes 786440 | tf_op jit(solution)/shard_map/ppermute | solution.py:200
  (14 other events, 132.7 us)

commit v5 on v4

--- a/solution.py
+++ b/solution.py
@@ -29,16 +29,15 @@
     return out
 
 
-def slots_kernel(first, last, late, n_wait, n_col, ratio, scalars, coords, cores_hbm, *refs):
+def slots_kernel(first, last, n_col, ratio, scalars, coords, cores_hbm, *refs):
     n_x = last - first
-    opens, closes = first == 0, last == ratio and late != 1
-    parts = [d for d in range(n_col) if late is None or d // 2 % 2 == late]
+    opens, closes = first == 0, last == ratio
+    parts = [*range(n_col)]
     src_refs, refs = refs[:n_col], refs[n_col:]
     tgt_refs, refs = refs[: len(parts) * n_x], refs[len(parts) * n_x :]
     tiles_hbm, refs = refs[0], refs[1:]
     if not opens:
         gs_in, refs = refs[0], refs[1:]
-    refs = refs[n_wait:]
     gt_outs, refs = refs[: len(parts) * n_x], refs[len(parts) * n_x :]
     gs_outs, refs = (refs[:2], refs[2:]) if closes else (refs[:1], refs[1:])
     cores, src, tgt, tiles, resids, left, right, gs_acc, gt_acc, slot_of, tgt_of, tile_sems, sems = refs
@@ -72,9 +71,6 @@
         step = lax.rem(x_pos - b // src_tiles + ratio, ratio)
         place = lax.rem(b, src_tiles)
         taken = (step >= first) & (step < last)
-        if late is not None:
-            part = mirror(place * tile // rows, n_col) ^ plane ^ col_pos
-            taken = taken & ((part // 2) % 2 == late)
         slot_of[count] = s
         tgt_of[count] = (step - first) * src_tiles + place
 
@@ -156,7 +152,7 @@
 
 
 def run_slots(
-    first, last, late, n_col, ratio, scalars, coords, cores, src_parts, tgt_parts, tiles, carried, wait=()
+    first, last, n_col, ratio, scalars, coords, cores, src_parts, tgt_parts, tiles, carried
 ):
     rows, rank = src_parts[0].shape
     cap, tile = tiles.shape[0], tiles.shape[1]
@@ -165,13 +161,13 @@
     smem_spec = pl.BlockSpec(memory_space=pltpu.SMEM)
     n_out = len(tgt_parts)
     outs = [jax.ShapeDtypeStruct((rows, rank), jnp.bfloat16)] * n_out
-    if last == ratio and late != 1:
+    if last == ratio:
         outs += [jax.ShapeDtypeStruct((n_col // 2, rows, rank), jnp.float32)] * 2
     else:
         outs += [jax.ShapeDtypeStruct((block, rank), jnp.float32)]
-    operands = [scalars, coords, cores, *src_parts, *tgt_parts, tiles, *carried, *wait]
+    operands = [scalars, coords, cores, *src_parts, *tgt_parts, tiles, *carried]
     outs = pl.pallas_call(
-        functools.partial(slots_kernel, first, last, late, len(wait), n_col, ratio),
+        functools.partial(slots_kernel, first, last, n_col, ratio),
         out_shape=outs,
         in_specs=[smem_spec, smem_spec] + [any_spec] * (len(operands) - 2),
         out_specs=[any_spec] * len(outs),
@@ -242,13 +238,13 @@
 
     halving = [d for d in range(n_col) if d // 2 % 2 == 1]
     direct = [d for d in range(n_col) if d // 2 % 2 == 0]
-    own_grad, src_grad = run_slots(0, 1, None, *fixed, [own[d] for d in range(n_col)], tiles, [])
+    own_grad, src_grad = run_slots(0, 1, *fixed, [own[d] for d in range(n_col)], tiles, [])
     came = {d: [to_pair(own_grad[d + 1])] for d in halving[::2]}
     arrived = {d: [to_owner(own_grad[d], d, 0)] for d in direct}
     grads = {d: [own_grad[d]] for d in range(n_col)}
     if ratio > 1:
         held = [v for d in range(n_col) for v in cross[d]]
-        target, src_grad = run_slots(1, ratio, None, *fixed, held, tiles, src_grad, own_grad)
+        target, src_grad = run_slots(1, ratio, *fixed, held, tiles, src_grad)
         target = {d: target[d * (ratio - 1) : (d + 1) * (ratio - 1)] for d in range(n_col)}
         target, came, arrived = lax.optimization_barrier((target, came, arrived))
         for d in range(n_col):

time: 94.3 us -> 91 us (0.965)
  waiting for transfers between devices: 21.4 us -> 18 us
  starting transfers between devices: 51.4 us -> 53.4 us
  Pallas kernels: 13.4 us -> 12 us
    ppermute x2, starting transfers between devices: 6.38 us -> 12.4 us  [to_pair(): return lax.ppermute(value, 'zz', [(p, p ^ 1) for p in range(planes)])]
    ppermute x6, starting transfers between devices: 12.3 us -> 9.19 us  [to_owner(): lax.ppermute(value, AXES, part_pairs(d, lambda p, x, j, q: (p, (x - t) %...]
    ppermute x5, starting transfers between devices: 11.4 us -> 8.66 us  [swap(): return lax.ppermute(value, 'col', [(i, i ^ bit) for i in range(n_col)])]
    ppermute x3, waiting for transfers between devices: 8.75 us -> 6.79 us  [local(): landed.append(lax.ppermute(term, AXES, pairs))]
    ppermute x6, waiting for transfers between devices: 9.54 us -> 7.89 us  [to_owner(): lax.ppermute(value, AXES, part_pairs(d, lambda p, x, j, q: (p, (x - t) %...]
    pallas_call x2, Pallas kernels: 13.4 us -> 12 us  [run_slots(): pl.pallas_call(functools.partial(slots_kernel, first, last, n_col, ratio)...]
    ppermute x4, starting transfers between devices: 10.9 us -> 11.9 us  [local(): own[d] = lax.ppermute(factors, AXES, [(b, a) for a, b in pairs])]
  transfers between devices with their start and end apart: 24 -> 24, of which waited for: 7 -> 7; matrix products, arithmetic and copies ran while one was open for 3% -> 3% of each run, Pallas kernels for 14% -> 13%
where the time goes in v5:
time: 91 us; the launch traced here: 90.6 us
  starting transfers between devices  53.4 us (59%)
  waiting for transfers between devices  18 us (20%)
  Pallas kernels  12 us (13%)
  other arithmetic  4.68 us (5%)
  local copies, waits for them, and re-layouts  1.51 us (2%)
  between operations  0.96 us (1%)
    ppermute x2, starting transfers between devices, to_pair(): return lax.ppermute(value, 'zz', [(p, p ^ 1) for p in range(planes)])  12.4 us
    pallas_call x2, Pallas kernels, run_slots(): pl.pallas_call(functools.partial(slots_kernel, first, last, n_col, ratio)...  12 us
    ppermute x4, starting transfers between devices, local(): own[d] = lax.ppermute(factors, AXES, [(b, a) for a, b in pairs])  11.9 us
    ppermute x6, starting transfers between devices, to_owner(): lax.ppermute(value, AXES, part_pairs(d, lambda p, x, j, q: (p, (x - t) %...  9.19 us
    ppermute x5, starting transfers between devices, swap(): return lax.ppermute(value, 'col', [(i, i ^ bit) for i in range(n_col)])  8.66 us
    ppermute x6, waiting for transfers between devices, to_owner(): lax.ppermute(value, AXES, part_pairs(d, lambda p, x, j, q: (p, (x - t) %...  7.89 us
    ppermute x3, waiting for transfers between devices, local(): landed.append(lax.ppermute(term, AXES, pairs))  6.79 us
    ppermute x3, starting transfers between devices, local(): landed.append(lax.ppermute(term, AXES, pairs))  6.22 us
  transfers between devices with their start and end apart: 24, of which 7 were waited for; matrix products, arithmetic and copies ran while one was open for 3% of the time, Pallas kernels for 13%

profile of v5, /device:TPU:0, one launch (start us, length us, event | category | flops | bytes accessed | tf_op | source)
XLA Modules:
  0.0 90.6 jit_solution(15256639983435404435)
XLA Ops:
  0.0 3.0 %collective-permute-start.1 = (bf16[512,256]{1,0:T(8,128)(2,1)}, bf16[512,256]{1,0:T(8,128)(2,1)S(1)}, u32[]{:S(2)}, u32[]{:S(2)}) collective-permute-start(bf16[512,256]{1,0:T(8,128)(2,1)} %refs_0_.3), channel_id=1, source_target_pairs={{0,2},{1,3},{2,0},{3,1},{4,6},{5,7},{6,4},{7,5},{8,10},{9,11},{10,... | collective-permute-start | bytes 786440 | tf_op jit(solution)/shard_map/ppermute | solution.py:196
  3.0 1.6 %collective-permute-start.2 = (bf16[512,256]{1,0:T(8,128)(2,1)}, bf16[512,256]{1,0:T(8,128)(2,1)S(1)}, u32[]{:S(2)}, u32[]{:S(2)}) collective-permute-start(bf16[512,256]{1,0:T(8,128)(2,1)} %refs_0_.3), channel_id=1, source_target_pairs={{0,0},{10,1},{17,2},{27,3},{4,4},{14,5},{21,6},{31,7},{2,8},{8,9},... | collective-permute-start | bytes 786440 | tf_op jit(solution)/shard_map/ppermute | solution.py:217
  4.6 3.1 %collective-permute-start = (bf16[512,256]{1,0:T(8,128)(2,1)}, bf16[512,256]{1,0:T(8,128)(2,1)S(1)}, u32[]{:S(2)}, u32[]{:S(2)}) collective-permute-start(bf16[512,256]{1,0:T(8,128)(2,1)} %refs_0_.3), channel_id=1, source_target_pairs={{0,1},{1,0},{2,3},{3,2},{4,5},{5,4},{6,7},{7,6},{8,9},{9,8},{10,11... | collective-permute-start | bytes 786440 | tf_op jit(solution)/shard_map/ppermute | solution.py:196
  7.6 2.6 %collective-permute-start.5 = (bf16[512,256]{1,0:T(8,128)(2,1)}, bf16[512,256]{1,0:T(8,128)(2,1)S(1)}, u32[]{:S(2)}, u32[]{:S(2)}) collective-permute-start(bf16[512,256]{1,0:T(8,128)(2,1)} %refs_0_.3), channel_id=1, source_target_pairs={{2,0},{8,1},{19,2},{25,3},{6,4},{12,5},{23,6},{29,7},{0,8},{10,9},... | collective-permute-start | bytes 786440 | tf_op jit(solution)/shard_map/ppermute | solution.py:217
  10.3 2.6 %collective-permute-start.7 = (bf16[512,256]{1,0:T(8,128)(2,1)}, bf16[512,256]{1,0:T(8,128)(2,1)S(1)}, u32[]{:S(2)}, u32[]{:S(2)}) collective-permute-start(bf16[512,256]{1,0:T(8,128)(2,1)} %refs_0_.3), channel_id=1, source_target_pairs={{1,0},{11,1},{16,2},{26,3},{5,4},{15,5},{20,6},{30,7},{3,8},{9,9},... | collective-permute-start | bytes 786440 | tf_op jit(solution)/shard_map/ppermute | solution.py:217
  12.9 5.0 %collective-permute-start.9 = (bf16[512,256]{1,0:T(8,128)(2,1)}, bf16[512,256]{1,0:T(8,128)(2,1)S(1)}, u32[]{:S(2)}, u32[]{:S(2)}) collective-permute-start(bf16[512,256]{1,0:T(8,128)(2,1)} %refs_0_.3), channel_id=1, source_target_pairs={{3,0},{9,1},{18,2},{24,3},{7,4},{13,5},{22,6},{28,7},{1,8},{11,9},... | collective-permute-start | bytes 786440 | tf_op jit(solution)/shard_map/ppermute | solution.py:217
  19.3 1.5 %collective-permute-start.4 = (bf16[512,256]{1,0:T(8,128)(2,1)S(1)}, bf16[512,256]{1,0:T(8,128)(2,1)S(1)}, u32[]{:S(2)}, u32[]{:S(2)}) collective-permute-start(bf16[512,256]{1,0:T(8,128)(2,1)S(1)} %collective-permute-done.2.refs_4_), channel_id=1, source_target_pairs={{0,4},{4,0},{1,5},{5,1},{2,6},{6,2},{3,7},{7,3},{8,12},{12,8},{9,1... | collective-permute-start | bytes 786440 | tf_op jit(solution)/shard_map/ppermute | solution.py:228
  22.6 1.5 %collective-permute-start.8 = (bf16[512,256]{1,0:T(8,128)(2,1)S(1)}, bf16[512,256]{1,0:T(8,128)(2,1)S(1)}, u32[]{:S(2)}, u32[]{:S(2)}) collective-permute-start(bf16[512,256]{1,0:T(8,128)(2,1)S(1)} %collective-permute-done.7.refs_6_), channel_id=1, source_target_pairs={{0,4},{4,0},{1,5},{5,1},{2,6},{6,2},{3,7},{7,3},{8,12},{12,8},{9,1... | collective-permute-start | bytes 786440 | tf_op jit(solution)/shard_map/ppermute | solution.py:228
  25.1 1.5 %collective-permute-start.10 = (bf16[512,256]{1,0:T(8,128)(2,1)S(1)}, bf16[512,256]{1,0:T(8,128)(2,1)S(1)}, u32[]{:S(2)}, u32[]{:S(2)}) collective-permute-start(bf16[512,256]{1,0:T(8,128)(2,1)S(1)} %collective-permute-done.9.refs_7_), channel_id=1, source_target_pairs={{0,4},{4,0},{1,5},{5,1},{2,6},{6,2},{3,7},{7,3},{8,12},{12,8},{9,1... | collective-permute-start | bytes 786440 | tf_op jit(solution)/shard_map/ppermute | solution.py:228
  27.3 6.6 %shard_map.55 = (bf16[512,256]{1,0:T(8,128)(2,1)}, bf16[512,256]{1,0:T(8,128)(2,1)}, bf16[512,256]{1,0:T(8,128)(2,1)}, bf16[512,256]{1,0:T(8,128)(2,1)}, f32[2048,256]{1,0:T(8,128)}) custom-call(s32[4]{0:T(128)} %pad_add_fusion.scalars, s32[3,32]{1,0:T(4,128)} %bitcast.10, bf16[8,256,256]{2,1,0:T(8,128)(2,1)} %cores_hbm.3, bf16[512,256]{1,0:T(8,128)(2,1)} %refs_0_.3, ...), custom_call_target="tpu_custom_call" | custom-call | tf_op jit(solution)/shard_map/pallas_call | solution.py:169
  33.9 8.4 %collective-permute-start.13 = (bf16[512,256]{1,0:T(8,128)(2,1)}, bf16[512,256]{1,0:T(8,128)(2,1)S(1)}, u32[]{:S(2)}, u32[]{:S(2)}) collective-permute-start(bf16[512,256]{1,0:T(8,128)(2,1)} %get-tuple-element.32), channel_id=1, source_target_pairs={{0,8},{8,0},{16,24},{24,16},{1,9},{9,1},{17,25},{25,17},{2,10},{10... | collective-permute-start | bytes 786440 | tf_op jit(solution)/shard_map/ppermute | solution.py:237
  42.3 1.6 %collective-permute-start.14 = (bf16[512,256]{1,0:T(8,128)(2,1)}, bf16[512,256]{1,0:T(8,128)(2,1)S(1)}, u32[]{:S(2)}, u32[]{:S(2)}) collective-permute-start(bf16[512,256]{1,0:T(8,128)(2,1)} %get-tuple-element.33), channel_id=1, source_target_pairs={{0,0},{1,2},{2,1},{3,3},{4,4},{5,6},{6,5},{7,7},{8,10},{9,8},{10,1... | collective-permute-start | bytes 786440 | tf_op jit(solution)/shard_map/ppermute | solution.py:234
  43.9 2.2 %collective-permute-start.15 = (bf16[512,256]{1,0:T(8,128)(2,1)}, bf16[512,256]{1,0:T(8,128)(2,1)S(1)}, u32[]{:S(2)}, u32[]{:S(2)}) collective-permute-start(bf16[512,256]{1,0:T(8,128)(2,1)} %get-tuple-element.34), channel_id=1, source_target_pairs={{0,2},{1,0},{2,3},{3,1},{4,6},{5,4},{6,7},{7,5},{8,8},{9,10},{10,9... | collective-permute-start | bytes 786440 | tf_op jit(solution)/shard_map/ppermute | solution.py:234
  46.9 5.5 %shard_map.56 = (bf16[512,256]{1,0:T(8,128)(2,1)}, bf16[512,256]{1,0:T(8,128)(2,1)}, bf16[512,256]{1,0:T(8,128)(2,1)}, bf16[512,256]{1,0:T(8,128)(2,1)}, f32[2,512,256]{2,1,0:T(8,128)}, /*index=5*/f32[2,512,256]{2,1,0:T(8,128)}) custom-call(s32[4]{0:T(128)} %pad_add_fusion.scalars, s32[3,32]{1,0:T(4,128)} %bitcast.11, bf16[8,256,256]{2,1,0:T(8,128)(2,1)} %cores_hbm.3, ...), custom_call_target="tpu_custom_call" | custom-call | tf_op jit(solution)/shard_map/pallas_call | solution.py:169
  52.5 4.0 %collective-permute-start.21 = (bf16[512,256]{1,0:T(8,128)(2,1)}, bf16[512,256]{1,0:T(8,128)(2,1)S(1)}, u32[]{:S(2)}, u32[]{:S(2)}) collective-permute-start(bf16[512,256]{1,0:T(8,128)(2,1)} %get-tuple-element.42), channel_id=1, source_target_pairs={{0,8},{8,0},{16,24},{24,16},{1,9},{9,1},{17,25},{25,17},{2,10},{10... | collective-permute-start | bytes 786440 | tf_op jit(solution)/shard_map/ppermute | solution.py:237
  57.1 2.4 %collective-permute-start.20 = (bf16[512,256]{1,0:T(8,128)(2,1)S(1)}, bf16[512,256]{1,0:T(8,128)(2,1)S(1)}, u32[]{:S(2)}, u32[]{:S(2)}) collective-permute-start(bf16[512,256]{1,0:T(8,128)(2,1)S(1)} %add_convert_fusion.2), channel_id=1, source_target_pairs={{0,1},{1,3},{2,0},{3,2},{4,5},{5,7},{6,4},{7,6},{8,11},{9,9},{10,1... | collective-permute-start | bytes 786440 | tf_op jit(solution)/shard_map/ppermute | solution.py:234
  60.6 1.9 %collective-permute-done.21 = bf16[512,256]{1,0:T(8,128)(2,1)S(1)} collective-permute-done((bf16[512,256]{1,0:T(8,128)(2,1)}, bf16[512,256]{1,0:T(8,128)(2,1)S(1)}, u32[]{:S(2)}, u32[]{:S(2)}) %collective-permute-start.21) | collective-permute-done | bytes 262176 | tf_op jit(solution)/shard_map/ppermute | solution.py:237
  65.2 2.7 %collective-permute-start.19 = (bf16[512,256]{1,0:T(8,128)(2,1)S(1)}, bf16[512,256]{1,0:T(8,128)(2,1)S(1)}, u32[]{:S(2)}, u32[]{:S(2)}) collective-permute-start(bf16[512,256]{1,0:T(8,128)(2,1)S(1)} %add_convert_fusion.3), channel_id=1, source_target_pairs={{0,8},{1,25},{2,2},{3,19},{4,12},{5,29},{6,6},{7,23},{8,0},{9,17},... | collective-permute-start | bytes 786440 | tf_op jit(solution)/shard_map/ppermute | solution.py:284
  67.9 2.2 %collective-permute-done.16 = bf16[512,256]{1,0:T(8,128)(2,1)S(1)} collective-permute-done((bf16[512,256]{1,0:T(8,128)(2,1)}, bf16[512,256]{1,0:T(8,128)(2,1)S(1)}, u32[]{:S(2)}, u32[]{:S(2)}) %collective-permute-start.16) | collective-permute-done | bytes 262176 | tf_op jit(solution)/shard_map/ppermute | solution.py:234
  70.8 5.3 %collective-permute-done.22 = bf16[512,256]{1,0:T(8,128)(2,1)S(1)} collective-permute-done((bf16[512,256]{1,0:T(8,128)(2,1)S(1)}, bf16[512,256]{1,0:T(8,128)(2,1)S(1)}, u32[]{:S(2)}, u32[]{:S(2)}) %collective-permute-start.22) | collective-permute-done | bytes 262176 | tf_op jit(solution)/shard_map/ppermute | solution.py:234
  77.0 2.9 %collective-permute-start.23 = (bf16[512,256]{1,0:T(8,128)(2,1)}, bf16[512,256]{1,0:T(8,128)(2,1)}, u32[]{:S(2)}, u32[]{:S(2)}) collective-permute-start(bf16[512,256]{1,0:T(8,128)(2,1)} %add_convert_fusion), channel_id=1, source_target_pairs={{0,16},{1,1},{2,26},{3,11},{4,20},{5,5},{6,30},{7,15},{8,24},{9,9}... | collective-permute-start | bytes 786440 | tf_op jit(solution)/shard_map/ppermute | solution.py:284
  80.1 1.4 %collective-permute-start.12 = (bf16[1,512,256]{2,1,0:T(8,128)(2,1)S(1)}, bf16[1,512,256]{2,1,0:T(8,128)(2,1)S(1)}, u32[]{:S(2)}, u32[]{:S(2)}) collective-permute-start(bf16[1,512,256]{2,1,0:T(8,128)(2,1)S(1)} %dynamic-slice_convert_fusion), channel_id=1, source_target_pairs={{0,2},{1,3},{2,0},{3,1},{4,6},{5,7},{6,4},{7,5},{8,10},{9,11},{10,... | collective-permute-start | bytes 786440 | tf_op jit(solution)/shard_map/ppermute | solution.py:196
  81.4 6.8 %collective-permute-done.23 = bf16[512,256]{1,0:T(8,128)(2,1)} collective-permute-done((bf16[512,256]{1,0:T(8,128)(2,1)}, bf16[512,256]{1,0:T(8,128)(2,1)}, u32[]{:S(2)}, u32[]{:S(2)}) %collective-permute-start.23) | collective-permute-done | bytes 262176 | tf_op jit(solution)/shard_map/ppermute | solution.py:284
  88.6 1.9 %fusion.1 = f32[512,256]{1,0:T(8,128)} fusion(bf16[512,256]{1,0:T(8,128)(2,1)} %collective-permute-done.23, bf16[512,256]{1,0:T(8,128)(2,1)S(1)} %collective-permute-done.19, bf16[512,256]{1,0:T(8,128)(2,1)S(1)} %collective-permute-done.17, bf16[1,512,256]{2,1,0:T(8,128)(2,1)S(1)} %collective-permute-done.12, f32[2,512,256]{2,1,0:T(8,128)S(1)} %add.43, ...), kind=kLoop, calls=%fused_computation.2 | loop fusion | flops 1441792 | bytes 2359300 | tf_op jit(solution)/shard_map/sub | solution.py:286
  (63 shorter events, 11.5 us)
Async XLA Ops:
  0.0 12.9 %collective-permute-start.1 = (bf16[512,256]{1,0:T(8,128)(2,1)}, bf16[512,256]{1,0:T(8,128)(2,1)S(1)}, u32[]{:S(2)}, u32[]{:S(2)}) collective-permute-start(bf16[512,256]{1,0:T(8,128)(2,1)} %refs_0_.3), channel_id=1, source_target_pairs={{0,2},{1,3},{2,0},{3,1},{4,6},{5,7},{6,4},{7,5},{8,10},{9,11},{10,... | collective-permute-start | bytes 786440 | tf_op jit(solution)/shard_map/ppermute | solution.py:196
  3.0 15.0 %collective-permute-start.2 = (bf16[512,256]{1,0:T(8,128)(2,1)}, bf16[512,256]{1,0:T(8,128)(2,1)S(1)}, u32[]{:S(2)}, u32[]{:S(2)}) collective-permute-start(bf16[512,256]{1,0:T(8,128)(2,1)} %refs_0_.3), channel_id=1, source_target_pairs={{0,0},{10,1},{17,2},{27,3},{4,4},{14,5},{21,6},{31,7},{2,8},{8,9},... | collective-permute-start | bytes 786440 | tf_op jit(solution)/shard_map/ppermute | solution.py:217
  4.6 14.7 %collective-permute-start = (bf16[512,256]{1,0:T(8,128)(2,1)}, bf16[512,256]{1,0:T(8,128)(2,1)S(1)}, u32[]{:S(2)}, u32[]{:S(2)}) collective-permute-start(bf16[512,256]{1,0:T(8,128)(2,1)} %refs_0_.3), channel_id=1, source_target_pairs={{0,1},{1,0},{2,3},{3,2},{4,5},{5,4},{6,7},{7,6},{8,9},{9,8},{10,11... | collective-permute-start | bytes 786440 | tf_op jit(solution)/shard_map/ppermute | solution.py:196
  7.6 13.1 %collective-permute-start.5 = (bf16[512,256]{1,0:T(8,128)(2,1)}, bf16[512,256]{1,0:T(8,128)(2,1)S(1)}, u32[]{:S(2)}, u32[]{:S(2)}) collective-permute-start(bf16[512,256]{1,0:T(8,128)(2,1)} %refs_0_.3), channel_id=1, source_target_pairs={{2,0},{8,1},{19,2},{25,3},{6,4},{12,5},{23,6},{29,7},{0,8},{10,9},... | collective-permute-start | bytes 786440 | tf_op jit(solution)/shard_map/ppermute | solution.py:217
  10.3 12.3 %collective-permute-start.7 = (bf16[512,256]{1,0:T(8,128)(2,1)}, bf16[512,256]{1,0:T(8,128)(2,1)S(1)}, u32[]{:S(2)}, u32[]{:S(2)}) collective-permute-start(bf16[512,256]{1,0:T(8,128)(2,1)} %refs_0_.3), channel_id=1, source_target_pairs={{1,0},{11,1},{16,2},{26,3},{5,4},{15,5},{20,6},{30,7},{3,8},{9,9},... | collective-permute-start | bytes 786440 | tf_op jit(solution)/shard_map/ppermute | solution.py:217
  12.9 12.2 %collective-permute-start.9 = (bf16[512,256]{1,0:T(8,128)(2,1)}, bf16[512,256]{1,0:T(8,128)(2,1)S(1)}, u32[]{:S(2)}, u32[]{:S(2)}) collective-permute-start(bf16[512,256]{1,0:T(8,128)(2,1)} %refs_0_.3), channel_id=1, source_target_pairs={{3,0},{9,1},{18,2},{24,3},{7,4},{13,5},{22,6},{28,7},{1,8},{11,9},... | collective-permute-start | bytes 786440 | tf_op jit(solution)/shard_map/ppermute | solution.py:217
  18.0 8.6 %collective-permute-start.3 = (bf16[512,256]{1,0:T(8,128)(2,1)S(1)}, bf16[512,256]{1,0:T(8,128)(2,1)S(1)}, u32[]{:S(2)}, u32[]{:S(2)}) collective-permute-start(bf16[512,256]{1,0:T(8,128)(2,1)S(1)} %collective-permute-done.1.refs_2_), channel_id=1, source_target_pairs={{0,1},{1,0},{2,3},{3,2},{4,5},{5,4},{6,7},{7,6},{8,9},{9,8},{10,11... | collective-permute-start | bytes 786440 | tf_op jit(solution)/shard_map/ppermute | solution.py:196
  19.3 23.0 %collective-permute-start.4 = (bf16[512,256]{1,0:T(8,128)(2,1)S(1)}, bf16[512,256]{1,0:T(8,128)(2,1)S(1)}, u32[]{:S(2)}, u32[]{:S(2)}) collective-permute-start(bf16[512,256]{1,0:T(8,128)(2,1)S(1)} %collective-permute-done.2.refs_4_), channel_id=1, source_target_pairs={{0,4},{4,0},{1,5},{5,1},{2,6},{6,2},{3,7},{7,3},{8,12},{12,8},{9,1... | collective-permute-start | bytes 786440 | tf_op jit(solution)/shard_map/ppermute | solution.py:228
  20.8 23.1 %collective-permute-start.6 = (bf16[512,256]{1,0:T(8,128)(2,1)S(1)}, bf16[512,256]{1,0:T(8,128)(2,1)S(1)}, u32[]{:S(2)}, u32[]{:S(2)}) collective-permute-start(bf16[512,256]{1,0:T(8,128)(2,1)S(1)} %collective-permute-done.5.refs_5_), channel_id=1, source_target_pairs={{0,4},{4,0},{1,5},{5,1},{2,6},{6,2},{3,7},{7,3},{8,12},{12,8},{9,1... | collective-permute-start | bytes 786440 | tf_op jit(solution)/shard_map/ppermute | solution.py:228
  22.6 23.5 %collective-permute-start.8 = (bf16[512,256]{1,0:T(8,128)(2,1)S(1)}, bf16[512,256]{1,0:T(8,128)(2,1)S(1)}, u32[]{:S(2)}, u32[]{:S(2)}) collective-permute-start(bf16[512,256]{1,0:T(8,128)(2,1)S(1)} %collective-permute-done.7.refs_6_), channel_id=1, source_target_pairs={{0,4},{4,0},{1,5},{5,1},{2,6},{6,2},{3,7},{7,3},{8,12},{12,8},{9,1... | collective-permute-start | bytes 786440 | tf_op jit(solution)/shard_map/ppermute | solution.py:228
  25.1 21.0 %collective-permute-start.10 = (bf16[512,256]{1,0:T(8,128)(2,1)S(1)}, bf16[512,256]{1,0:T(8,128)(2,1)S(1)}, u32[]{:S(2)}, u32[]{:S(2)}) collective-permute-start(bf16[512,256]{1,0:T(8,128)(2,1)S(1)} %collective-permute-done.9.refs_7_), channel_id=1, source_target_pairs={{0,4},{4,0},{1,5},{5,1},{2,6},{6,2},{3,7},{7,3},{8,12},{12,8},{9,1... | collective-permute-start | bytes 786440 | tf_op jit(solution)/shard_map/ppermute | solution.py:228
  33.9 18.6 %collective-permute-start.13 = (bf16[512,256]{1,0:T(8,128)(2,1)}, bf16[512,256]{1,0:T(8,128)(2,1)S(1)}, u32[]{:S(2)}, u32[]{:S(2)}) collective-permute-start(bf16[512,256]{1,0:T(8,128)(2,1)} %get-tuple-element.32), channel_id=1, source_target_pairs={{0,8},{8,0},{16,24},{24,16},{1,9},{9,1},{17,25},{25,17},{2,10},{10... | collective-permute-start | bytes 786440 | tf_op jit(solution)/shard_map/ppermute | solution.py:237
  42.3 10.1 %collective-permute-start.14 = (bf16[512,256]{1,0:T(8,128)(2,1)}, bf16[512,256]{1,0:T(8,128)(2,1)S(1)}, u32[]{:S(2)}, u32[]{:S(2)}) collective-permute-start(bf16[512,256]{1,0:T(8,128)(2,1)} %get-tuple-element.33), channel_id=1, source_target_pairs={{0,0},{1,2},{2,1},{3,3},{4,4},{5,6},{6,5},{7,7},{8,10},{9,8},{10,1... | collective-permute-start | bytes 786440 | tf_op jit(solution)/shard_map/ppermute | solution.py:234
  43.9 8.5 %collective-permute-start.15 = (bf16[512,256]{1,0:T(8,128)(2,1)}, bf16[512,256]{1,0:T(8,128)(2,1)S(1)}, u32[]{:S(2)}, u32[]{:S(2)}) collective-permute-start(bf16[512,256]{1,0:T(8,128)(2,1)} %get-tuple-element.34), channel_id=1, source_target_pairs={{0,2},{1,0},{2,3},{3,1},{4,6},{5,4},{6,7},{7,5},{8,8},{9,10},{10,9... | collective-permute-start | bytes 786440 | tf_op jit(solution)/shard_map/ppermute | solution.py:234
  52.5 10.0 %collective-permute-start.21 = (bf16[512,256]{1,0:T(8,128)(2,1)}, bf16[512,256]{1,0:T(8,128)(2,1)S(1)}, u32[]{:S(2)}, u32[]{:S(2)}) collective-permute-start(bf16[512,256]{1,0:T(8,128)(2,1)} %get-tuple-element.42), channel_id=1, source_target_pairs={{0,8},{8,0},{16,24},{24,16},{1,9},{9,1},{17,25},{25,17},{2,10},{10... | collective-permute-start | bytes 786440 | tf_op jit(solution)/shard_map/ppermute | solution.py:237
  56.4 23.4 %collective-permute-start.11 = (f32[2,512,256]{2,1,0:T(8,128)}, f32[2,512,256]{2,1,0:T(8,128)S(1)}, u32[]{:S(2)}, u32[]{:S(2)}) collective-permute-start(f32[2,512,256]{2,1,0:T(8,128)} %get-tuple-element.27), channel_id=1, source_target_pairs={{0,1},{1,0},{2,3},{3,2},{4,5},{5,4},{6,7},{7,6},{8,9},{9,8},{10,11... | collective-permute-start | bytes 3145736 | tf_op jit(solution)/shard_map/ppermute | solution.py:196
  56.4 8.7 %collective-permute-start.18 = (bf16[512,256]{1,0:T(8,128)(2,1)}, bf16[512,256]{1,0:T(8,128)(2,1)S(1)}, u32[]{:S(2)}, u32[]{:S(2)}) collective-permute-start(bf16[512,256]{1,0:T(8,128)(2,1)} %get-tuple-element.38), channel_id=1, source_target_pairs={{0,6},{1,4},{2,7},{3,5},{4,2},{5,0},{6,3},{7,1},{8,12},{9,14},{10,... | collective-permute-start | bytes 786440 | tf_op jit(solution)/shard_map/ppermute | solution.py:234
  57.1 13.8 %collective-permute-start.20 = (bf16[512,256]{1,0:T(8,128)(2,1)S(1)}, bf16[512,256]{1,0:T(8,128)(2,1)S(1)}, u32[]{:S(2)}, u32[]{:S(2)}) collective-permute-start(bf16[512,256]{1,0:T(8,128)(2,1)S(1)} %add_convert_fusion.2), channel_id=1, source_target_pairs={{0,1},{1,3},{2,0},{3,2},{4,5},{5,7},{6,4},{7,6},{8,11},{9,9},{10,1... | collective-permute-start | bytes 786440 | tf_op jit(solution)/shard_map/ppermute | solution.py:234
  59.5 10.6 %collective-permute-start.16 = (bf16[512,256]{1,0:T(8,128)(2,1)}, bf16[512,256]{1,0:T(8,128)(2,1)S(1)}, u32[]{:S(2)}, u32[]{:S(2)}) collective-permute-start(bf16[512,256]{1,0:T(8,128)(2,1)} %get-tuple-element.36), channel_id=1, source_target_pairs={{0,4},{1,6},{2,5},{3,7},{4,0},{5,2},{6,1},{7,3},{8,14},{9,12},{10,... | collective-permute-start | bytes 786440 | tf_op jit(solution)/shard_map/ppermute | solution.py:234
  63.5 12.7 %collective-permute-start.22 = (bf16[512,256]{1,0:T(8,128)(2,1)S(1)}, bf16[512,256]{1,0:T(8,128)(2,1)S(1)}, u32[]{:S(2)}, u32[]{:S(2)}) collective-permute-start(bf16[512,256]{1,0:T(8,128)(2,1)S(1)} %add_convert_fusion.1), channel_id=1, source_target_pairs={{0,5},{1,7},{2,4},{3,6},{4,1},{5,3},{6,0},{7,2},{8,15},{9,13},{10,... | collective-permute-start | bytes 786440 | tf_op jit(solution)/shard_map/ppermute | solution.py:234
  65.2 16.2 %collective-permute-start.19 = (bf16[512,256]{1,0:T(8,128)(2,1)S(1)}, bf16[512,256]{1,0:T(8,128)(2,1)S(1)}, u32[]{:S(2)}, u32[]{:S(2)}) collective-permute-start(bf16[512,256]{1,0:T(8,128)(2,1)S(1)} %add_convert_fusion.3), channel_id=1, source_target_pairs={{0,8},{1,25},{2,2},{3,19},{4,12},{5,29},{6,6},{7,23},{8,0},{9,17},... | collective-permute-start | bytes 786440 | tf_op jit(solution)/shard_map/ppermute | solution.py:284
  70.2 11.3 %collective-permute-start.17 = (bf16[512,256]{1,0:T(8,128)(2,1)S(1)}, bf16[512,256]{1,0:T(8,128)(2,1)S(1)}, u32[]{:S(2)}, u32[]{:S(2)}) collective-permute-start(bf16[512,256]{1,0:T(8,128)(2,1)S(1)} %add_convert_fusion.4), channel_id=1, source_target_pairs={{0,0},{1,17},{2,10},{3,27},{4,4},{5,21},{6,14},{7,31},{8,8},{9,25}... | collective-permute-start | bytes 786440 | tf_op jit(solution)/shard_map/ppermute | solution.py:284
  77.0 11.2 %collective-permute-start.23 = (bf16[512,256]{1,0:T(8,128)(2,1)}, bf16[512,256]{1,0:T(8,128)(2,1)}, u32[]{:S(2)}, u32[]{:S(2)}) collective-permute-start(bf16[512,256]{1,0:T(8,128)(2,1)} %add_convert_fusion), channel_id=1, source_target_pairs={{0,16},{1,1},{2,26},{3,11},{4,20},{5,5},{6,30},{7,15},{8,24},{9,9}... | collective-permute-start | bytes 786440 | tf_op jit(solution)/shard_map/ppermute | solution.py:284
  80.1 8.6 %collective-permute-start.12 = (bf16[1,512,256]{2,1,0:T(8,128)(2,1)S(1)}, bf16[1,512,256]{2,1,0:T(8,128)(2,1)S(1)}, u32[]{:S(2)}, u32[]{:S(2)}) collective-permute-start(bf16[1,512,256]{2,1,0:T(8,128)(2,1)S(1)} %dynamic-slice_convert_fusion), channel_id=1, source_target_pairs={{0,2},{1,3},{2,0},{3,1},{4,6},{5,7},{6,4},{7,5},{8,10},{9,11},{10,... | collective-permute-start | bytes 786440 | tf_op jit(solution)/shard_map/ppermute | solution.py:196
  (14 other events, 123.2 us)

commit v6 on v5

--- a/solution.py
+++ b/solution.py
@@ -134,8 +134,10 @@
     if closes:
         for h in range(n_col // 2):
             for n in range(2):
-                at = pl.multiple_of((2 * h + ((col_pos + n) & 1)) * rows, rows)
-                outs.append((gs_acc.at[pl.ds(at, rows)], gs_outs[n].at[h]))
+                at = pl.ds(pl.multiple_of((2 * h + ((col_pos + n) & 1)) * rows, rows), rows)
+                if n == 1:
+                    src[at] = gs_acc[at].astype(src.dtype)
+                outs.append(((src if n else gs_acc).at[at], gs_outs[n].at[h]))
     else:
         outs.append((gs_acc, gs_outs[0]))
     outs = [pltpu.make_async_copy(a, b, sems.at[i]) for i, (a, b) in enumerate(outs)]
@@ -162,7 +164,7 @@
     n_out = len(tgt_parts)
     outs = [jax.ShapeDtypeStruct((rows, rank), jnp.bfloat16)] * n_out
     if last == ratio:
-        outs += [jax.ShapeDtypeStruct((n_col // 2, rows, rank), jnp.float32)] * 2
+        outs += [jax.ShapeDtypeStruct((n_col // 2, rows, rank), kind) for kind in (jnp.float32, jnp.bfloat16)]
     else:
         outs += [jax.ShapeDtypeStruct((block, rank), jnp.float32)]
     operands = [scalars, coords, cores, *src_parts, *tgt_parts, tiles, *carried]
@@ -256,7 +258,7 @@
                 arrived[d].append(to_owner(grads[d][t], d, t))
     src_keep, src_send = src_grad
 
-    src_sum = src_keep + swap(src_send, 1, n_col)
+    src_sum = src_keep + swap(src_send, 1, n_col).astype(jnp.float32)
     bit = 2
     while bit < n_col:
         pairs = src_sum.reshape(src_sum.shape[0] // 2, 2, rows, rank)

time: 91 us -> 91.4 us (level)
  Pallas kernels: 12 us -> 15.1 us
  starting transfers between devices: 53.4 us -> 51.7 us
    ppermute x6, waiting for transfers between devices: 7.89 us -> 3.99 us  [to_owner(): lax.ppermute(value, AXES, part_pairs(d, lambda p, x, j, q: (p, (x - t) %...]
    ppermute x5, waiting for transfers between devices: 0.43 us -> 3.91 us  [swap(): return lax.ppermute(value, 'col', [(i, i ^ bit) for i in range(n_col)])]
    pallas_call x2, Pallas kernels: 12 us -> 15.1 us  [run_slots(): pl.pallas_call(functools.partial(slots_kernel, first, last, n_col, ratio)...]
    ppermute x2, starting transfers between devices: 12.4 us -> 10.2 us  [to_pair(): return lax.ppermute(value, 'zz', [(p, p ^ 1) for p in range(planes)])]
    ppermute x5, starting transfers between devices: 8.66 us -> 10.3 us  [swap(): return lax.ppermute(value, 'col', [(i, i ^ bit) for i in range(n_col)])]
    add x1, other arithmetic: 0.14 us -> 1.33 us  [local(): src_sum = src_keep + swap(src_send, 1, n_col).astype(jnp.float32)]
    sub x1, other arithmetic: 1.93 us -> 0.98 us  [local(): return weight_decay * factors.astype(jnp.float32) - total / tile]
  transfers between devices with their start and end apart: 24 -> 24, of which waited for: 7 -> 6; matrix products, arithmetic and copies ran while one was open for 3% -> 4% of each run, Pallas kernels for 13% -> 17%
where the time goes in v6:
time: 91.4 us; the launch traced here: 91.3 us
  starting transfers between devices  51.7 us (57%)
  waiting for transfers between devices  17.7 us (19%)
  Pallas kernels  15.1 us (17%)
  other arithmetic  4.25 us (5%)
  local copies, waits for them, and re-layouts  1.49 us (2%)
  between operations  0.97 us (1%)
    pallas_call x2, Pallas kernels, run_slots(): pl.pallas_call(functools.partial(slots_kernel, first, last, n_col, ratio)...  15.1 us
    ppermute x4, starting transfers between devices, local(): own[d] = lax.ppermute(factors, AXES, [(b, a) for a, b in pairs])  11.9 us
    ppermute x5, starting transfers between devices, swap(): return lax.ppermute(value, 'col', [(i, i ^ bit) for i in range(n_col)])  10.3 us
    ppermute x2, starting transfers between devices, to_pair(): return lax.ppermute(value, 'zz', [(p, p ^ 1) for p in range(planes)])  10.2 us
    ppermute x6, starting transfers between devices, to_owner(): lax.ppermute(value, AXES, part_pairs(d, lambda p, x, j, q: (p, (x - t) %...  9 us
    ppermute x3, waiting for transfers between devices, local(): landed.append(lax.ppermute(term, AXES, pairs))  6.12 us
    ppermute x3, starting transfers between devices, local(): landed.append(lax.ppermute(term, AXES, pairs))  5.37 us
    ppermute x4, starting transfers between devices, local(): lax.ppermute(own[d], 'xx', [(x, (x + s) % ratio) for x in range(ratio)])  5.01 us
  transfers between devices with their start and end apart: 24, of which 6 were waited for; matrix products, arithmetic and copies ran while one was open for 4% of the time, Pallas kernels for 17%

profile of v6, /device:TPU:0, one launch (start us, length us, event | category | flops | bytes accessed | tf_op | source)
XLA Modules:
  0.0 91.3 jit_solution(1684235084317250897)
XLA Ops:
  0.0 3.0 %collective-permute-start.1 = (bf16[512,256]{1,0:T(8,128)(2,1)}, bf16[512,256]{1,0:T(8,128)(2,1)S(1)}, u32[]{:S(2)}, u32[]{:S(2)}) collective-permute-start(bf16[512,256]{1,0:T(8,128)(2,1)} %refs_0_.3), channel_id=1, source_target_pairs={{0,2},{1,3},{2,0},{3,1},{4,6},{5,7},{6,4},{7,5},{8,10},{9,11},{10,... | collective-permute-start | bytes 786440 | tf_op jit(solution)/shard_map/ppermute | solution.py:198
  3.0 1.6 %collective-permute-start.2 = (bf16[512,256]{1,0:T(8,128)(2,1)}, bf16[512,256]{1,0:T(8,128)(2,1)S(1)}, u32[]{:S(2)}, u32[]{:S(2)}) collective-permute-start(bf16[512,256]{1,0:T(8,128)(2,1)} %refs_0_.3), channel_id=1, source_target_pairs={{0,0},{10,1},{17,2},{27,3},{4,4},{14,5},{21,6},{31,7},{2,8},{8,9},... | collective-permute-start | bytes 786440 | tf_op jit(solution)/shard_map/ppermute | solution.py:219
  4.6 3.1 %collective-permute-start = (bf16[512,256]{1,0:T(8,128)(2,1)}, bf16[512,256]{1,0:T(8,128)(2,1)S(1)}, u32[]{:S(2)}, u32[]{:S(2)}) collective-permute-start(bf16[512,256]{1,0:T(8,128)(2,1)} %refs_0_.3), channel_id=1, source_target_pairs={{0,1},{1,0},{2,3},{3,2},{4,5},{5,4},{6,7},{7,6},{8,9},{9,8},{10,11... | collective-permute-start | bytes 786440 | tf_op jit(solution)/shard_map/ppermute | solution.py:198
  7.6 2.6 %collective-permute-start.5 = (bf16[512,256]{1,0:T(8,128)(2,1)}, bf16[512,256]{1,0:T(8,128)(2,1)S(1)}, u32[]{:S(2)}, u32[]{:S(2)}) collective-permute-start(bf16[512,256]{1,0:T(8,128)(2,1)} %refs_0_.3), channel_id=1, source_target_pairs={{2,0},{8,1},{19,2},{25,3},{6,4},{12,5},{23,6},{29,7},{0,8},{10,9},... | collective-permute-start | bytes 786440 | tf_op jit(solution)/shard_map/ppermute | solution.py:219
  10.3 2.6 %collective-permute-start.7 = (bf16[512,256]{1,0:T(8,128)(2,1)}, bf16[512,256]{1,0:T(8,128)(2,1)S(1)}, u32[]{:S(2)}, u32[]{:S(2)}) collective-permute-start(bf16[512,256]{1,0:T(8,128)(2,1)} %refs_0_.3), channel_id=1, source_target_pairs={{1,0},{11,1},{16,2},{26,3},{5,4},{15,5},{20,6},{30,7},{3,8},{9,9},... | collective-permute-start | bytes 786440 | tf_op jit(solution)/shard_map/ppermute | solution.py:219
  12.9 5.0 %collective-permute-start.9 = (bf16[512,256]{1,0:T(8,128)(2,1)}, bf16[512,256]{1,0:T(8,128)(2,1)S(1)}, u32[]{:S(2)}, u32[]{:S(2)}) collective-permute-start(bf16[512,256]{1,0:T(8,128)(2,1)} %refs_0_.3), channel_id=1, source_target_pairs={{3,0},{9,1},{18,2},{24,3},{7,4},{13,5},{22,6},{28,7},{1,8},{11,9},... | collective-permute-start | bytes 786440 | tf_op jit(solution)/shard_map/ppermute | solution.py:219
  19.3 1.5 %collective-permute-start.4 = (bf16[512,256]{1,0:T(8,128)(2,1)S(1)}, bf16[512,256]{1,0:T(8,128)(2,1)S(1)}, u32[]{:S(2)}, u32[]{:S(2)}) collective-permute-start(bf16[512,256]{1,0:T(8,128)(2,1)S(1)} %collective-permute-done.2.refs_4_), channel_id=1, source_target_pairs={{0,4},{4,0},{1,5},{5,1},{2,6},{6,2},{3,7},{7,3},{8,12},{12,8},{9,1... | collective-permute-start | bytes 786440 | tf_op jit(solution)/shard_map/ppermute | solution.py:230
  22.6 1.5 %collective-permute-start.8 = (bf16[512,256]{1,0:T(8,128)(2,1)S(1)}, bf16[512,256]{1,0:T(8,128)(2,1)S(1)}, u32[]{:S(2)}, u32[]{:S(2)}) collective-permute-start(bf16[512,256]{1,0:T(8,128)(2,1)S(1)} %collective-permute-done.7.refs_6_), channel_id=1, source_target_pairs={{0,4},{4,0},{1,5},{5,1},{2,6},{6,2},{3,7},{7,3},{8,12},{12,8},{9,1... | collective-permute-start | bytes 786440 | tf_op jit(solution)/shard_map/ppermute | solution.py:230
  25.1 1.5 %collective-permute-start.10 = (bf16[512,256]{1,0:T(8,128)(2,1)S(1)}, bf16[512,256]{1,0:T(8,128)(2,1)S(1)}, u32[]{:S(2)}, u32[]{:S(2)}) collective-permute-start(bf16[512,256]{1,0:T(8,128)(2,1)S(1)} %collective-permute-done.9.refs_7_), channel_id=1, source_target_pairs={{0,4},{4,0},{1,5},{5,1},{2,6},{6,2},{3,7},{7,3},{8,12},{12,8},{9,1... | collective-permute-start | bytes 786440 | tf_op jit(solution)/shard_map/ppermute | solution.py:230
  27.3 6.7 %shard_map.55 = (bf16[512,256]{1,0:T(8,128)(2,1)}, bf16[512,256]{1,0:T(8,128)(2,1)}, bf16[512,256]{1,0:T(8,128)(2,1)}, bf16[512,256]{1,0:T(8,128)(2,1)}, f32[2048,256]{1,0:T(8,128)}) custom-call(s32[4]{0:T(128)} %pad_add_fusion.scalars, s32[3,32]{1,0:T(4,128)} %bitcast.10, bf16[8,256,256]{2,1,0:T(8,128)(2,1)} %cores_hbm.3, bf16[512,256]{1,0:T(8,128)(2,1)} %refs_0_.3, ...), custom_call_target="tpu_custom_call" | custom-call | tf_op jit(solution)/shard_map/pallas_call | solution.py:171
  34.0 8.4 %collective-permute-start.13 = (bf16[512,256]{1,0:T(8,128)(2,1)}, bf16[512,256]{1,0:T(8,128)(2,1)S(1)}, u32[]{:S(2)}, u32[]{:S(2)}) collective-permute-start(bf16[512,256]{1,0:T(8,128)(2,1)} %get-tuple-element.32), channel_id=1, source_target_pairs={{0,8},{8,0},{16,24},{24,16},{1,9},{9,1},{17,25},{25,17},{2,10},{10... | collective-permute-start | bytes 786440 | tf_op jit(solution)/shard_map/ppermute | solution.py:239
  42.4 1.6 %collective-permute-start.14 = (bf16[512,256]{1,0:T(8,128)(2,1)}, bf16[512,256]{1,0:T(8,128)(2,1)S(1)}, u32[]{:S(2)}, u32[]{:S(2)}) collective-permute-start(bf16[512,256]{1,0:T(8,128)(2,1)} %get-tuple-element.33), channel_id=1, source_target_pairs={{0,0},{1,2},{2,1},{3,3},{4,4},{5,6},{6,5},{7,7},{8,10},{9,8},{10,1... | collective-permute-start | bytes 786440 | tf_op jit(solution)/shard_map/ppermute | solution.py:236
  44.0 3.2 %collective-permute-start.15 = (bf16[512,256]{1,0:T(8,128)(2,1)}, bf16[512,256]{1,0:T(8,128)(2,1)S(1)}, u32[]{:S(2)}, u32[]{:S(2)}) collective-permute-start(bf16[512,256]{1,0:T(8,128)(2,1)} %get-tuple-element.34), channel_id=1, source_target_pairs={{0,2},{1,0},{2,3},{3,1},{4,6},{5,4},{6,7},{7,5},{8,8},{9,10},{10,9... | collective-permute-start | bytes 786440 | tf_op jit(solution)/shard_map/ppermute | solution.py:236
  48.1 8.5 %shard_map.56 = (bf16[512,256]{1,0:T(8,128)(2,1)}, bf16[512,256]{1,0:T(8,128)(2,1)}, bf16[512,256]{1,0:T(8,128)(2,1)}, bf16[512,256]{1,0:T(8,128)(2,1)}, f32[2,5...) custom-call(s32[4]{0:T(128)} %pad_add_fusion.scalars, s32[3,32]{1,0:T(4,128)} %bitcast.11, bf16[8,256,256]{2,1,0:T(8,128)(2,1)} %cores_hbm.3, ...), custom_call_target="tpu_custom_call" | custom-call | tf_op jit(solution)/shard_map/pallas_call | solution.py:171
  56.6 1.7 %collective-permute-start.21 = (bf16[512,256]{1,0:T(8,128)(2,1)}, bf16[512,256]{1,0:T(8,128)(2,1)S(1)}, u32[]{:S(2)}, u32[]{:S(2)}) collective-permute-start(bf16[512,256]{1,0:T(8,128)(2,1)} %get-tuple-element.42), channel_id=1, source_target_pairs={{0,8},{8,0},{16,24},{24,16},{1,9},{9,1},{17,25},{25,17},{2,10},{10... | collective-permute-start | bytes 786440 | tf_op jit(solution)/shard_map/ppermute | solution.py:239
  59.4 1.9 %collective-permute-start.20 = (bf16[512,256]{1,0:T(8,128)(2,1)S(1)}, bf16[512,256]{1,0:T(8,128)(2,1)S(1)}, u32[]{:S(2)}, u32[]{:S(2)}) collective-permute-start(bf16[512,256]{1,0:T(8,128)(2,1)S(1)} %add_convert_fusion.2), channel_id=1, source_target_pairs={{0,1},{1,3},{2,0},{3,2},{4,5},{5,7},{6,4},{7,6},{8,11},{9,9},{10,1... | collective-permute-start | bytes 786440 | tf_op jit(solution)/shard_map/ppermute | solution.py:236
  62.5 2.7 %collective-permute-done.21 = bf16[512,256]{1,0:T(8,128)(2,1)S(1)} collective-permute-done((bf16[512,256]{1,0:T(8,128)(2,1)}, bf16[512,256]{1,0:T(8,128)(2,1)S(1)}, u32[]{:S(2)}, u32[]{:S(2)}) %collective-permute-start.21) | collective-permute-done | bytes 262176 | tf_op jit(solution)/shard_map/ppermute | solution.py:239
  66.9 2.8 %collective-permute-start.19 = (bf16[512,256]{1,0:T(8,128)(2,1)S(1)}, bf16[512,256]{1,0:T(8,128)(2,1)S(1)}, u32[]{:S(2)}, u32[]{:S(2)}) collective-permute-start(bf16[512,256]{1,0:T(8,128)(2,1)S(1)} %add_convert_fusion.3), channel_id=1, source_target_pairs={{0,8},{1,25},{2,2},{3,19},{4,12},{5,29},{6,6},{7,23},{8,0},{9,17},... | collective-permute-start | bytes 786440 | tf_op jit(solution)/shard_map/ppermute | solution.py:286
  69.7 3.4 %collective-permute-done.16 = bf16[512,256]{1,0:T(8,128)(2,1)S(1)} collective-permute-done((bf16[512,256]{1,0:T(8,128)(2,1)}, bf16[512,256]{1,0:T(8,128)(2,1)S(1)}, u32[]{:S(2)}, u32[]{:S(2)}) %collective-permute-start.16) | collective-permute-done | bytes 262176 | tf_op jit(solution)/shard_map/ppermute | solution.py:236
  73.9 1.3 %convert_add_fusion = f32[2,512,256]{2,1,0:T(8,128)S(1)} fusion(f32[2,512,256]{2,1,0:T(8,128)} %get-tuple-element.26, bf16[2,512,256]{2,1,0:T(8,128)(2,1)S(1)} %collective-permute-done.11), kind=kLoop, calls=%fused_computation | loop fusion | flops 524288 | bytes 2621440 | tf_op jit(solution)/shard_map/add | solution.py:261
  75.3 2.9 %collective-permute-start.12 = (bf16[1,512,256]{2,1,0:T(8,128)(2,1)S(1)}, bf16[1,512,256]{2,1,0:T(8,128)(2,1)S(1)}, u32[]{:S(2)}, u32[]{:S(2)}) collective-permute-start(bf16[1,512,256]{2,1,0:T(8,128)(2,1)S(1)} %dynamic-slice_convert_fusion), channel_id=1, source_target_pairs={{0,2},{1,3},{2,0},{3,1},{4,6},{5,7},{6,4},{7,5},{8,10},{9,11},{10,... | collective-permute-start | bytes 786440 | tf_op jit(solution)/shard_map/ppermute | solution.py:198
  78.3 1.9 %collective-permute-start.23 = (bf16[512,256]{1,0:T(8,128)(2,1)S(1)}, bf16[512,256]{1,0:T(8,128)(2,1)S(1)}, u32[]{:S(2)}, u32[]{:S(2)}) collective-permute-start(bf16[512,256]{1,0:T(8,128)(2,1)S(1)} %add_convert_fusion), channel_id=1, source_target_pairs={{0,16},{1,1},{2,26},{3,11},{4,20},{5,5},{6,30},{7,15},{8,24},{9,9}... | collective-permute-start | bytes 786440 | tf_op jit(solution)/shard_map/ppermute | solution.py:286
  80.3 3.9 %collective-permute-done.12 = bf16[1,512,256]{2,1,0:T(8,128)(2,1)S(1)} collective-permute-done((bf16[1,512,256]{2,1,0:T(8,128)(2,1)S(1)}, bf16[1,512,256]{2,1,0:T(8,128)(2,1)S(1)}, u32[]{:S(2)}, u32[]{:S(2)}) %collective-permute-start.12) | collective-permute-done | bytes 262176 | tf_op jit(solution)/shard_map/ppermute | solution.py:198
  84.2 6.1 %collective-permute-done.23 = bf16[512,256]{1,0:T(8,128)(2,1)S(1)} collective-permute-done((bf16[512,256]{1,0:T(8,128)(2,1)S(1)}, bf16[512,256]{1,0:T(8,128)(2,1)S(1)}, u32[]{:S(2)}, u32[]{:S(2)}) %collective-permute-start.23) | collective-permute-done | bytes 262176 | tf_op jit(solution)/shard_map/ppermute | solution.py:286
  (61 shorter events, 10.7 us)
Async XLA Ops:
  0.0 12.9 %collective-permute-start.1 = (bf16[512,256]{1,0:T(8,128)(2,1)}, bf16[512,256]{1,0:T(8,128)(2,1)S(1)}, u32[]{:S(2)}, u32[]{:S(2)}) collective-permute-start(bf16[512,256]{1,0:T(8,128)(2,1)} %refs_0_.3), channel_id=1, source_target_pairs={{0,2},{1,3},{2,0},{3,1},{4,6},{5,7},{6,4},{7,5},{8,10},{9,11},{10,... | collective-permute-start | bytes 786440 | tf_op jit(solution)/shard_map/ppermute | solution.py:198
  3.0 15.0 %collective-permute-start.2 = (bf16[512,256]{1,0:T(8,128)(2,1)}, bf16[512,256]{1,0:T(8,128)(2,1)S(1)}, u32[]{:S(2)}, u32[]{:S(2)}) collective-permute-start(bf16[512,256]{1,0:T(8,128)(2,1)} %refs_0_.3), channel_id=1, source_target_pairs={{0,0},{10,1},{17,2},{27,3},{4,4},{14,5},{21,6},{31,7},{2,8},{8,9},... | collective-permute-start | bytes 786440 | tf_op jit(solution)/shard_map/ppermute | solution.py:219
  4.6 14.7 %collective-permute-start = (bf16[512,256]{1,0:T(8,128)(2,1)}, bf16[512,256]{1,0:T(8,128)(2,1)S(1)}, u32[]{:S(2)}, u32[]{:S(2)}) collective-permute-start(bf16[512,256]{1,0:T(8,128)(2,1)} %refs_0_.3), channel_id=1, source_target_pairs={{0,1},{1,0},{2,3},{3,2},{4,5},{5,4},{6,7},{7,6},{8,9},{9,8},{10,11... | collective-permute-start | bytes 786440 | tf_op jit(solution)/shard_map/ppermute | solution.py:198
  7.6 13.1 %collective-permute-start.5 = (bf16[512,256]{1,0:T(8,128)(2,1)}, bf16[512,256]{1,0:T(8,128)(2,1)S(1)}, u32[]{:S(2)}, u32[]{:S(2)}) collective-permute-start(bf16[512,256]{1,0:T(8,128)(2,1)} %refs_0_.3), channel_id=1, source_target_pairs={{2,0},{8,1},{19,2},{25,3},{6,4},{12,5},{23,6},{29,7},{0,8},{10,9},... | collective-permute-start | bytes 786440 | tf_op jit(solution)/shard_map/ppermute | solution.py:219
  10.3 12.3 %collective-permute-start.7 = (bf16[512,256]{1,0:T(8,128)(2,1)}, bf16[512,256]{1,0:T(8,128)(2,1)S(1)}, u32[]{:S(2)}, u32[]{:S(2)}) collective-permute-start(bf16[512,256]{1,0:T(8,128)(2,1)} %refs_0_.3), channel_id=1, source_target_pairs={{1,0},{11,1},{16,2},{26,3},{5,4},{15,5},{20,6},{30,7},{3,8},{9,9},... | collective-permute-start | bytes 786440 | tf_op jit(solution)/shard_map/ppermute | solution.py:219
  12.9 12.2 %collective-permute-start.9 = (bf16[512,256]{1,0:T(8,128)(2,1)}, bf16[512,256]{1,0:T(8,128)(2,1)S(1)}, u32[]{:S(2)}, u32[]{:S(2)}) collective-permute-start(bf16[512,256]{1,0:T(8,128)(2,1)} %refs_0_.3), channel_id=1, source_target_pairs={{3,0},{9,1},{18,2},{24,3},{7,4},{13,5},{22,6},{28,7},{1,8},{11,9},... | collective-permute-start | bytes 786440 | tf_op jit(solution)/shard_map/ppermute | solution.py:219
  18.0 8.6 %collective-permute-start.3 = (bf16[512,256]{1,0:T(8,128)(2,1)S(1)}, bf16[512,256]{1,0:T(8,128)(2,1)S(1)}, u32[]{:S(2)}, u32[]{:S(2)}) collective-permute-start(bf16[512,256]{1,0:T(8,128)(2,1)S(1)} %collective-permute-done.1.refs_2_), channel_id=1, source_target_pairs={{0,1},{1,0},{2,3},{3,2},{4,5},{5,4},{6,7},{7,6},{8,9},{9,8},{10,11... | collective-permute-start | bytes 786440 | tf_op jit(solution)/shard_map/ppermute | solution.py:198
  19.3 23.2 %collective-permute-start.4 = (bf16[512,256]{1,0:T(8,128)(2,1)S(1)}, bf16[512,256]{1,0:T(8,128)(2,1)S(1)}, u32[]{:S(2)}, u32[]{:S(2)}) collective-permute-start(bf16[512,256]{1,0:T(8,128)(2,1)S(1)} %collective-permute-done.2.refs_4_), channel_id=1, source_target_pairs={{0,4},{4,0},{1,5},{5,1},{2,6},{6,2},{3,7},{7,3},{8,12},{12,8},{9,1... | collective-permute-start | bytes 786440 | tf_op jit(solution)/shard_map/ppermute | solution.py:230
  20.8 23.3 %collective-permute-start.6 = (bf16[512,256]{1,0:T(8,128)(2,1)S(1)}, bf16[512,256]{1,0:T(8,128)(2,1)S(1)}, u32[]{:S(2)}, u32[]{:S(2)}) collective-permute-start(bf16[512,256]{1,0:T(8,128)(2,1)S(1)} %collective-permute-done.5.refs_5_), channel_id=1, source_target_pairs={{0,4},{4,0},{1,5},{5,1},{2,6},{6,2},{3,7},{7,3},{8,12},{12,8},{9,1... | collective-permute-start | bytes 786440 | tf_op jit(solution)/shard_map/ppermute | solution.py:230
  22.6 24.7 %collective-permute-start.8 = (bf16[512,256]{1,0:T(8,128)(2,1)S(1)}, bf16[512,256]{1,0:T(8,128)(2,1)S(1)}, u32[]{:S(2)}, u32[]{:S(2)}) collective-permute-start(bf16[512,256]{1,0:T(8,128)(2,1)S(1)} %collective-permute-done.7.refs_6_), channel_id=1, source_target_pairs={{0,4},{4,0},{1,5},{5,1},{2,6},{6,2},{3,7},{7,3},{8,12},{12,8},{9,1... | collective-permute-start | bytes 786440 | tf_op jit(solution)/shard_map/ppermute | solution.py:230
  25.1 22.2 %collective-permute-start.10 = (bf16[512,256]{1,0:T(8,128)(2,1)S(1)}, bf16[512,256]{1,0:T(8,128)(2,1)S(1)}, u32[]{:S(2)}, u32[]{:S(2)}) collective-permute-start(bf16[512,256]{1,0:T(8,128)(2,1)S(1)} %collective-permute-done.9.refs_7_), channel_id=1, source_target_pairs={{0,4},{4,0},{1,5},{5,1},{2,6},{6,2},{3,7},{7,3},{8,12},{12,8},{9,1... | collective-permute-start | bytes 786440 | tf_op jit(solution)/shard_map/ppermute | solution.py:230
  34.0 22.6 %collective-permute-start.13 = (bf16[512,256]{1,0:T(8,128)(2,1)}, bf16[512,256]{1,0:T(8,128)(2,1)S(1)}, u32[]{:S(2)}, u32[]{:S(2)}) collective-permute-start(bf16[512,256]{1,0:T(8,128)(2,1)} %get-tuple-element.32), channel_id=1, source_target_pairs={{0,8},{8,0},{16,24},{24,16},{1,9},{9,1},{17,25},{25,17},{2,10},{10... | collective-permute-start | bytes 786440 | tf_op jit(solution)/shard_map/ppermute | solution.py:239
  42.4 14.2 %collective-permute-start.14 = (bf16[512,256]{1,0:T(8,128)(2,1)}, bf16[512,256]{1,0:T(8,128)(2,1)S(1)}, u32[]{:S(2)}, u32[]{:S(2)}) collective-permute-start(bf16[512,256]{1,0:T(8,128)(2,1)} %get-tuple-element.33), channel_id=1, source_target_pairs={{0,0},{1,2},{2,1},{3,3},{4,4},{5,6},{6,5},{7,7},{8,10},{9,8},{10,1... | collective-permute-start | bytes 786440 | tf_op jit(solution)/shard_map/ppermute | solution.py:236
  44.0 12.6 %collective-permute-start.15 = (bf16[512,256]{1,0:T(8,128)(2,1)}, bf16[512,256]{1,0:T(8,128)(2,1)S(1)}, u32[]{:S(2)}, u32[]{:S(2)}) collective-permute-start(bf16[512,256]{1,0:T(8,128)(2,1)} %get-tuple-element.34), channel_id=1, source_target_pairs={{0,2},{1,0},{2,3},{3,1},{4,6},{5,4},{6,7},{7,5},{8,8},{9,10},{10,9... | collective-permute-start | bytes 786440 | tf_op jit(solution)/shard_map/ppermute | solution.py:236
  56.6 8.6 %collective-permute-start.21 = (bf16[512,256]{1,0:T(8,128)(2,1)}, bf16[512,256]{1,0:T(8,128)(2,1)S(1)}, u32[]{:S(2)}, u32[]{:S(2)}) collective-permute-start(bf16[512,256]{1,0:T(8,128)(2,1)} %get-tuple-element.42), channel_id=1, source_target_pairs={{0,8},{8,0},{16,24},{24,16},{1,9},{9,1},{17,25},{25,17},{2,10},{10... | collective-permute-start | bytes 786440 | tf_op jit(solution)/shard_map/ppermute | solution.py:239
  58.4 15.5 %collective-permute-start.11 = (bf16[2,512,256]{2,1,0:T(8,128)(2,1)}, bf16[2,512,256]{2,1,0:T(8,128)(2,1)S(1)}, u32[]{:S(2)}, u32[]{:S(2)}) collective-permute-start(bf16[2,512,256]{2,1,0:T(8,128)(2,1)} %get-tuple-element.27), channel_id=1, source_target_pairs={{0,1},{1,0},{2,3},{3,2},{4,5},{5,4},{6,7},{7,6},{8,9},{9,8},{10,11... | collective-permute-start | bytes 1572872 | tf_op jit(solution)/shard_map/ppermute | solution.py:198
  58.4 8.5 %collective-permute-start.18 = (bf16[512,256]{1,0:T(8,128)(2,1)}, bf16[512,256]{1,0:T(8,128)(2,1)S(1)}, u32[]{:S(2)}, u32[]{:S(2)}) collective-permute-start(bf16[512,256]{1,0:T(8,128)(2,1)} %get-tuple-element.38), channel_id=1, source_target_pairs={{0,6},{1,4},{2,7},{3,5},{4,2},{5,0},{6,3},{7,1},{8,12},{9,14},{10,... | collective-permute-start | bytes 786440 | tf_op jit(solution)/shard_map/ppermute | solution.py:236
  59.4 18.8 %collective-permute-start.20 = (bf16[512,256]{1,0:T(8,128)(2,1)S(1)}, bf16[512,256]{1,0:T(8,128)(2,1)S(1)}, u32[]{:S(2)}, u32[]{:S(2)}) collective-permute-start(bf16[512,256]{1,0:T(8,128)(2,1)S(1)} %add_convert_fusion.2), channel_id=1, source_target_pairs={{0,1},{1,3},{2,0},{3,2},{4,5},{5,7},{6,4},{7,6},{8,11},{9,9},{10,1... | collective-permute-start | bytes 786440 | tf_op jit(solution)/shard_map/ppermute | solution.py:236
  61.4 11.8 %collective-permute-start.16 = (bf16[512,256]{1,0:T(8,128)(2,1)}, bf16[512,256]{1,0:T(8,128)(2,1)S(1)}, u32[]{:S(2)}, u32[]{:S(2)}) collective-permute-start(bf16[512,256]{1,0:T(8,128)(2,1)} %get-tuple-element.36), channel_id=1, source_target_pairs={{0,4},{1,6},{2,5},{3,7},{4,0},{5,2},{6,1},{7,3},{8,14},{9,12},{10,... | collective-permute-start | bytes 786440 | tf_op jit(solution)/shard_map/ppermute | solution.py:236
  66.2 12.0 %collective-permute-start.22 = (bf16[512,256]{1,0:T(8,128)(2,1)S(1)}, bf16[512,256]{1,0:T(8,128)(2,1)S(1)}, u32[]{:S(2)}, u32[]{:S(2)}) collective-permute-start(bf16[512,256]{1,0:T(8,128)(2,1)S(1)} %add_convert_fusion.1), channel_id=1, source_target_pairs={{0,5},{1,7},{2,4},{3,6},{4,1},{5,3},{6,0},{7,2},{8,15},{9,13},{10,... | collective-permute-start | bytes 786440 | tf_op jit(solution)/shard_map/ppermute | solution.py:236
  66.9 13.3 %collective-permute-start.19 = (bf16[512,256]{1,0:T(8,128)(2,1)S(1)}, bf16[512,256]{1,0:T(8,128)(2,1)S(1)}, u32[]{:S(2)}, u32[]{:S(2)}) collective-permute-start(bf16[512,256]{1,0:T(8,128)(2,1)S(1)} %add_convert_fusion.3), channel_id=1, source_target_pairs={{0,8},{1,25},{2,2},{3,19},{4,12},{5,29},{6,6},{7,23},{8,0},{9,17},... | collective-permute-start | bytes 786440 | tf_op jit(solution)/shard_map/ppermute | solution.py:286
  73.2 7.0 %collective-permute-start.17 = (bf16[512,256]{1,0:T(8,128)(2,1)S(1)}, bf16[512,256]{1,0:T(8,128)(2,1)S(1)}, u32[]{:S(2)}, u32[]{:S(2)}) collective-permute-start(bf16[512,256]{1,0:T(8,128)(2,1)S(1)} %add_convert_fusion.4), channel_id=1, source_target_pairs={{0,0},{1,17},{2,10},{3,27},{4,4},{5,21},{6,14},{7,31},{8,8},{9,25}... | collective-permute-start | bytes 786440 | tf_op jit(solution)/shard_map/ppermute | solution.py:286
  75.3 8.9 %collective-permute-start.12 = (bf16[1,512,256]{2,1,0:T(8,128)(2,1)S(1)}, bf16[1,512,256]{2,1,0:T(8,128)(2,1)S(1)}, u32[]{:S(2)}, u32[]{:S(2)}) collective-permute-start(bf16[1,512,256]{2,1,0:T(8,128)(2,1)S(1)} %dynamic-slice_convert_fusion), channel_id=1, source_target_pairs={{0,2},{1,3},{2,0},{3,1},{4,6},{5,7},{6,4},{7,5},{8,10},{9,11},{10,... | collective-permute-start | bytes 786440 | tf_op jit(solution)/shard_map/ppermute | solution.py:198
  78.3 12.0 %collective-permute-start.23 = (bf16[512,256]{1,0:T(8,128)(2,1)S(1)}, bf16[512,256]{1,0:T(8,128)(2,1)S(1)}, u32[]{:S(2)}, u32[]{:S(2)}) collective-permute-start(bf16[512,256]{1,0:T(8,128)(2,1)S(1)} %add_convert_fusion), channel_id=1, source_target_pairs={{0,16},{1,1},{2,26},{3,11},{4,20},{5,5},{6,30},{7,15},{8,24},{9,9}... | collective-permute-start | bytes 786440 | tf_op jit(solution)/shard_map/ppermute | solution.py:286
  (13 other events, 96.5 us)

commit v7 on v6

--- a/solution.py
+++ b/solution.py
@@ -111,12 +111,16 @@
             resids[i] = resid.astype(jnp.bfloat16)
         return carry
 
-    def gradients(g, carry):
+    def source_sums(g, carry):
         for u in range(UNROLL):
             i = g * UNROLL + u
-            resid = resids[i]
-            gs_acc[place(coords[1, slot_of[i]])] += dot(resid, right[i])
-            gt_acc[place(tgt_of[i])] += dot(resid, left[i], CONTRACT_FIRST)
+            gs_acc[place(coords[1, slot_of[i]])] += dot(resids[i], right[i])
+        return carry
+
+    def target_sums(g, carry):
+        for u in range(UNROLL):
+            i = g * UNROLL + u
+            gt_acc[place(tgt_of[i])] += dot(resids[i], left[i], CONTRACT_FIRST)
         return carry
 
     def arrive(i, carry):
@@ -128,7 +132,7 @@
     lax.fori_loop(0, groups, residuals, 0)
     if not opens:
         gs_copy.wait()
-    lax.fori_loop(0, groups, gradients, 0)
+    lax.fori_loop(0, groups, source_sums, 0)
 
     outs = []
     if closes:
@@ -143,6 +147,7 @@
     outs = [pltpu.make_async_copy(a, b, sems.at[i]) for i, (a, b) in enumerate(outs)]
     for copy in outs:
         copy.start()
+    lax.fori_loop(0, groups, target_sums, 0)
     for i, d in enumerate(parts):
         for n in range(n_x):
             tgt[part_at(d, n)] = gt_acc[part_at(d, n)].astype(tgt.dtype)

time: 91.4 us -> 90.2 us (0.987); the launches traced: 91.3 us -> 89.1 us
  starting transfers between devices: 51.7 us -> 54 us
  Pallas kernels: 15.1 us -> 12.9 us
  waiting for transfers between devices: 17.7 us -> 15.6 us
    ppermute x6, starting transfers between devices: 9 us -> 14.2 us  [to_owner(): lax.ppermute(value, AXES, part_pairs(d, lambda p, x, j, q: (p, (x - t) %...]
    ppermute x2, starting transfers between devices: 10.2 us -> 5.49 us  [to_pair(): return lax.ppermute(value, 'zz', [(p, p ^ 1) for p in range(planes)])]
    pallas_call x2, Pallas kernels: 15.1 us -> 12.9 us  [run_slots(): pl.pallas_call(functools.partial(slots_kernel, first, last, n_col, ratio)...]
    ppermute x5, waiting for transfers between devices: 3.91 us -> 2.03 us  [swap(): return lax.ppermute(value, 'col', [(i, i ^ bit) for i in range(n_col)])]
    ppermute x3, starting transfers between devices: 5.37 us -> 6.81 us  [local(): landed.append(lax.ppermute(term, AXES, pairs))]
  transfers between devices with their start and end apart: 24 -> 24, of which waited for: 6 -> 7; matrix products, arithmetic and copies ran while one was open for 4% -> 4% of each run, Pallas kernels for 17% -> 14%
where the time goes in v7:
time: 90.2 us; the launch traced here: 89.1 us
  starting transfers between devices  54 us (60%)
  waiting for transfers between devices  15.6 us (17%)
  Pallas kernels  12.9 us (14%)
  other arithmetic  4.25 us (5%)
  local copies, waits for them, and re-layouts  1.49 us (2%)
  between operations  0.97 us (1%)
    ppermute x6, starting transfers between devices, to_owner(): lax.ppermute(value, AXES, part_pairs(d, lambda p, x, j, q: (p, (x - t) %...  14.2 us
    pallas_call x2, Pallas kernels, run_slots(): pl.pallas_call(functools.partial(slots_kernel, first, last, n_col, ratio)...  12.9 us
    ppermute x4, starting transfers between devices, local(): own[d] = lax.ppermute(factors, AXES, [(b, a) for a, b in pairs])  11.9 us
    ppermute x5, starting transfers between devices, swap(): return lax.ppermute(value, 'col', [(i, i ^ bit) for i in range(n_col)])  10.6 us
    ppermute x3, starting transfers between devices, local(): landed.append(lax.ppermute(term, AXES, pairs))  6.81 us
    ppermute x3, waiting for transfers between devices, local(): landed.append(lax.ppermute(term, AXES, pairs))  6.04 us
    ppermute x2, starting transfers between devices, to_pair(): return lax.ppermute(value, 'zz', [(p, p ^ 1) for p in range(planes)])  5.49 us
    ppermute x4, starting transfers between devices, local(): lax.ppermute(own[d], 'xx', [(x, (x + s) % ratio) for x in range(ratio)])  5.01 us
  transfers between devices with their start and end apart: 24, of which 7 were waited for; matrix products, arithmetic and copies ran while one was open for 4% of the time, Pallas kernels for 14%

profile of v7, /device:TPU:0, one launch (start us, length us, event | category | flops | bytes accessed | tf_op | source)
XLA Modules:
  0.0 89.1 jit_solution(4181027545663350656)
XLA Ops:
  0.0 3.0 %collective-permute-start.1 = (bf16[512,256]{1,0:T(8,128)(2,1)}, bf16[512,256]{1,0:T(8,128)(2,1)S(1)}, u32[]{:S(2)}, u32[]{:S(2)}) collective-permute-start(bf16[512,256]{1,0:T(8,128)(2,1)} %refs_0_.3), channel_id=1, source_target_pairs={{0,2},{1,3},{2,0},{3,1},{4,6},{5,7},{6,4},{7,5},{8,10},{9,11},{10,... | collective-permute-start | bytes 786440 | tf_op jit(solution)/shard_map/ppermute | solution.py:203
  3.0 1.6 %collective-permute-start.2 = (bf16[512,256]{1,0:T(8,128)(2,1)}, bf16[512,256]{1,0:T(8,128)(2,1)S(1)}, u32[]{:S(2)}, u32[]{:S(2)}) collective-permute-start(bf16[512,256]{1,0:T(8,128)(2,1)} %refs_0_.3), channel_id=1, source_target_pairs={{0,0},{10,1},{17,2},{27,3},{4,4},{14,5},{21,6},{31,7},{2,8},{8,9},... | collective-permute-start | bytes 786440 | tf_op jit(solution)/shard_map/ppermute | solution.py:224
  4.6 3.1 %collective-permute-start = (bf16[512,256]{1,0:T(8,128)(2,1)}, bf16[512,256]{1,0:T(8,128)(2,1)S(1)}, u32[]{:S(2)}, u32[]{:S(2)}) collective-permute-start(bf16[512,256]{1,0:T(8,128)(2,1)} %refs_0_.3), channel_id=1, source_target_pairs={{0,1},{1,0},{2,3},{3,2},{4,5},{5,4},{6,7},{7,6},{8,9},{9,8},{10,11... | collective-permute-start | bytes 786440 | tf_op jit(solution)/shard_map/ppermute | solution.py:203
  7.6 2.6 %collective-permute-start.5 = (bf16[512,256]{1,0:T(8,128)(2,1)}, bf16[512,256]{1,0:T(8,128)(2,1)S(1)}, u32[]{:S(2)}, u32[]{:S(2)}) collective-permute-start(bf16[512,256]{1,0:T(8,128)(2,1)} %refs_0_.3), channel_id=1, source_target_pairs={{2,0},{8,1},{19,2},{25,3},{6,4},{12,5},{23,6},{29,7},{0,8},{10,9},... | collective-permute-start | bytes 786440 | tf_op jit(solution)/shard_map/ppermute | solution.py:224
  10.3 2.6 %collective-permute-start.7 = (bf16[512,256]{1,0:T(8,128)(2,1)}, bf16[512,256]{1,0:T(8,128)(2,1)S(1)}, u32[]{:S(2)}, u32[]{:S(2)}) collective-permute-start(bf16[512,256]{1,0:T(8,128)(2,1)} %refs_0_.3), channel_id=1, source_target_pairs={{1,0},{11,1},{16,2},{26,3},{5,4},{15,5},{20,6},{30,7},{3,8},{9,9},... | collective-permute-start | bytes 786440 | tf_op jit(solution)/shard_map/ppermute | solution.py:224
  12.9 5.0 %collective-permute-start.9 = (bf16[512,256]{1,0:T(8,128)(2,1)}, bf16[512,256]{1,0:T(8,128)(2,1)S(1)}, u32[]{:S(2)}, u32[]{:S(2)}) collective-permute-start(bf16[512,256]{1,0:T(8,128)(2,1)} %refs_0_.3), channel_id=1, source_target_pairs={{3,0},{9,1},{18,2},{24,3},{7,4},{13,5},{22,6},{28,7},{1,8},{11,9},... | collective-permute-start | bytes 786440 | tf_op jit(solution)/shard_map/ppermute | solution.py:224
  19.3 1.5 %collective-permute-start.4 = (bf16[512,256]{1,0:T(8,128)(2,1)S(1)}, bf16[512,256]{1,0:T(8,128)(2,1)S(1)}, u32[]{:S(2)}, u32[]{:S(2)}) collective-permute-start(bf16[512,256]{1,0:T(8,128)(2,1)S(1)} %collective-permute-done.2.refs_4_), channel_id=1, source_target_pairs={{0,4},{4,0},{1,5},{5,1},{2,6},{6,2},{3,7},{7,3},{8,12},{12,8},{9,1... | collective-permute-start | bytes 786440 | tf_op jit(solution)/shard_map/ppermute | solution.py:235
  22.6 1.5 %collective-permute-start.8 = (bf16[512,256]{1,0:T(8,128)(2,1)S(1)}, bf16[512,256]{1,0:T(8,128)(2,1)S(1)}, u32[]{:S(2)}, u32[]{:S(2)}) collective-permute-start(bf16[512,256]{1,0:T(8,128)(2,1)S(1)} %collective-permute-done.7.refs_6_), channel_id=1, source_target_pairs={{0,4},{4,0},{1,5},{5,1},{2,6},{6,2},{3,7},{7,3},{8,12},{12,8},{9,1... | collective-permute-start | bytes 786440 | tf_op jit(solution)/shard_map/ppermute | solution.py:235
  25.1 1.5 %collective-permute-start.10 = (bf16[512,256]{1,0:T(8,128)(2,1)S(1)}, bf16[512,256]{1,0:T(8,128)(2,1)S(1)}, u32[]{:S(2)}, u32[]{:S(2)}) collective-permute-start(bf16[512,256]{1,0:T(8,128)(2,1)S(1)} %collective-permute-done.9.refs_7_), channel_id=1, source_target_pairs={{0,4},{4,0},{1,5},{5,1},{2,6},{6,2},{3,7},{7,3},{8,12},{12,8},{9,1... | collective-permute-start | bytes 786440 | tf_op jit(solution)/shard_map/ppermute | solution.py:235
  27.3 6.4 %shard_map.55 = (bf16[512,256]{1,0:T(8,128)(2,1)}, bf16[512,256]{1,0:T(8,128)(2,1)}, bf16[512,256]{1,0:T(8,128)(2,1)}, bf16[512,256]{1,0:T(8,128)(2,1)}, f32[2048,256]{1,0:T(8,128)}) custom-call(s32[4]{0:T(128)} %pad_add_fusion.scalars, s32[3,32]{1,0:T(4,128)} %bitcast.10, bf16[8,256,256]{2,1,0:T(8,128)(2,1)} %cores_hbm.3, bf16[512,256]{1,0:T(8,128)(2,1)} %refs_0_.3, ...), custom_call_target="tpu_custom_call" | custom-call | tf_op jit(solution)/shard_map/pallas_call | solution.py:176
  33.7 4.8 %collective-permute-start.13 = (bf16[512,256]{1,0:T(8,128)(2,1)}, bf16[512,256]{1,0:T(8,128)(2,1)S(1)}, u32[]{:S(2)}, u32[]{:S(2)}) collective-permute-start(bf16[512,256]{1,0:T(8,128)(2,1)} %get-tuple-element.32), channel_id=1, source_target_pairs={{0,8},{8,0},{16,24},{24,16},{1,9},{9,1},{17,25},{25,17},{2,10},{10... | collective-permute-start | bytes 786440 | tf_op jit(solution)/shard_map/ppermute | solution.py:244
  38.5 1.6 %collective-permute-start.14 = (bf16[512,256]{1,0:T(8,128)(2,1)}, bf16[512,256]{1,0:T(8,128)(2,1)S(1)}, u32[]{:S(2)}, u32[]{:S(2)}) collective-permute-start(bf16[512,256]{1,0:T(8,128)(2,1)} %get-tuple-element.33), channel_id=1, source_target_pairs={{0,0},{1,2},{2,1},{3,3},{4,4},{5,6},{6,5},{7,7},{8,10},{9,8},{10,1... | collective-permute-start | bytes 786440 | tf_op jit(solution)/shard_map/ppermute | solution.py:241
  40.1 5.8 %collective-permute-start.15 = (bf16[512,256]{1,0:T(8,128)(2,1)}, bf16[512,256]{1,0:T(8,128)(2,1)S(1)}, u32[]{:S(2)}, u32[]{:S(2)}) collective-permute-start(bf16[512,256]{1,0:T(8,128)(2,1)} %get-tuple-element.34), channel_id=1, source_target_pairs={{0,2},{1,0},{2,3},{3,1},{4,6},{5,4},{6,7},{7,5},{8,8},{9,10},{10,9... | collective-permute-start | bytes 786440 | tf_op jit(solution)/shard_map/ppermute | solution.py:241
  46.7 6.4 %shard_map.56 = (bf16[512,256]{1,0:T(8,128)(2,1)}, bf16[512,256]{1,0:T(8,128)(2,1)}, bf16[512,256]{1,0:T(8,128)(2,1)}, bf16[512,256]{1,0:T(8,128)(2,1)}, f32[2,5...) custom-call(s32[4]{0:T(128)} %pad_add_fusion.scalars, s32[3,32]{1,0:T(4,128)} %bitcast.11, bf16[8,256,256]{2,1,0:T(8,128)(2,1)} %cores_hbm.3, ...), custom_call_target="tpu_custom_call" | custom-call | tf_op jit(solution)/shard_map/pallas_call | solution.py:176
  54.1 3.5 %collective-permute-start.18 = (bf16[512,256]{1,0:T(8,128)(2,1)}, bf16[512,256]{1,0:T(8,128)(2,1)S(1)}, u32[]{:S(2)}, u32[]{:S(2)}) collective-permute-start(bf16[512,256]{1,0:T(8,128)(2,1)} %get-tuple-element.38), channel_id=1, source_target_pairs={{0,6},{1,4},{2,7},{3,5},{4,2},{5,0},{6,3},{7,1},{8,12},{9,14},{10,... | collective-permute-start | bytes 786440 | tf_op jit(solution)/shard_map/ppermute | solution.py:241
  57.7 1.9 %collective-permute-start.20 = (bf16[512,256]{1,0:T(8,128)(2,1)S(1)}, bf16[512,256]{1,0:T(8,128)(2,1)S(1)}, u32[]{:S(2)}, u32[]{:S(2)}) collective-permute-start(bf16[512,256]{1,0:T(8,128)(2,1)S(1)} %add_convert_fusion.2), channel_id=1, source_target_pairs={{0,1},{1,3},{2,0},{3,2},{4,5},{5,7},{6,4},{7,6},{8,11},{9,9},{10,1... | collective-permute-start | bytes 786440 | tf_op jit(solution)/shard_map/ppermute | solution.py:241
  59.7 2.0 %collective-permute-done.21 = bf16[512,256]{1,0:T(8,128)(2,1)S(1)} collective-permute-done((bf16[512,256]{1,0:T(8,128)(2,1)}, bf16[512,256]{1,0:T(8,128)(2,1)S(1)}, u32[]{:S(2)}, u32[]{:S(2)}) %collective-permute-start.21) | collective-permute-done | bytes 262176 | tf_op jit(solution)/shard_map/ppermute | solution.py:244
  64.9 2.2 %collective-permute-start.19 = (bf16[512,256]{1,0:T(8,128)(2,1)S(1)}, bf16[512,256]{1,0:T(8,128)(2,1)S(1)}, u32[]{:S(2)}, u32[]{:S(2)}) collective-permute-start(bf16[512,256]{1,0:T(8,128)(2,1)S(1)} %add_convert_fusion.3), channel_id=1, source_target_pairs={{0,8},{1,25},{2,2},{3,19},{4,12},{5,29},{6,6},{7,23},{8,0},{9,17},... | collective-permute-start | bytes 786440 | tf_op jit(solution)/shard_map/ppermute | solution.py:291
  67.1 3.3 %collective-permute-done.16 = bf16[512,256]{1,0:T(8,128)(2,1)S(1)} collective-permute-done((bf16[512,256]{1,0:T(8,128)(2,1)}, bf16[512,256]{1,0:T(8,128)(2,1)S(1)}, u32[]{:S(2)}, u32[]{:S(2)}) %collective-permute-start.16) | collective-permute-done | bytes 262176 | tf_op jit(solution)/shard_map/ppermute | solution.py:241
  71.2 1.3 %convert_add_fusion = f32[2,512,256]{2,1,0:T(8,128)S(1)} fusion(f32[2,512,256]{2,1,0:T(8,128)} %get-tuple-element.26, bf16[2,512,256]{2,1,0:T(8,128)(2,1)S(1)} %collective-permute-done.11), kind=kLoop, calls=%fused_computation | loop fusion | flops 524288 | bytes 2621440 | tf_op jit(solution)/shard_map/add | solution.py:266
  72.5 3.1 %collective-permute-start.12 = (bf16[1,512,256]{2,1,0:T(8,128)(2,1)S(1)}, bf16[1,512,256]{2,1,0:T(8,128)(2,1)S(1)}, u32[]{:S(2)}, u32[]{:S(2)}) collective-permute-start(bf16[1,512,256]{2,1,0:T(8,128)(2,1)S(1)} %dynamic-slice_convert_fusion), channel_id=1, source_target_pairs={{0,2},{1,3},{2,0},{3,1},{4,6},{5,7},{6,4},{7,5},{8,10},{9,11},{10,... | collective-permute-start | bytes 786440 | tf_op jit(solution)/shard_map/ppermute | solution.py:203
  76.2 3.9 %collective-permute-start.23 = (bf16[512,256]{1,0:T(8,128)(2,1)S(1)}, bf16[512,256]{1,0:T(8,128)(2,1)S(1)}, u32[]{:S(2)}, u32[]{:S(2)}) collective-permute-start(bf16[512,256]{1,0:T(8,128)(2,1)S(1)} %add_convert_fusion), channel_id=1, source_target_pairs={{0,16},{1,1},{2,26},{3,11},{4,20},{5,5},{6,30},{7,15},{8,24},{9,9}... | collective-permute-start | bytes 786440 | tf_op jit(solution)/shard_map/ppermute | solution.py:291
  80.1 2.0 %collective-permute-done.12 = bf16[1,512,256]{2,1,0:T(8,128)(2,1)S(1)} collective-permute-done((bf16[1,512,256]{2,1,0:T(8,128)(2,1)S(1)}, bf16[1,512,256]{2,1,0:T(8,128)(2,1)S(1)}, u32[]{:S(2)}, u32[]{:S(2)}) %collective-permute-start.12) | collective-permute-done | bytes 262176 | tf_op jit(solution)/shard_map/ppermute | solution.py:203
  82.1 6.0 %collective-permute-done.23 = bf16[512,256]{1,0:T(8,128)(2,1)S(1)} collective-permute-done((bf16[512,256]{1,0:T(8,128)(2,1)S(1)}, bf16[512,256]{1,0:T(8,128)(2,1)S(1)}, u32[]{:S(2)}, u32[]{:S(2)}) %collective-permute-start.23) | collective-permute-done | bytes 262176 | tf_op jit(solution)/shard_map/ppermute | solution.py:291
  (61 shorter events, 11.4 us)
Async XLA Ops:
  0.0 12.9 %collective-permute-start.1 = (bf16[512,256]{1,0:T(8,128)(2,1)}, bf16[512,256]{1,0:T(8,128)(2,1)S(1)}, u32[]{:S(2)}, u32[]{:S(2)}) collective-permute-start(bf16[512,256]{1,0:T(8,128)(2,1)} %refs_0_.3), channel_id=1, source_target_pairs={{0,2},{1,3},{2,0},{3,1},{4,6},{5,7},{6,4},{7,5},{8,10},{9,11},{10,... | collective-permute-start | bytes 786440 | tf_op jit(solution)/shard_map/ppermute | solution.py:203
  3.0 15.0 %collective-permute-start.2 = (bf16[512,256]{1,0:T(8,128)(2,1)}, bf16[512,256]{1,0:T(8,128)(2,1)S(1)}, u32[]{:S(2)}, u32[]{:S(2)}) collective-permute-start(bf16[512,256]{1,0:T(8,128)(2,1)} %refs_0_.3), channel_id=1, source_target_pairs={{0,0},{10,1},{17,2},{27,3},{4,4},{14,5},{21,6},{31,7},{2,8},{8,9},... | collective-permute-start | bytes 786440 | tf_op jit(solution)/shard_map/ppermute | solution.py:224
  4.6 14.7 %collective-permute-start = (bf16[512,256]{1,0:T(8,128)(2,1)}, bf16[512,256]{1,0:T(8,128)(2,1)S(1)}, u32[]{:S(2)}, u32[]{:S(2)}) collective-permute-start(bf16[512,256]{1,0:T(8,128)(2,1)} %refs_0_.3), channel_id=1, source_target_pairs={{0,1},{1,0},{2,3},{3,2},{4,5},{5,4},{6,7},{7,6},{8,9},{9,8},{10,11... | collective-permute-start | bytes 786440 | tf_op jit(solution)/shard_map/ppermute | solution.py:203
  7.6 13.1 %collective-permute-start.5 = (bf16[512,256]{1,0:T(8,128)(2,1)}, bf16[512,256]{1,0:T(8,128)(2,1)S(1)}, u32[]{:S(2)}, u32[]{:S(2)}) collective-permute-start(bf16[512,256]{1,0:T(8,128)(2,1)} %refs_0_.3), channel_id=1, source_target_pairs={{2,0},{8,1},{19,2},{25,3},{6,4},{12,5},{23,6},{29,7},{0,8},{10,9},... | collective-permute-start | bytes 786440 | tf_op jit(solution)/shard_map/ppermute | solution.py:224
  10.3 12.3 %collective-permute-start.7 = (bf16[512,256]{1,0:T(8,128)(2,1)}, bf16[512,256]{1,0:T(8,128)(2,1)S(1)}, u32[]{:S(2)}, u32[]{:S(2)}) collective-permute-start(bf16[512,256]{1,0:T(8,128)(2,1)} %refs_0_.3), channel_id=1, source_target_pairs={{1,0},{11,1},{16,2},{26,3},{5,4},{15,5},{20,6},{30,7},{3,8},{9,9},... | collective-permute-start | bytes 786440 | tf_op jit(solution)/shard_map/ppermute | solution.py:224
  12.9 12.2 %collective-permute-start.9 = (bf16[512,256]{1,0:T(8,128)(2,1)}, bf16[512,256]{1,0:T(8,128)(2,1)S(1)}, u32[]{:S(2)}, u32[]{:S(2)}) collective-permute-start(bf16[512,256]{1,0:T(8,128)(2,1)} %refs_0_.3), channel_id=1, source_target_pairs={{3,0},{9,1},{18,2},{24,3},{7,4},{13,5},{22,6},{28,7},{1,8},{11,9},... | collective-permute-start | bytes 786440 | tf_op jit(solution)/shard_map/ppermute | solution.py:224
  18.0 8.6 %collective-permute-start.3 = (bf16[512,256]{1,0:T(8,128)(2,1)S(1)}, bf16[512,256]{1,0:T(8,128)(2,1)S(1)}, u32[]{:S(2)}, u32[]{:S(2)}) collective-permute-start(bf16[512,256]{1,0:T(8,128)(2,1)S(1)} %collective-permute-done.1.refs_2_), channel_id=1, source_target_pairs={{0,1},{1,0},{2,3},{3,2},{4,5},{5,4},{6,7},{7,6},{8,9},{9,8},{10,11... | collective-permute-start | bytes 786440 | tf_op jit(solution)/shard_map/ppermute | solution.py:203
  19.3 19.2 %collective-permute-start.4 = (bf16[512,256]{1,0:T(8,128)(2,1)S(1)}, bf16[512,256]{1,0:T(8,128)(2,1)S(1)}, u32[]{:S(2)}, u32[]{:S(2)}) collective-permute-start(bf16[512,256]{1,0:T(8,128)(2,1)S(1)} %collective-permute-done.2.refs_4_), channel_id=1, source_target_pairs={{0,4},{4,0},{1,5},{5,1},{2,6},{6,2},{3,7},{7,3},{8,12},{12,8},{9,1... | collective-permute-start | bytes 786440 | tf_op jit(solution)/shard_map/ppermute | solution.py:235
  20.8 19.3 %collective-permute-start.6 = (bf16[512,256]{1,0:T(8,128)(2,1)S(1)}, bf16[512,256]{1,0:T(8,128)(2,1)S(1)}, u32[]{:S(2)}, u32[]{:S(2)}) collective-permute-start(bf16[512,256]{1,0:T(8,128)(2,1)S(1)} %collective-permute-done.5.refs_5_), channel_id=1, source_target_pairs={{0,4},{4,0},{1,5},{5,1},{2,6},{6,2},{3,7},{7,3},{8,12},{12,8},{9,1... | collective-permute-start | bytes 786440 | tf_op jit(solution)/shard_map/ppermute | solution.py:235
  22.6 23.3 %collective-permute-start.8 = (bf16[512,256]{1,0:T(8,128)(2,1)S(1)}, bf16[512,256]{1,0:T(8,128)(2,1)S(1)}, u32[]{:S(2)}, u32[]{:S(2)}) collective-permute-start(bf16[512,256]{1,0:T(8,128)(2,1)S(1)} %collective-permute-done.7.refs_6_), channel_id=1, source_target_pairs={{0,4},{4,0},{1,5},{5,1},{2,6},{6,2},{3,7},{7,3},{8,12},{12,8},{9,1... | collective-permute-start | bytes 786440 | tf_op jit(solution)/shard_map/ppermute | solution.py:235
  25.1 20.8 %collective-permute-start.10 = (bf16[512,256]{1,0:T(8,128)(2,1)S(1)}, bf16[512,256]{1,0:T(8,128)(2,1)S(1)}, u32[]{:S(2)}, u32[]{:S(2)}) collective-permute-start(bf16[512,256]{1,0:T(8,128)(2,1)S(1)} %collective-permute-done.9.refs_7_), channel_id=1, source_target_pairs={{0,4},{4,0},{1,5},{5,1},{2,6},{6,2},{3,7},{7,3},{8,12},{12,8},{9,1... | collective-permute-start | bytes 786440 | tf_op jit(solution)/shard_map/ppermute | solution.py:235
  33.7 19.5 %collective-permute-start.13 = (bf16[512,256]{1,0:T(8,128)(2,1)}, bf16[512,256]{1,0:T(8,128)(2,1)S(1)}, u32[]{:S(2)}, u32[]{:S(2)}) collective-permute-start(bf16[512,256]{1,0:T(8,128)(2,1)} %get-tuple-element.32), channel_id=1, source_target_pairs={{0,8},{8,0},{16,24},{24,16},{1,9},{9,1},{17,25},{25,17},{2,10},{10... | collective-permute-start | bytes 786440 | tf_op jit(solution)/shard_map/ppermute | solution.py:244
  38.5 14.7 %collective-permute-start.14 = (bf16[512,256]{1,0:T(8,128)(2,1)}, bf16[512,256]{1,0:T(8,128)(2,1)S(1)}, u32[]{:S(2)}, u32[]{:S(2)}) collective-permute-start(bf16[512,256]{1,0:T(8,128)(2,1)} %get-tuple-element.33), channel_id=1, source_target_pairs={{0,0},{1,2},{2,1},{3,3},{4,4},{5,6},{6,5},{7,7},{8,10},{9,8},{10,1... | collective-permute-start | bytes 786440 | tf_op jit(solution)/shard_map/ppermute | solution.py:241
  40.1 13.1 %collective-permute-start.15 = (bf16[512,256]{1,0:T(8,128)(2,1)}, bf16[512,256]{1,0:T(8,128)(2,1)S(1)}, u32[]{:S(2)}, u32[]{:S(2)}) collective-permute-start(bf16[512,256]{1,0:T(8,128)(2,1)} %get-tuple-element.34), channel_id=1, source_target_pairs={{0,2},{1,0},{2,3},{3,1},{4,6},{5,4},{6,7},{7,5},{8,8},{9,10},{10,9... | collective-permute-start | bytes 786440 | tf_op jit(solution)/shard_map/ppermute | solution.py:241
  53.2 8.5 %collective-permute-start.21 = (bf16[512,256]{1,0:T(8,128)(2,1)}, bf16[512,256]{1,0:T(8,128)(2,1)S(1)}, u32[]{:S(2)}, u32[]{:S(2)}) collective-permute-start(bf16[512,256]{1,0:T(8,128)(2,1)} %get-tuple-element.42), channel_id=1, source_target_pairs={{0,8},{8,0},{16,24},{24,16},{1,9},{9,1},{17,25},{25,17},{2,10},{10... | collective-permute-start | bytes 786440 | tf_op jit(solution)/shard_map/ppermute | solution.py:244
  53.9 17.2 %collective-permute-start.11 = (bf16[2,512,256]{2,1,0:T(8,128)(2,1)}, bf16[2,512,256]{2,1,0:T(8,128)(2,1)S(1)}, u32[]{:S(2)}, u32[]{:S(2)}) collective-permute-start(bf16[2,512,256]{2,1,0:T(8,128)(2,1)} %get-tuple-element.27), channel_id=1, source_target_pairs={{0,1},{1,0},{2,3},{3,2},{4,5},{5,4},{6,7},{7,6},{8,9},{9,8},{10,11... | collective-permute-start | bytes 1572872 | tf_op jit(solution)/shard_map/ppermute | solution.py:203
  54.1 10.7 %collective-permute-start.18 = (bf16[512,256]{1,0:T(8,128)(2,1)}, bf16[512,256]{1,0:T(8,128)(2,1)S(1)}, u32[]{:S(2)}, u32[]{:S(2)}) collective-permute-start(bf16[512,256]{1,0:T(8,128)(2,1)} %get-tuple-element.38), channel_id=1, source_target_pairs={{0,6},{1,4},{2,7},{3,5},{4,2},{5,0},{6,3},{7,1},{8,12},{9,14},{10,... | collective-permute-start | bytes 786440 | tf_op jit(solution)/shard_map/ppermute | solution.py:241
  57.7 17.9 %collective-permute-start.20 = (bf16[512,256]{1,0:T(8,128)(2,1)S(1)}, bf16[512,256]{1,0:T(8,128)(2,1)S(1)}, u32[]{:S(2)}, u32[]{:S(2)}) collective-permute-start(bf16[512,256]{1,0:T(8,128)(2,1)S(1)} %add_convert_fusion.2), channel_id=1, source_target_pairs={{0,1},{1,3},{2,0},{3,2},{4,5},{5,7},{6,4},{7,6},{8,11},{9,9},{10,1... | collective-permute-start | bytes 786440 | tf_op jit(solution)/shard_map/ppermute | solution.py:241
  59.7 10.7 %collective-permute-start.16 = (bf16[512,256]{1,0:T(8,128)(2,1)}, bf16[512,256]{1,0:T(8,128)(2,1)S(1)}, u32[]{:S(2)}, u32[]{:S(2)}) collective-permute-start(bf16[512,256]{1,0:T(8,128)(2,1)} %get-tuple-element.36), channel_id=1, source_target_pairs={{0,4},{1,6},{2,5},{3,7},{4,0},{5,2},{6,1},{7,3},{8,14},{9,12},{10,... | collective-permute-start | bytes 786440 | tf_op jit(solution)/shard_map/ppermute | solution.py:241
  62.7 13.4 %collective-permute-start.22 = (bf16[512,256]{1,0:T(8,128)(2,1)S(1)}, bf16[512,256]{1,0:T(8,128)(2,1)S(1)}, u32[]{:S(2)}, u32[]{:S(2)}) collective-permute-start(bf16[512,256]{1,0:T(8,128)(2,1)S(1)} %add_convert_fusion.1), channel_id=1, source_target_pairs={{0,5},{1,7},{2,4},{3,6},{4,1},{5,3},{6,0},{7,2},{8,15},{9,13},{10,... | collective-permute-start | bytes 786440 | tf_op jit(solution)/shard_map/ppermute | solution.py:241
  64.9 15.2 %collective-permute-start.19 = (bf16[512,256]{1,0:T(8,128)(2,1)S(1)}, bf16[512,256]{1,0:T(8,128)(2,1)S(1)}, u32[]{:S(2)}, u32[]{:S(2)}) collective-permute-start(bf16[512,256]{1,0:T(8,128)(2,1)S(1)} %add_convert_fusion.3), channel_id=1, source_target_pairs={{0,8},{1,25},{2,2},{3,19},{4,12},{5,29},{6,6},{7,23},{8,0},{9,17},... | collective-permute-start | bytes 786440 | tf_op jit(solution)/shard_map/ppermute | solution.py:291
  70.5 9.6 %collective-permute-start.17 = (bf16[512,256]{1,0:T(8,128)(2,1)S(1)}, bf16[512,256]{1,0:T(8,128)(2,1)S(1)}, u32[]{:S(2)}, u32[]{:S(2)}) collective-permute-start(bf16[512,256]{1,0:T(8,128)(2,1)S(1)} %add_convert_fusion.4), channel_id=1, source_target_pairs={{0,0},{1,17},{2,10},{3,27},{4,4},{5,21},{6,14},{7,31},{8,8},{9,25}... | collective-permute-start | bytes 786440 | tf_op jit(solution)/shard_map/ppermute | solution.py:291
  72.5 9.5 %collective-permute-start.12 = (bf16[1,512,256]{2,1,0:T(8,128)(2,1)S(1)}, bf16[1,512,256]{2,1,0:T(8,128)(2,1)S(1)}, u32[]{:S(2)}, u32[]{:S(2)}) collective-permute-start(bf16[1,512,256]{2,1,0:T(8,128)(2,1)S(1)} %dynamic-slice_convert_fusion), channel_id=1, source_target_pairs={{0,2},{1,3},{2,0},{3,1},{4,6},{5,7},{6,4},{7,5},{8,10},{9,11},{10,... | collective-permute-start | bytes 786440 | tf_op jit(solution)/shard_map/ppermute | solution.py:203
  76.2 12.0 %collective-permute-start.23 = (bf16[512,256]{1,0:T(8,128)(2,1)S(1)}, bf16[512,256]{1,0:T(8,128)(2,1)S(1)}, u32[]{:S(2)}, u32[]{:S(2)}) collective-permute-start(bf16[512,256]{1,0:T(8,128)(2,1)S(1)} %add_convert_fusion), channel_id=1, source_target_pairs={{0,16},{1,1},{2,26},{3,11},{4,20},{5,5},{6,30},{7,15},{8,24},{9,9}... | collective-permute-start | bytes 786440 | tf_op jit(solution)/shard_map/ppermute | solution.py:291
  (13 other events, 102.5 us)
